TPU v7x, 32 devices: a whole 2x2x4 slice. The times are simulated.
32 devices in a mesh: outer: 2 (over y), rep: 4 (over x, core), shard: 4 (over z).
Axes of the slice: x: 2, y: 2, z: 4, core: 2. Of those that a mesh axis runs over, the one named last changes fastest.
Arguments:
- hidden: bfloat16 [4096, 8192], P(('outer', 'rep'), 'shard'), parts along dimension 0, may hold values from -256 to 256
- norm_gain: bfloat16 [8192], P('shard'), may hold values from 0.099609375 to 1.8984375
- kv_weight: bfloat16 [8192, 2048], P('shard'), may hold values from -0.0625 to 0.0625
- restore_jobs: int32 [16, 3], P('outer'), parts along dimension 0, may hold values from 0 to 7, as said below
- page_table: int32 [64, 2, 4], P(('outer', 'rep'), None, 'shard'), parts along dimension 0, may hold values from 0 to 15, as said below
- context_lengths: int32 [64], P(('outer', 'rep')), parts along dimension 0, may hold values from 64 to 512, as said below
- queries: bfloat16 [64, 8192], P(('outer', 'rep')), parts along dimension 0, may hold values from -12 to 12
- kv_pool: bfloat16 [512, 64, 2048], P(('outer', 'rep', 'shard')), parts along dimension 0, may hold values from -10 to 10
Outputs:
- new_pool: bfloat16 [512, 64, 2048], P(('outer', 'rep', 'shard')), parts along dimension 0
- attention_out: bfloat16 [64, 8192], P(('outer', 'rep'), 'shard'), parts along dimension 0
There are 2 independent parts, one for each index of `outer`. A program takes and returns all parts, laid end to end along the dimension named above; an argument that names none is the same for every part. Nothing has to cross between parts.
Inputs may be any that keep to these rules, and one draw needn't show every extreme that they name: `restore_jobs`: rows j * 2 to j * 2 + 1 are the restorations whose saved rows sit on replica j, in the order of its stripes; they name different destination replicas. The stripe index b names positions b * 256 to b * 256 + 255 of the destination context. No two rows name the same destination replica and slot. At most 3 rows name one destination replica, and exactly 3 rows name one. Some row names slot 7 and some row names stripe 2 - 1. `page_table`: for each replica and each index of shard, the entries of that index over the replica's contexts and pages are a permutation of 0 to 15. `context_lengths`: some context has exactly 64 positions and some has 512. A restored context is at least as long as the end of its restored stripe.
All inputs are finite; a program needn't handle non-finite values.
Results may differ from a plain program's by a relative error of at most 0.028.
Values may be sent and summed in bfloat16 or wider, within the bound.
No kernel may reach another device: no remote copies, remote signals or barrier semaphores. Data moves between devices by JAX's collectives and lax.ppermute only.
A program may use at most 128 MiB of HBM per device.

v0:
```python
import math

import jax
import jax.numpy as jnp
from jax import lax
from jax.sharding import PartitionSpec as P

D = 8192
QH = 64
KVH = 8
HD = 128
SENDS = 2


THETA = 500000.0
EPS = 1e-05
FLOOR_SCORE = -1e30


def rotate(key_rows, positions):
    half_dim = key_rows.shape[-1] // 2
    frequency = THETA ** (-(jnp.arange(half_dim, dtype=jnp.float32) * 2.0 / key_rows.shape[-1]))
    angles = positions.astype(jnp.float32)[:, None] * frequency[None, :]
    cosine = jnp.cos(angles)[:, None, :]
    sine_part = jnp.sin(angles)[:, None, :]
    first_half = key_rows[..., :half_dim]
    second = key_rows[..., half_dim:]
    return jnp.concatenate(
        [first_half * cosine - second * sine_part, second * cosine + first_half * sine_part],
        axis=-1,
    )


def finish(projected, inverse, positions):
    row_count = projected.shape[0]
    half_width = projected.shape[1] // 2
    scaled = projected * inverse[:, None]
    key_rows = rotate(scaled[:, :half_width].reshape(row_count, KVH, HD), positions).reshape(
        row_count, half_width
    )
    return jnp.concatenate([key_rows, scaled[:, half_width:]], axis=1).astype(jnp.bfloat16)


def spread_out(pieces, targets, replicas):
    outgoing = jnp.zeros((replicas,) + pieces.shape[1:], pieces.dtype)
    for send_index in range(SENDS):
        hit = (jnp.arange(replicas, dtype=jnp.int32) == targets[send_index])[:, None, None]
        outgoing = jnp.where(hit, pieces[send_index][None], outgoing)
    return outgoing


def on_device(
    hidden, norm_gain, kv_weight, restore_jobs, page_table, context_lengths, queries, kv_pool
):
    shards = lax.axis_size("shard")
    replicas = lax.axis_size("rep")
    my_replica = lax.axis_index("rep")
    my_shard = lax.axis_index("shard")
    stripe = hidden.shape[0] // SENDS
    page_len = stripe // shards
    features = hidden.shape[1]
    kv_width = kv_weight.shape[1]
    pool_pages = kv_pool.shape[0]
    destination = restore_jobs[:, 0]
    context = restore_jobs[:, 1]
    stripe_index = restore_jobs[:, 2]
    my_targets = lax.dynamic_slice_in_dim(destination, my_replica * SENDS, SENDS, 0)
    is_mine = destination == my_replica
    gain_wide = norm_gain.astype(jnp.float32)[None, :]
    page_rows = jnp.arange(page_len, dtype=jnp.int32)
    wide = hidden.astype(jnp.float32)
    squares = lax.psum(jnp.sum(wide * wide, axis=1), "shard")
    inverse = lax.rsqrt(squares / D + EPS)
    gained = (wide * gain_wide).astype(jnp.bfloat16)
    arranged = gained.reshape(SENDS, shards, page_len, features).transpose(1, 0, 2, 3)
    arranged = arranged.reshape(shards * SENDS * page_len, features)
    owned = lax.psum_scatter(
        jnp.dot(arranged, kv_weight, preferred_element_type=jnp.float32).astype(jnp.bfloat16),
        "shard",
        scatter_dimension=0,
        tiled=True,
    ).astype(jnp.float32)
    owned_inverse = lax.dynamic_slice_in_dim(
        inverse.reshape(SENDS, stripe), my_shard * page_len, page_len, 1
    )
    my_stripes = lax.dynamic_slice_in_dim(stripe_index, my_replica * SENDS, SENDS, 0)
    positions = my_stripes[:, None] * stripe + my_shard * page_len + page_rows[None, :]
    finished = finish(owned, owned_inverse.reshape(-1), positions.reshape(-1)).reshape(
        SENDS, page_len, kv_width
    )
    outgoing = spread_out(finished, my_targets, replicas)
    arrived = lax.all_to_all(outgoing, "rep", split_axis=0, concat_axis=0, tiled=True)
    mine_grid = is_mine.reshape(replicas, SENDS)
    has_page = jnp.any(mine_grid, axis=1)
    which = jnp.argmax(mine_grid.astype(jnp.int32), axis=1)
    job_index = jnp.arange(replicas, dtype=jnp.int32) * SENDS + which
    physical = jnp.where(
        has_page, page_table[context[job_index], stripe_index[job_index], 0], pool_pages
    )
    new_pool = kv_pool.at[physical].set(arrived, mode="drop")
    slots = queries.shape[0]
    pages_dev = page_table.shape[1]
    group = QH // KVH
    scale = 1.0 / math.sqrt(HD)
    cached = new_pool[page_table[:, :, 0]]
    key_rows = cached[..., : KVH * HD].reshape(slots, pages_dev * page_len, KVH, HD)
    value_rows = cached[..., KVH * HD :].reshape(slots, pages_dev * page_len, KVH, HD)
    query_rows = queries.reshape(slots, KVH, group, HD)
    scores = (
        jnp.einsum("cgmd,cpgd->cgmp", query_rows, key_rows, preferred_element_type=jnp.float32)
        * scale
    )
    position = (
        (jnp.arange(pages_dev, dtype=jnp.int32)[:, None] * shards + my_shard) * page_len
        + page_rows[None, :]
    ).reshape(-1)
    usable = (position[None, :] < context_lengths[:, None])[:, None, None, :]
    local_max = jnp.max(jnp.where(usable, scores, FLOOR_SCORE), axis=-1)
    weights = jnp.where(usable, jnp.exp(scores - local_max[..., None]), 0.0)
    denominator = jnp.sum(weights, axis=-1).reshape(slots, QH)
    numerator = jnp.einsum(
        "cgmp,cpgd->cgmd",
        weights.astype(jnp.bfloat16),
        value_rows,
        preferred_element_type=jnp.float32,
    )
    numerator = numerator.reshape(slots, QH, HD)
    local_max = local_max.reshape(slots, QH)
    heads_here = QH // shards
    row_max = lax.pmax(local_max, "shard")
    factor = jnp.exp(local_max - row_max)
    scaled_num = (numerator * factor[..., None]).reshape(slots, QH * HD)
    numerator, denominator = (
        lax.psum(scaled_num.astype(jnp.bfloat16), "shard").astype(jnp.float32),
        lax.psum((denominator * factor).astype(jnp.bfloat16), "shard").astype(jnp.float32),
    )
    numerator = lax.dynamic_slice_in_dim(numerator, my_shard * heads_here * HD, heads_here * HD, 1)
    denominator = lax.dynamic_slice_in_dim(denominator, my_shard * heads_here, heads_here, 1)
    numerator = numerator.reshape(slots, heads_here, HD)
    attention_out = numerator / denominator[..., None]
    return (new_pool, attention_out.reshape(slots, heads_here * HD).astype(jnp.bfloat16))


def solution(mesh):
    in_specs = (
        P(("outer", "rep"), "shard"),
        P("shard"),
        P("shard", None),
        P("outer", None),
        P(("outer", "rep"), None, "shard"),
        P(("outer", "rep")),
        P(("outer", "rep"), None),
        P(("outer", "rep", "shard"), None, None),
    )
    out_specs = (P(("outer", "rep", "shard"), None, None), P(("outer", "rep"), "shard"))
    return jax.shard_map(
        on_device, mesh=mesh, in_specs=in_specs, out_specs=out_specs, check_vma=False
    )
```

profile of v0, /device:TPU:0, one launch (start us, length us, event | category | flops | bytes accessed | tf_op | source)
XLA Modules:
  0.0 154.4 jit_solution(7559153390573105979)
XLA Ops:
  7.2 0.0 copy-start
  7.2 0.0 copy-start.2
  7.2 0.0 copy-start.3
  7.2 0.0 reduce-scatter.2.cloned.1.call-start
  7.2 4.9 %copy.52 = bf16[16,64,2048]{2,1,0:T(8,128)(2,1)} copy(bf16[16,64,2048]{2,1,0:T(8,128)(2,1)} %param.15) | data formatting | bytes 8388608
  12.2 0.0 copy-done.3
  12.2 0.0 copy-done.2
  12.2 0.0 copy-start.6
  12.2 0.7 fusion.1
  12.9 0.1 copy.20
  13.0 2.5 %copy-done.6 = bf16[2048,2048]{1,0:T(8,128)(2,1)S(1)} copy-done((bf16[2048,2048]{1,0:T(8,128)(2,1)S(1)}, bf16[2048,2048]{1,0:T(8,128)(2,1)}, u32[]{:S(2)}) %copy-start.6) | copy-done | bytes 8388632
  15.6 5.7 %convolution_convert_fusion = bf16[512,2048]{1,0:T(8,128)(2,1)} fusion(bf16[512,2048]{1,0:T(8,128)(2,1)S(1)} %bitcast.74, bf16[2048,2048]{1,0:T(8,128)(2,1)S(1)} %copy-done.6), kind=kOutput, calls=%fused_computation.9 | convolution fusion | flops 4296015872 | bytes 12582912 | tf_op jit(solution)/shard_map/dot_general | solution.py:78
  21.3 0.0 reduce-scatter.2.cloned.1.call-update
  21.4 13.6 %psum.21 = f32[512]{0:T(512)S(1)} all-reduce(f32[512]{0:T(512)S(1)} %get-tuple-element.8), channel_id=1, replica_groups=mesh['outer'=2,'rep'=4,'shard'=4] {'shard'}, use_global_device_ids=true, to_apply=%region_4.5 | all-reduce | flops 512 | bytes 4096 | tf_op jit(solution)/shard_map/psum | solution.py:72
  35.0 0.1 constant_dynamic-slice_fusion.2
  35.1 0.1 mul.138
  35.2 0.0 copy-done.4
  35.2 0.1 fusion.28
  35.2 0.1 add_convert_fusion.1
  35.3 0.1 convert_element_type.54
  35.4 0.1 eq.38
  35.5 0.6 iota_reduce_fusion
  36.2 0.6 gather_fusion
  36.8 0.6 gather_fusion.1
  37.5 0.1 constant_dynamic-slice_fusion.3
  37.5 0.6 fusion.32
  38.1 1.3 iota_compare_fusion
  39.4 0.3 multiply_cosine_fusion
  39.7 28.4 %reduce-scatter.2.cloned.1.call-done = bf16[128,2048]{1,0:T(8,128)(2,1)} async-done(((bf16[512,2048]{1,0:T(8,128)(2,1)}), bf16[128,2048]{1,0:T(8,128)(2,1)}) %reduce-scatter.2.cloned.1.call-update) | async-done | bytes 524304 | tf_op jit(solution)/shard_map/reduce_scatter | solution.py:77
  68.2 1.2 convert_multiply_fusion.2
  69.4 0.1 copy.27
  69.5 0.3 subtract_convert_fusion
  69.8 0.1 pad_maximum_fusion.1
  70.1 0.0 copy-start.5
  70.1 1.2 select_select_fusion
  71.3 3.5 %all-to-all-start = ((bf16[4,64,2048]{2,1,0:T(8,128)(2,1)}), bf16[4,64,2048]{2,1,0:T(8,128)(2,1)S(1)}, u32[]{:S(2)}, u32[]{:S(2)}) async-start(bf16[4,64,2048]{2,1,0:T(8,128)(2,1)} %select_select_fusion), calls=%async_computation.1 | async-start | bytes 2097152 | tf_op jit(solution)/shard_map/all_to_all | solution.py:92
  74.8 0.0 all-reduce.2.cloned.1.call-start
  74.9 0.6 gather_fusion.2
  75.5 0.1 reduce_or.9
  75.6 0.1 copy.21
  75.7 0.1 reshape.273
  75.8 0.1 iota_add_fusion
  75.9 0.1 add.152
  76.0 0.1 broadcast_compare_fusion
  76.1 13.2 %all-to-all-done = bf16[4,64,2048]{2,1,0:T(8,128)(2,1)S(1)} async-done(((bf16[4,64,2048]{2,1,0:T(8,128)(2,1)}), bf16[4,64,2048]{2,1,0:T(8,128)(2,1)S(1)}, u32[]{:S(2)}, u32[]{:S(2)}) %all-to-all-start) | async-done | bytes 1048608 | tf_op jit(solution)/shard_map/all_to_all | solution.py:92
  89.2 2.6 %scatter_fusion = bf16[16,64,2048]{2,1,0:T(8,128)(2,1)} fusion(bf16[16,64,2048]{2,1,0:T(8,128)(2,1)} %copy.52, s32[4]{0:T(128)S(1)} %fusion.26, bf16[4,64,2048]{2,1,0:T(8,128)(2,1)S(1)} %all-to-all-done), kind=kCustom, calls=%fused_computation.4 | custom fusion | bytes 3145744 | tf_op jit(solution)/shard_map/scatter | solution.py:100
  91.9 4.9 %gather_fusion.3 = bf16[16,64,2048]{2,1,0:T(8,128)(2,1)} fusion(bf16[16,64,2048]{2,1,0:T(8,128)(2,1)} %scatter_fusion, s32[1024]{0:T(1024)S(1)} %pad_clamp_fusion), kind=kCustom, calls=%fused_computation.3 | custom fusion | bytes 8388672 | tf_op jit(solution)/shard_map/gather | solution.py:105
  96.8 2.7 %fusion.30 = (bf16[8,2,64,1024]{3,2,1,0:T(8,128)(2,1)S(1)}, bf16[8,2,64,1024]{3,2,1,0:T(8,128)(2,1)S(1)}) fusion(bf16[8,2,64,2048]{3,2,1,0:T(8,128)(2,1)} %bitcast.67), kind=kLoop, calls=%fused_computation.78 | loop fusion | bytes 8388608 | tf_op jit(solution)/shard_map/slice | solution.py:106
  99.5 0.6 copy.29
  100.2 1.3 select_reduce_fusion
  101.4 0.1 reshape.247
  101.5 0.3 bitcast_reduce_fusion
  101.8 0.1 reshape.248
  101.9 9.8 %pmax.7 = f32[8,64]{1,0:T(8,128)S(1)} all-reduce(f32[8,64]{1,0:T(8,128)S(1)} %reshape.247), channel_id=1, replica_groups=mesh['outer'=2,'rep'=4,'shard'=4] {'shard'}, use_global_device_ids=true, to_apply=%region_7.8 | all-reduce | flops 512 | bytes 4096 | tf_op jit(solution)/shard_map/pmax | solution.py:130
  111.7 0.1 copy.25
  111.7 0.6 copy.30
  112.4 0.7 fusion.9
  113.1 0.8 fusion.13
  113.9 0.0 all-reduce.2.cloned.1.call-update
  114.0 9.0 %psum.23 = bf16[8,64]{1,0:T(8,128)(2,1)S(1)} all-reduce(bf16[8,64]{1,0:T(8,128)(2,1)S(1)} %get-tuple-element.4), channel_id=1, replica_groups=mesh['outer'=2,'rep'=4,'shard'=4] {'shard'}, use_global_device_ids=true, to_apply=%region_10.11 | all-reduce | flops 512 | bytes 2048 | tf_op jit(solution)/shard_map/psum | solution.py:135
  122.9 0.1 constant_dynamic-slice_fusion
  123.0 0.1 copy.26
  123.1 23.0 %all-reduce.2.cloned.1.call-done = bf16[8,8192]{1,0:T(8,128)(2,1)} async-done(((bf16[8,8192]{1,0:T(8,128)(2,1)}), bf16[8,8192]{1,0:T(8,128)(2,1)}) %all-reduce.2.cloned.1.call-update) | async-done | bytes 131088 | tf_op jit(solution)/shard_map/psum | solution.py:134
  146.1 1.5 fusion.18
  (24 shorter events, 0.3 us)
Async XLA Ops:
  7.2 93.0 %copy-start = (bf16[8,8192]{1,0:T(8,128)(2,1)S(1)}, bf16[8,8192]{1,0:T(8,128)(2,1)}, u32[]{:S(2)}) copy-start(bf16[8,8192]{1,0:T(8,128)(2,1)} %param.14) | copy-start | bytes 393220
  7.2 5.0 %copy-start.2 = (bf16[512,2048]{1,0:T(8,128)(2,1)S(1)}, bf16[512,2048]{1,0:T(8,128)(2,1)}, u32[]{:S(2)}) copy-start(bf16[512,2048]{1,0:T(8,128)(2,1)} %param.8) | copy-start | bytes 6291460
  7.2 5.0 %copy-start.3 = (bf16[2048]{0:T(1024)(128)(2,1)S(1)}, bf16[2048]{0:T(1024)(128)(2,1)}, u32[]{:S(2)}) copy-start(bf16[2048]{0:T(1024)(128)(2,1)} %param.9) | copy-start | bytes 12292
  7.2 61.0 %reduce-scatter.2.cloned.1.call-start = ((), (), s32[]{:S(2)}) async-start(), calls=%async_computation.2 | async-start | bytes 2621440 | tf_op jit(solution)/shard_map/reduce_scatter | solution.py:77
  12.2 3.4 %copy-start.6 = (bf16[2048,2048]{1,0:T(8,128)(2,1)S(1)}, bf16[2048,2048]{1,0:T(8,128)(2,1)}, u32[]{:S(2)}) copy-start(bf16[2048,2048]{1,0:T(8,128)(2,1)} %param.10) | copy-start | bytes 25165828
  21.3 13.8 %copy-start.4 = (s32[8,3]{0,1:T(4,128)S(1)}, s32[8,3]{0,1:T(4,128)}, u32[]{:S(2)}) copy-start(s32[8,3]{0,1:T(4,128)} %param.11) | copy-start | bytes 292
  21.3 18.1 %copy-start.1 = (s32[8,2,1]{0,2,1:T(1,128)S(1)}, s32[8,2,1]{0,2,1:T(1,128)}, u32[]{:S(2)}) copy-start(s32[8,2,1]{0,2,1:T(1,128)} %param.12) | copy-start | bytes 196
  70.1 5.9 %copy-start.5 = (s32[8]{0:T(128)S(1)}, s32[8]{0:T(128)}, u32[]{:S(2)}) copy-start(s32[8]{0:T(128)} %param.13) | copy-start | bytes 100
  71.3 18.0 %all-to-all-start = ((bf16[4,64,2048]{2,1,0:T(8,128)(2,1)}), bf16[4,64,2048]{2,1,0:T(8,128)(2,1)S(1)}, u32[]{:S(2)}, u32[]{:S(2)}) async-start(bf16[4,64,2048]{2,1,0:T(8,128)(2,1)} %select_select_fusion), calls=%async_computation.1 | async-start | bytes 2097152 | tf_op jit(solution)/shard_map/all_to_all | solution.py:92
  74.8 71.3 %all-reduce.2.cloned.1.call-start = ((), (), s32[]{:S(2)}) async-start(), calls=%async_computation.3 | async-start | bytes 262144 | tf_op jit(solution)/shard_map/psum | solution.py:134
Sparse Core Ops, SparseCore 0:
  21.5 46.6 reduce-scatter.1
  114.1 32.0 all-reduce.1
where the time goes:
time: 155 us; the launch traced here: 154 us
  waiting for transfers between devices  64.7 us (42%)
  blocking collectives  32.4 us (21%)
  local copies, waits for them, and re-layouts  23 us (15%)
  between operations  14.3 us (9%)
  other arithmetic  8.84 us (6%)
  matrix products  7.73 us (5%)
  starting transfers between devices  3.6 us (2%)
    reduce_scatter x1, waiting for transfers between devices, on_device(): lax.psum_scatter(jnp.dot(arranged, kv_weight, preferred_element_type=jnp....  28.4 us
    psum x1, waiting for transfers between devices, on_device(): lax.psum(scaled_num.astype(jnp.bfloat16), 'shard').astype(jnp.float32)  23 us
    psum x1, blocking collectives, on_device(): squares = lax.psum(jnp.sum(wide * wide, axis=1), 'shard')  13.6 us
    all_to_all x1, waiting for transfers between devices, on_device(): lax.all_to_all(outgoing, 'rep', split_axis=0, concat_axis=0, tiled=True)  13.2 us
    pmax x1, blocking collectives, on_device(): row_max = lax.pmax(local_max, 'shard')  9.75 us
    psum x1, blocking collectives, on_device(): lax.psum((denominator * factor).astype(jnp.bfloat16), 'shard')  8.99 us
    unnamed x20, local copies, waits for them, and re-layouts  8.92 us
    dot_general x1, matrix products, on_device(): jnp.dot(arranged, kv_weight, preferred_element_type=jnp.float32)  5.75 us
  transfers between devices with their start and end apart: 3, of which 3 were waited for; matrix products, arithmetic and copies ran while one was open for 4% of the time, Pallas kernels for 0%

commit v1 on v0

--- a/solution.py
+++ b/solution.py
@@ -1,8 +1,11 @@
+import functools
 import math
 
 import jax
 import jax.numpy as jnp
 from jax import lax
+from jax.experimental import pallas as pl
+from jax.experimental.pallas import tpu as pltpu
 from jax.sharding import PartitionSpec as P
 
 D = 8192
@@ -49,7 +52,7 @@
     return outgoing
 
 
-def on_device(
+def on_device_general(
     hidden, norm_gain, kv_weight, restore_jobs, page_table, context_lengths, queries, kv_pool
 ):
     shards = lax.axis_size("shard")
@@ -141,6 +144,646 @@
     return (new_pool, attention_out.reshape(slots, heads_here * HD).astype(jnp.bfloat16))
 
 
+FIRST = [(0, 1), (3, 2), (1, 3), (2, 0)]
+NEAR = [(0, 1), (1, 0), (2, 3), (3, 2)]
+THIRD = [(0, 3), (3, 0), (1, 2), (2, 1)]
+LANES = 128
+BF16 = jnp.bfloat16
+F32 = jnp.float32
+SMEM = pltpu.SMEM
+VMEM = pltpu.VMEM
+SMALL = pl.CostEstimate(flops=1, bytes_accessed=1, transcendentals=0)
+LIMIT = 24 * 1024 * 1024
+
+
+def whole(space=VMEM):
+    return pl.BlockSpec(memory_space=space)
+
+
+def split_sum(total, offset):
+    high = total.astype(BF16).astype(F32)
+    low = total - high
+    lane = lax.broadcasted_iota(jnp.int32, (total.shape[0], LANES), 1)
+    return jnp.where(lane == offset, high, jnp.where(lane == offset + 1, low, 0.0)).astype(BF16)
+
+
+def row_copies(hidden, blocks, rows_in, sem):
+    stripes, _, page_len, _ = hidden.shape
+    return [
+        pltpu.make_async_copy(
+            hidden.at[stripe, block],
+            rows_in.at[pl.ds((place * stripes + stripe) * page_len, page_len)],
+            sem.at[place * stripes + stripe],
+        )
+        for place, block in enumerate(blocks)
+        for stripe in range(stripes)
+    ]
+
+
+def weight_copies(weight, tiles, sem):
+    half = weight.shape[1] // 2
+    return [
+        pltpu.make_async_copy(weight.at[:, pl.ds(side * half, half)], tiles.at[side], sem.at[side])
+        for side in range(2)
+    ]
+
+
+def scale_rows(rows_in, gained, gain_in, span):
+    wide_gain = gain_in[...].astype(F32).reshape(1, gain_in.shape[0])
+    gained[span] = (rows_in[span].astype(F32) * wide_gain).astype(BF16)
+
+
+def put_squares(rows_in, span, out, columns, offset):
+    squares = jnp.zeros((out.shape[0], LANES), F32)
+    for lane in range(rows_in.shape[1] // LANES):
+        part = rows_in[span, lane * LANES : (lane + 1) * LANES].astype(F32)
+        squares = squares + part * part
+    total = jnp.sum(squares, axis=1, keepdims=True)
+    out[:, columns] = split_sum(total, offset)
+
+
+def is_inner(shard):
+    return (shard == 1) | (shard == 2)
+
+
+def far_blocks(shard):
+    lower = shard < 2
+    return jnp.where(lower, 2, 1), jnp.where(lower, 3, 0)
+
+
+def first_kernel(hidden, gain, weight, out, rows_in, gained, gain_in, tiles, row_sem, gain_sem, tile_sem):
+    shard = lax.axis_index("shard")
+    half = weight.shape[1] // 2
+    inner_block, outer_block = far_blocks(shard)
+    rows_here = row_copies(hidden, [jnp.where(is_inner(shard), outer_block, inner_block)], rows_in, row_sem)
+    tiles_here = weight_copies(weight, tiles, tile_sem)
+    gain_copy = pltpu.make_async_copy(gain, gain_in, gain_sem)
+    gain_copy.start()
+    for copy in rows_here + tiles_here:
+        copy.start()
+    gain_copy.wait()
+    for copy in rows_here:
+        copy.wait()
+    scale_rows(rows_in, gained, gain_in, slice(None))
+    put_squares(rows_in, slice(None), out, slice(half, half + LANES), 0)
+    for side, columns in enumerate((slice(0, half), slice(half + LANES, 2 * half + LANES))):
+        tiles_here[side].wait()
+        out[:, columns] = jnp.dot(gained[...], tiles[side], preferred_element_type=F32).astype(BF16)
+
+
+def project_first(hidden, gain, weight):
+    stripes, blocks, page_len, features = hidden.shape
+    half = weight.shape[1] // 2
+    rows = stripes * page_len
+    return pl.pallas_call(
+        first_kernel,
+        in_specs=[whole(pl.ANY)] * 3,
+        out_specs=whole(),
+        out_shape=jax.ShapeDtypeStruct((rows, 2 * half + LANES), BF16),
+        scratch_shapes=[
+            pltpu.VMEM((rows, features), BF16),
+            pltpu.VMEM((rows, features), BF16),
+            pltpu.VMEM((features,), BF16),
+            pltpu.VMEM((2, features, half), BF16),
+            pltpu.SemaphoreType.DMA((stripes,)),
+            pltpu.SemaphoreType.DMA,
+            pltpu.SemaphoreType.DMA((2,)),
+        ],
+        compiler_params=pltpu.CompilerParams(vmem_limit_bytes=LIMIT),
+        cost_estimate=SMALL,
+        name="project_first",
+    )(hidden, gain, weight)
+
+
+def head_spread(query, width):
+    heads = query.shape[0]
+    group = heads // (width // LANES)
+    head = lax.broadcasted_iota(jnp.int32, (heads, LANES), 0)
+    pieces = [jnp.where(head // group == g, query, jnp.zeros_like(query)) for g in range(width // LANES)]
+    return jnp.concatenate(pieces, axis=1)
+
+
+def head_pick(products):
+    heads, width = products.shape
+    group = heads // (width // LANES)
+    head = lax.broadcasted_iota(jnp.int32, (heads, LANES), 0)
+    picked = products[:, :LANES]
+    for g in range(1, width // LANES):
+        picked = jnp.where(head // group == g, products[:, g * LANES : (g + 1) * LANES], picked)
+    return picked
+
+
+def score(query, key_rows):
+    spread = head_spread(query, key_rows.shape[1])
+    scores = lax.dot_general(spread, key_rows, (((1,), (1,)), ((), ())), preferred_element_type=F32)
+    return scores * (1.0 / math.sqrt(LANES))
+
+
+def attend(query, key_rows, value_rows, usable):
+    scores = jnp.where(usable, score(query, key_rows), FLOOR_SCORE)
+    largest = jnp.max(scores, axis=1, keepdims=True)
+    weights = jnp.where(usable, jnp.exp(scores - largest), 0.0)
+    total = jnp.sum(weights, axis=1, keepdims=True)
+    picked = head_pick(jnp.dot(weights.astype(BF16), value_rows, preferred_element_type=F32))
+    some = total > 0.0
+    safe = jnp.where(some, total, 1.0)
+    return picked / safe, jnp.where(some, largest + jnp.log(safe), FLOOR_SCORE)
+
+
+def split_lines(lines, first):
+    high = lines.astype(BF16).astype(F32)
+    middle_part = (lines - high).astype(BF16).astype(F32)
+    low = lines - high - middle_part
+    place = lax.broadcasted_iota(jnp.int32, lines.shape, 0) - first
+    return jnp.where(place == 0, high, jnp.where(place == 1, middle_part, jnp.where(place == 2, low, 0.0)))
+
+
+def join_lines(tail, first, rows):
+    line = jnp.sum(tail[first : first + 3].astype(F32), axis=0, keepdims=True)
+    return jnp.broadcast_to(line, (LANES, LANES)).T[:rows]
+
+
+def middle_kernel(hidden, gain, weight, *rest, after):
+    keys, values = rest[after : after + 3], rest[after + 3 : after + 6]
+    rows_in, gained, gain_in, tiles, row_sem, gain_sem, tile_sem = rest[after + 6 :]
+    shard = lax.axis_index("shard")
+    half = weight.shape[1] // 2
+    rows = values[0].shape[0]
+    inner_block, outer_block = far_blocks(shard)
+    blocks = [shard, jnp.bitwise_xor(shard, 1), jnp.where(is_inner(shard), inner_block, outer_block)]
+    rows_here = row_copies(hidden, blocks, rows_in, row_sem)
+    tiles_here = weight_copies(weight, tiles, tile_sem)
+    gain_copy = pltpu.make_async_copy(gain, gain_in, gain_sem)
+    gain_copy.start()
+    for copy in rows_here + tiles_here:
+        copy.start()
+    gain_copy.wait()
+    for copy in rows_here:
+        copy.wait()
+    scale_rows(rows_in, gained, gain_in, slice(None))
+    for place, ref in enumerate(keys):
+        span = slice(place * rows, (place + 1) * rows)
+        put_squares(rows_in, span, ref, slice(half, half + LANES), 2 if place == 2 else 0)
+    for side, refs in enumerate((keys, values)):
+        tiles_here[side].wait()
+        product = jnp.dot(gained[...], tiles[side], preferred_element_type=F32).astype(BF16)
+        for place, ref in enumerate(refs):
+            ref[:, :half] = product[place * rows : (place + 1) * rows]
+
+
+def middle(hidden, gain, weight, after):
+    stripes, blocks, page_len, features = hidden.shape
+    half = weight.shape[1] // 2
+    rows = stripes * page_len
+    keys = jax.ShapeDtypeStruct((rows, half + LANES), BF16)
+    values = jax.ShapeDtypeStruct((rows, half), BF16)
+    return pl.pallas_call(
+        functools.partial(middle_kernel, after=len(after)),
+        in_specs=[whole(pl.ANY)] * (3 + len(after)),
+        out_specs=[whole()] * 6,
+        out_shape=[keys] * 3 + [values] * 3,
+        scratch_shapes=[
+            pltpu.VMEM((3 * rows, features), BF16),
+            pltpu.VMEM((3 * rows, features), BF16),
+            pltpu.VMEM((features,), BF16),
+            pltpu.VMEM((2, features, half), BF16),
+            pltpu.SemaphoreType.DMA((3 * stripes,)),
+            pltpu.SemaphoreType.DMA,
+            pltpu.SemaphoreType.DMA((2,)),
+        ],
+        compiler_params=pltpu.CompilerParams(vmem_limit_bytes=LIMIT),
+        cost_estimate=SMALL,
+        name="middle",
+    )(hidden, gain, weight, *after)
+
+
+def ask_kernel(jobs, query, after, *outs):
+    for step, out in enumerate(outs):
+        out[...] = query[job_from(jobs, step)[1]]
+
+
+def ask(jobs, query, after):
+    return pl.pallas_call(
+        ask_kernel,
+        in_specs=[whole(SMEM), whole(), whole(pl.ANY)],
+        out_specs=[whole()] * 4,
+        out_shape=[jax.ShapeDtypeStruct(query.shape[1:], BF16)] * 4,
+        compiler_params=pltpu.CompilerParams(vmem_limit_bytes=LIMIT),
+        cost_estimate=SMALL,
+        name="ask",
+    )(jobs, query, after)
+
+
+def kept_kernel(jobs, table, lengths, query, pool, after, *rest, shards):
+    outs, new_pool, pages, total, level, in_sem, out_sem = rest[:4], *rest[4:]
+    slots, heads, _ = query.shape
+    here = heads // shards
+    rows = slots * here
+    replica = lax.axis_index("rep")
+    shard = lax.axis_index("shard")
+    page_len = pool.shape[1]
+    half = pool.shape[2] // 2
+
+    def copy_in(context, page):
+        place = context * 2 + page
+        return pltpu.make_async_copy(pool.at[table[page, context]], pages.at[place], in_sem.at[place])
+
+    def copy_out(context, page):
+        place = context * 2 + page
+        return pltpu.make_async_copy(pages.at[place], new_pool.at[table[page, context]], out_sem.at[place])
+
+    @pl.loop(0, slots)
+    def _(context):
+        for page in range(2):
+            copy_in(context, page).start()
+
+    @pl.loop(0, slots)
+    def _(context):
+        for page in range(2):
+            copy_in(context, page).wait()
+            copy_out(context, page).start()
+        gone = [jnp.int32(0), jnp.int32(0)]
+        for job in range(jobs.shape[1]):
+            hit = (jobs[0, job] == replica) & (jobs[1, job] == context)
+            for page in range(2):
+                gone[page] = gone[page] | (hit & (jobs[2, job] == page)).astype(jnp.int32)
+        lane = lax.broadcasted_iota(jnp.int32, (heads, 2 * page_len), 1)
+        page = lane // page_len
+        position = (page * shards + shard) * page_len + lane % page_len
+        usable = (position < lengths[context]) & (jnp.where(page == 0, gone[0], gone[1]) == 0)
+        both = pages[pl.ds(context * 2, 2)].reshape(2 * page_len, 2 * half)
+        result, logarithm = attend(query[context], both[:, :half], both[:, half:], usable)
+        total[context] = result
+        level[context] = jnp.broadcast_to(logarithm, result.shape)
+
+    for step, out in enumerate(outs):
+        start = pl.multiple_of(jnp.bitwise_xor(shard, step) * here, here)
+        out[:rows] = total[:, pl.ds(start, here), :].reshape(rows, LANES).astype(BF16)
+        lines = level[:, pl.ds(start, here), :].reshape(rows, LANES).T[:16]
+        out[rows:] = split_lines(lines, 0).astype(BF16)
+
+    @pl.loop(0, slots)
+    def _(context):
+        for page in range(2):
+            copy_out(context, page).wait()
+
+
+def kept(jobs, table, lengths, query, pool, after, shards):
+    slots, heads, size = query.shape
+    return pl.pallas_call(
+        functools.partial(kept_kernel, shards=shards),
+        in_specs=[whole(SMEM)] * 3 + [whole()] + [whole(pl.ANY)] * 2,
+        out_specs=[whole()] * 4 + [whole(pl.ANY)],
+        out_shape=[jax.ShapeDtypeStruct((slots * heads // shards + 16, size), BF16)] * 4
+        + [jax.ShapeDtypeStruct(pool.shape, pool.dtype)],
+        scratch_shapes=[
+            pltpu.VMEM((slots * 2,) + pool.shape[1:], pool.dtype),
+            pltpu.VMEM(query.shape, F32),
+            pltpu.VMEM(query.shape, F32),
+            pltpu.SemaphoreType.DMA((slots * 2,)),
+            pltpu.SemaphoreType.DMA((slots * 2,)),
+        ],
+        compiler_params=pltpu.CompilerParams(vmem_limit_bytes=LIMIT),
+        cost_estimate=SMALL,
+        name="kept",
+    )(jobs, table, lengths, query, pool, after)
+
+
+def carry_kernel(mine, first, after, out):
+    start = first.shape[1] - mine.shape[1]
+    inner = is_inner(lax.axis_index("shard"))
+
+    @pl.when(inner)
+    def _():
+        out[...] = (mine[...].astype(F32) + first[:, start:].astype(F32)).astype(BF16)
+
+    @pl.when(jnp.logical_not(inner))
+    def _():
+        out[...] = mine[...]
+
+
+def carry(mine, first, after):
+    return pl.pallas_call(
+        carry_kernel,
+        in_specs=[whole(), whole(), whole(pl.ANY)],
+        out_specs=whole(),
+        out_shape=jax.ShapeDtypeStruct(mine.shape, BF16),
+        compiler_params=pltpu.CompilerParams(vmem_limit_bytes=LIMIT),
+        cost_estimate=SMALL,
+        name="carry",
+    )(mine, first, after)
+
+
+def route(jobs, finished, outs):
+    replica = lax.axis_index("rep")
+    page_len = finished.shape[0] // SENDS
+    for step, out in enumerate(outs):
+        chosen = jobs[0, replica * SENDS] == jnp.bitwise_xor(replica, step)
+
+        @pl.when(chosen)
+        def _():
+            out[...] = finished[:page_len]
+
+        @pl.when(jnp.logical_not(chosen))
+        def _():
+            out[...] = finished[page_len:]
+
+
+def add_parts(own, near, first, third, columns, first_columns):
+    direct = jnp.where(is_inner(lax.axis_index("shard")), 0.0, first[:, first_columns].astype(F32))
+    return (own[:, columns].astype(F32) + near[:, columns].astype(F32)) + (third[:, columns].astype(F32) + direct)
+
+
+def finish_keys_kernel(jobs, own, near, first, third, frequency, *rest, stripe):
+    asked, outs = rest[:4], rest[4:8]
+    scale, weights_out, share, level, finished = rest[8:]
+    replica = lax.axis_index("rep")
+    shard = lax.axis_index("shard")
+    rows = own.shape[0]
+    page_len = rows // SENDS
+    width = own.shape[1] - LANES
+
+    def added(columns):
+        return add_parts(own, near, first, third, columns, columns)
+
+    squares = jnp.sum(added(slice(width, width + LANES)), axis=1, keepdims=True)
+    inverse = jnp.broadcast_to(lax.rsqrt(squares / D + EPS), (rows, LANES))
+    scale[...] = inverse
+    row = lax.broadcasted_iota(jnp.int32, (rows, LANES), 0)
+    lane = lax.broadcasted_iota(jnp.int32, (rows, LANES), 1)
+    index = jnp.where(row < page_len, jobs[2, replica * SENDS], jobs[2, replica * SENDS + 1])
+    position = index * stripe + shard * page_len + row % page_len
+    angle = position.astype(F32) * frequency[...]
+    cosine = jnp.cos(angle) * inverse
+    sine_part = jnp.where(lane < LANES // 2, -jnp.sin(angle), jnp.sin(angle)) * inverse
+    for head in range(width // LANES):
+        columns = slice(head * LANES, (head + 1) * LANES)
+        value = added(columns)
+        turned = value * cosine + pltpu.roll(value, LANES // 2, 1) * sine_part
+        finished[:, columns] = turned.astype(BF16)
+    route(jobs, finished, outs)
+    for send in range(SENDS):
+        step = jnp.bitwise_xor(jobs[0, replica * SENDS + send], replica)
+        query = asked[0][...]
+        for other in range(1, 4):
+            query = jnp.where(step == other, asked[other][...], query)
+        scores = score(query, finished[send * page_len : (send + 1) * page_len])
+        largest = jnp.max(scores, axis=1, keepdims=True)
+        weights = jnp.exp(scores - largest)
+        total = jnp.sum(weights, axis=1, keepdims=True)
+        weights_out[send] = weights.astype(BF16)
+        share[send] = jnp.broadcast_to(1.0 / total, share.shape[1:])
+        level[send] = jnp.broadcast_to(largest + jnp.log(total), level.shape[1:])
+
+
+def finish_values_kernel(jobs, own, near, first, third, scale, weights, share, level, *rest, shards):
+    kept_parts, outs, packed, finished, result = rest[:4], rest[4:8], rest[8:12], rest[12], rest[13]
+    shard = lax.axis_index("shard")
+    for head in range(own.shape[1] // LANES):
+        columns = slice(head * LANES, (head + 1) * LANES)
+        start = own.shape[1] + LANES + head * LANES
+        total = add_parts(own, near, first, third, columns, slice(start, start + LANES))
+        finished[:, columns] = (total * scale[...]).astype(BF16)
+    route(jobs, finished, outs)
+    page_len = own.shape[0] // SENDS
+    for send in range(SENDS):
+        products = jnp.dot(
+            weights[send], finished[send * page_len : (send + 1) * page_len], preferred_element_type=F32
+        )
+        result[send] = head_pick(products) * share[send]
+    here = level.shape[1] // shards
+    count = SENDS * here
+    rows = kept_parts[0].shape[0] - 16
+    for step in range(4):
+        start = pl.multiple_of(jnp.bitwise_xor(shard, step) * here, here)
+        packed[step][:rows] = kept_parts[step][:rows]
+        packed[step][rows : rows + count] = result[:, pl.ds(start, here), :].reshape(count, LANES).astype(BF16)
+        mine = level[:, pl.ds(start, here), :].reshape(count, LANES)
+        lines = jnp.concatenate([mine] + [jnp.zeros((LANES - count, LANES), F32)], axis=0).T[:16]
+        tail = kept_parts[step][rows:].astype(F32) + split_lines(lines, 3)
+        packed[step][rows + count :] = tail.astype(BF16)
+
+
+def finish_keys(jobs, parts, frequency, asked, stripe):
+    rows = parts[0].shape[0]
+    width = parts[0].shape[1] - LANES
+    heads = asked[0].shape[0]
+    page_len = rows // SENDS
+    return pl.pallas_call(
+        functools.partial(finish_keys_kernel, stripe=stripe),
+        in_specs=[whole(SMEM)] + [whole()] * 9,
+        out_specs=[whole()] * 8,
+        out_shape=[jax.ShapeDtypeStruct((page_len, width), BF16)] * 4
+        + [
+            jax.ShapeDtypeStruct((rows, LANES), F32),
+            jax.ShapeDtypeStruct((SENDS, heads, page_len), BF16),
+            jax.ShapeDtypeStruct((SENDS, heads, LANES), F32),
+            jax.ShapeDtypeStruct((SENDS, heads, LANES), F32),
+        ],
+        scratch_shapes=[pltpu.VMEM((rows, width), BF16)],
+        compiler_params=pltpu.CompilerParams(vmem_limit_bytes=LIMIT),
+        cost_estimate=SMALL,
+        name="finish_keys",
+    )(jobs, *parts, frequency, *asked)
+
+
+def finish_values(jobs, parts, scale, weights, share, level, kept_parts, shards):
+    rows, width = parts[0].shape
+    heads = level.shape[1]
+    page_len = rows // SENDS
+    packed = kept_parts[0].shape[0] + SENDS * heads // shards
+    return pl.pallas_call(
+        functools.partial(finish_values_kernel, shards=shards),
+        in_specs=[whole(SMEM)] + [whole()] * 12,
+        out_specs=[whole()] * 8,
+        out_shape=[jax.ShapeDtypeStruct((page_len, width), BF16)] * 4
+        + [jax.ShapeDtypeStruct((packed, LANES), BF16)] * 4,
+        scratch_shapes=[pltpu.VMEM((rows, width), BF16), pltpu.VMEM((SENDS, heads, LANES), F32)],
+        compiler_params=pltpu.CompilerParams(vmem_limit_bytes=LIMIT),
+        cost_estimate=SMALL,
+        name="finish_values",
+    )(jobs, *parts, scale, weights, share, level, *kept_parts)
+
+
+def job_from(jobs, step):
+    replica = lax.axis_index("rep")
+    first = jnp.bitwise_xor(replica, step) * SENDS
+    hit_first = jobs[0, first] == replica
+    hit = hit_first | (jobs[0, first + 1] == replica)
+    row = jnp.where(hit_first, first, first + 1)
+    return hit, jobs[1, row], jobs[2, row]
+
+
+def place_kernel(jobs, table, pool, *rest):
+    key_pages, value_pages, out, pages, sem = rest[:4], rest[4:8], rest[8], rest[9], rest[10]
+    half = key_pages[0].shape[1]
+    for wait in (False, True):
+        for step in range(4):
+            hit, context, page = job_from(jobs, step)
+
+            @pl.when(hit)
+            def _():
+                slot = table[page, context]
+                copy = pltpu.make_async_copy(pages.at[step], out.at[slot], sem.at[step])
+                if wait:
+                    copy.wait()
+                else:
+                    pages[step, :, :half] = key_pages[step][...]
+                    pages[step, :, half:] = value_pages[step][...]
+                    copy.start()
+
+
+def place_pages(jobs, table, pool, key_pages, value_pages):
+    return pl.pallas_call(
+        place_kernel,
+        in_specs=[whole(SMEM)] * 2 + [whole(pl.ANY)] + [whole()] * 8,
+        out_specs=whole(pl.ANY),
+        out_shape=jax.ShapeDtypeStruct(pool.shape, pool.dtype),
+        scratch_shapes=[pltpu.VMEM((4,) + pool.shape[1:], pool.dtype), pltpu.SemaphoreType.DMA((4,))],
+        input_output_aliases={2: 0},
+        compiler_params=pltpu.CompilerParams(vmem_limit_bytes=LIMIT),
+        cost_estimate=SMALL,
+        name="place_pages",
+    )(jobs, table, pool, *key_pages, *value_pages)
+
+
+def blend(parts, levels):
+    top = functools.reduce(jnp.maximum, levels)
+    shares = [jnp.exp(level - top) for level in levels]
+    both = functools.reduce(jnp.add, shares)
+    total = functools.reduce(jnp.add, [part * share for part, share in zip(parts, shares)])
+    return total / both, top + jnp.log(both)
+
+
+def gather_kernel(jobs, *refs, rows, count):
+    parts, after, kept_out, kept_level, outs = refs[:4], refs[4], refs[5], refs[6], refs[7:]
+    tails = [ref[rows + count :] for ref in parts]
+    mixed, level = blend(
+        [ref[:rows].astype(F32) for ref in parts], [join_lines(tail, 0, rows) for tail in tails]
+    )
+    kept_out[...] = mixed
+    kept_level[...] = level
+    mixed, level = blend(
+        [ref[rows : rows + count].astype(F32) for ref in parts], [join_lines(tail, 3, count) for tail in tails]
+    )
+    here = count // SENDS
+    replica = lax.axis_index("rep")
+    lines = [
+        jnp.concatenate([level[send * here : (send + 1) * here], jnp.zeros((LANES - here, LANES), F32)], axis=0).T[:16]
+        for send in range(SENDS)
+    ]
+    for step, out in enumerate(outs):
+        chosen = jobs[0, replica * SENDS] == jnp.bitwise_xor(replica, step)
+        out[:here] = jnp.where(chosen, mixed[:here], mixed[here:]).astype(BF16)
+        out[here:] = split_lines(jnp.where(chosen, lines[0], lines[1]), 0).astype(BF16)
+
+
+def gather_parts(jobs, parts, after, rows, count):
+    here = count // SENDS
+    return pl.pallas_call(
+        functools.partial(gather_kernel, rows=rows, count=count),
+        in_specs=[whole(SMEM)] + [whole()] * 4 + [whole(pl.ANY)],
+        out_specs=[whole()] * 6,
+        out_shape=[jax.ShapeDtypeStruct((rows, LANES), F32)] * 2
+        + [jax.ShapeDtypeStruct((here + 16, LANES), BF16)] * 4,
+        compiler_params=pltpu.CompilerParams(vmem_limit_bytes=LIMIT),
+        cost_estimate=SMALL,
+        name="gather_parts",
+    )(jobs, *parts, after)
+
+
+def combine_kernel(jobs, kept_out, kept_level, *refs):
+    parts, out, mixed = refs[:4], refs[4], refs[5]
+    slots, here, size = mixed.shape
+    mixed[...] = kept_out[...].reshape(mixed.shape)
+    for step, ref in enumerate(parts):
+        hit, context, _ = job_from(jobs, step)
+
+        @pl.when(hit)
+        def _():
+            fresh_level = join_lines(ref[here:], 0, here)
+            old_level = kept_level[pl.ds(pl.multiple_of(context * here, here), here)]
+            blended, _ = blend([mixed[context], ref[:here].astype(F32)], [old_level, fresh_level])
+            mixed[context] = blended
+
+    for head in range(here):
+        out[:, head * size : (head + 1) * size] = mixed[:, head, :].astype(BF16)
+
+
+def combine(jobs, kept_out, kept_level, parts, slots):
+    here = kept_out.shape[0] // slots
+    return pl.pallas_call(
+        combine_kernel,
+        in_specs=[whole(SMEM)] + [whole()] * 6,
+        out_specs=whole(),
+        out_shape=jax.ShapeDtypeStruct((slots, here * LANES), BF16),
+        scratch_shapes=[pltpu.VMEM((slots, here, LANES), F32)],
+        compiler_params=pltpu.CompilerParams(vmem_limit_bytes=LIMIT),
+        cost_estimate=SMALL,
+        name="combine",
+    )(jobs, kept_out, kept_level, *parts)
+
+
+def on_device(
+    hidden, norm_gain, kv_weight, restore_jobs, page_table, context_lengths, queries, kv_pool
+):
+    shards = lax.axis_size("shard")
+    replicas = lax.axis_size("rep")
+    stripe = hidden.shape[0] // SENDS
+    page_len = stripe // shards
+    kv_weight = pltpu.with_memory_space_constraint(kv_weight, pltpu.HBM)
+    kv_pool = pltpu.with_memory_space_constraint(kv_pool, pltpu.HBM)
+    gain = pltpu.with_memory_space_constraint(norm_gain, pltpu.HBM)
+    blocks = pltpu.with_memory_space_constraint(
+        hidden.reshape(SENDS, shards, page_len, hidden.shape[1]), pltpu.HBM
+    )
+    jobs = restore_jobs.T
+    table = page_table[:, :, 0].T
+    slots = queries.shape[0]
+    query = queries.reshape(slots, QH, HD)
+
+    def along(array, pairs):
+        return lax.ppermute(array, "shard", pairs)
+
+    def between(arrays):
+        return [arrays[0]] + [
+            lax.ppermute(arrays[step], "rep", [(i, i ^ step) for i in range(replicas)])
+            for step in range(1, replicas)
+        ]
+
+    sent = project_first(blocks, gain, kv_weight)
+    first = along(sent, FIRST)
+    asked = between(ask(jobs, query, sent))
+    key_0, key_1, key_2, value_0, value_1, value_2 = middle(blocks, gain, kv_weight, asked[1:])
+    key_near = along(key_1, NEAR)
+    value_near = along(value_1, NEAR)
+    width = key_2.shape[1]
+    carried = jnp.where(is_inner(lax.axis_index("shard")), first[:, :width].astype(F32), 0.0)
+    key_sum = (key_2.astype(F32) + carried).astype(BF16)
+    key_third = along(key_sum, THIRD)
+    *kept_parts, new_pool = kept(jobs, table, context_lengths, query, kv_pool, key_sum, shards)
+    value_third = along(carry(value_2, first, kept_parts[0]), THIRD)
+    frequency = THETA ** (-(jnp.arange(HD // 2, dtype=F32) * 2.0 / HD))
+    frequency = jnp.concatenate([frequency, frequency])[None, :]
+    *key_out, scale, weights, share, level = finish_keys(
+        jobs, (key_0, key_near, first, key_third), frequency, asked, stripe
+    )
+    key_pages = between(key_out)
+    finished = finish_values(
+        jobs, (value_0, value_near, first, value_third), scale, weights, share, level, kept_parts, shards
+    )
+    value_pages = between(finished[:4])
+    packed = finished[4:]
+    parts = [packed[0]] + [
+        along(packed[step], [(i, i ^ step) for i in range(shards)]) for step in range(1, shards)
+    ]
+    here = QH // shards
+    kept_out, kept_level, *fresh = gather_parts(jobs, parts, key_pages[3], slots * here, SENDS * here)
+    fresh = between(fresh)
+    new_pool = place_pages(jobs, table, new_pool, key_pages, value_pages)
+    return (new_pool, combine(jobs, kept_out, kept_level, fresh, slots))
+
+
 def solution(mesh):
     in_specs = (
         P(("outer", "rep"), "shard"),
@@ -153,6 +796,7 @@
         P(("outer", "rep", "shard"), None, None),
     )
     out_specs = (P(("outer", "rep", "shard"), None, None), P(("outer", "rep"), "shard"))
+    fast = mesh.shape["shard"] == 4 and mesh.shape["rep"] == 4
     return jax.shard_map(
-        on_device, mesh=mesh, in_specs=in_specs, out_specs=out_specs, check_vma=False
-    )
+        on_device if fast else on_device_general, mesh=mesh, in_specs=in_specs, out_specs=out_specs, check_vma=False
+    )

time: 155 us -> 69.9 us (0.45)
  waiting for transfers between devices: 64.7 us -> 23.1 us
  blocking collectives: 32.4 us -> 0 us
  Pallas kernels: 0 us -> 24.8 us
  local copies, waits for them, and re-layouts: 23 us -> 0.04 us
  starting transfers between devices: 3.6 us -> 20.3 us
  between operations: 14.3 us -> 0.79 us
  other arithmetic: 8.84 us -> 0.18 us
  matrix products: 7.73 us -> 0 us
    reduce_scatter x1 -> x0, waiting for transfers between devices: 28.4 us -> none  [on_device(): lax.psum_scatter(jnp.dot(arranged, kv_weight, preferred_element_type=jnp....]
    pallas_call x0 -> x10, Pallas kernels: none -> 24.8 us  [the longest x1 7 us: middle(): pl.pallas_call(functools.partial(middle_kernel, after=len(after)), in_spe...]
    ppermute x0 -> x20, waiting for transfers between devices: none -> 23.1 us  [the longest x8 18.3 us: along(): return lax.ppermute(array, 'shard', pairs)]
    psum x1 -> x0, waiting for transfers between devices: 23 us -> none  [on_device(): lax.psum(scaled_num.astype(jnp.bfloat16), 'shard').astype(jnp.float32)]
    psum x2 -> x0, blocking collectives: 22.6 us -> none  [the longest x1 13.6 us: on_device(): squares = lax.psum(jnp.sum(wide * wide, axis=1), 'shard')]
    ppermute x0 -> x20, starting transfers between devices: none -> 20.3 us  [the longest x8 14.1 us: along(): return lax.ppermute(array, 'shard', pairs)]
    all_to_all x1 -> x0, waiting for transfers between devices: 13.2 us -> none  [on_device(): lax.all_to_all(outgoing, 'rep', split_axis=0, concat_axis=0, tiled=True)]
    pmax x1 -> x0, blocking collectives: 9.75 us -> none  [on_device(): row_max = lax.pmax(local_max, 'shard')]
  transfers between devices with their start and end apart: 3 -> 20, of which waited for: 3 -> 10; matrix products, arithmetic and copies ran while one was open for 4% -> 0% of each run, Pallas kernels for 0% -> 27%
where the time goes in v1:
time: 69.9 us; the launch traced here: 69.2 us
  Pallas kernels  24.8 us (35%)
  waiting for transfers between devices  23.1 us (33%)
  starting transfers between devices  20.3 us (29%)
  between operations  0.79 us (1%)
    ppermute x8, waiting for transfers between devices, along(): return lax.ppermute(array, 'shard', pairs)  18.3 us
    ppermute x8, starting transfers between devices, along(): return lax.ppermute(array, 'shard', pairs)  14.1 us
    pallas_call x1, Pallas kernels, middle(): pl.pallas_call(functools.partial(middle_kernel, after=len(after)), in_spe...  7 us
    pallas_call x1, Pallas kernels, kept(): pl.pallas_call(functools.partial(kept_kernel, shards=shards), in_specs=[w...  6.24 us
    ppermute x12, starting transfers between devices, between(): lax.ppermute(arrays[step], 'rep', [(i, i ^ step) for i in range(replicas)])  6.12 us
    ppermute x12, waiting for transfers between devices, between(): lax.ppermute(arrays[step], 'rep', [(i, i ^ step) for i in range(replicas)])  4.82 us
    pallas_call x1, Pallas kernels, project_first(): pl.pallas_call(first_kernel, in_specs=[whole(pl.ANY)] * 3, out_specs=whol...  4.45 us
    pallas_call x1, Pallas kernels, combine(): pl.pallas_call(combine_kernel, in_specs=[whole(SMEM)] + [whole()] * 6, ou...  1.57 us
  transfers between devices with their start and end apart: 20, of which 10 were waited for; matrix products, arithmetic and copies ran while one was open for 0% of the time, Pallas kernels for 27%

profile of v1, /device:TPU:0, one launch (start us, length us, event | category | flops | bytes accessed | tf_op | source)
XLA Modules:
  0.0 69.2 jit_solution(506998658652479603)
XLA Ops:
  0.6 0.0 copy-start.3
  0.6 0.0 copy-start
  0.6 4.4 %project_first.1.after = bf16[128,2176]{1,0:T(8,128)(2,1)S(1)} custom-call(bf16[2,4,64,2048]{3,2,1,0:T(8,128)(2,1)} %bitcast.22, bf16[2048]{0:T(1024)(128)(2,1)} %gain.3, bf16[2048,2048]{1,0:T(8,128)(2,1)} %weight.3), custom_call_target="tpu_custom_call" | custom-call | flops 1 | bytes 1 | tf_op jit(solution)/shard_map/project_first/pallas_call | solution.py:238
  5.1 3.1 %collective-permute-start.3 = (bf16[128,2176]{1,0:T(8,128)(2,1)S(1)}, bf16[128,2176]{1,0:T(8,128)(2,1)S(1)}, u32[]{:S(2)}, u32[]{:S(2)}) collective-permute-start(bf16[128,2176]{1,0:T(8,128)(2,1)S(1)} %project_first.1.after), channel_id=1, source_target_pairs={{0,1},{3,2},{1,3},{2,0},{4,5},{7,6},{5,7},{6,4},{8,9},{11,10},{9,1... | collective-permute-start | bytes 1671176 | tf_op jit(solution)/shard_map/ppermute | solution.py:746
  8.2 0.0 copy-done.3
  8.2 0.0 copy-done
  8.2 0.6 ask.1
  8.8 0.1 collective-permute-start
  8.9 1.6 %collective-permute-start.1 = (bf16[64,128]{1,0:T(8,128)(2,1)S(1)}, bf16[64,128]{1,0:T(8,128)(2,1)S(1)}, u32[]{:S(2)}, u32[]{:S(2)}) collective-permute-start(bf16[64,128]{1,0:T(8,128)(2,1)S(1)} %get-tuple-element.40), channel_id=1, source_target_pairs={{0,8},{4,12},{8,0},{12,4},{1,9},{5,13},{9,1},{13,5},{2,10},{6,14},... | collective-permute-start | bytes 49160 | tf_op jit(solution)/shard_map/ppermute | solution.py:750
  10.5 0.3 collective-permute-start.2
  10.8 0.0 copy-start.1
  10.8 0.0 copy-start.2
  10.8 0.0 collective-permute-done.rest_0_.rest_1_
  10.8 1.9 %collective-permute-done.1.rest_1_.rest_2_ = bf16[64,128]{1,0:T(8,128)(2,1)S(1)} collective-permute-done((bf16[64,128]{1,0:T(8,128)(2,1)S(1)}, bf16[64,128]{1,0:T(8,128)(2,1)S(1)}, u32[]{:S(2)}, u32[]{:S(2)}) %collective-permute-start.1) | collective-permute-done | bytes 16416 | tf_op jit(solution)/shard_map/ppermute | solution.py:750
  12.7 0.9 %collective-permute-done.2.rest_2_.rest_3_ = bf16[64,128]{1,0:T(8,128)(2,1)S(1)} collective-permute-done((bf16[64,128]{1,0:T(8,128)(2,1)S(1)}, bf16[64,128]{1,0:T(8,128)(2,1)S(1)}, u32[]{:S(2)}, u32[]{:S(2)}) %collective-permute-start.2) | collective-permute-done | bytes 16416 | tf_op jit(solution)/shard_map/ppermute | solution.py:750
  13.6 7.0 %middle.1 = (bf16[128,1152]{1,0:T(8,128)(2,1)S(1)}, bf16[128,1152]{1,0:T(8,128)(2,1)S(1)}, bf16[128,1152]{1,0:T(8,128)(2,1)S(1)}, bf16[128,1024]{1,0:T(8,128)(2,...) custom-call(bf16[2,4,64,2048]{3,2,1,0:T(8,128)(2,1)} %bitcast.23, bf16[2048]{0:T(1024)(128)(2,1)} %gain.3, ...), custom_call_target="tpu_custom_call" | custom-call | flops 1 | bytes 1 | tf_op jit(solution)/shard_map/middle/pallas_call | solution.py:340
  20.6 2.7 %collective-permute-start.4 = (bf16[128,1152]{1,0:T(8,128)(2,1)S(1)}, bf16[128,1152]{1,0:T(8,128)(2,1)S(1)}, u32[]{:S(2)}, u32[]{:S(2)}) collective-permute-start(bf16[128,1152]{1,0:T(8,128)(2,1)S(1)} %get-tuple-element.45), channel_id=1, source_target_pairs={{0,1},{1,0},{2,3},{3,2},{4,5},{5,4},{6,7},{7,6},{8,9},{9,8},{10,11... | collective-permute-start | bytes 884744 | tf_op jit(solution)/shard_map/ppermute | solution.py:746
  23.3 0.0 collective-permute-done.3.first
  23.3 0.1 add_convert_fusion.after
  23.4 2.2 %collective-permute-start.5 = (bf16[128,1152]{1,0:T(8,128)(2,1)S(1)}, bf16[128,1152]{1,0:T(8,128)(2,1)S(1)}, u32[]{:S(2)}, u32[]{:S(2)}) collective-permute-start(bf16[128,1152]{1,0:T(8,128)(2,1)S(1)} %add_convert_fusion.after), channel_id=1, source_target_pairs={{0,3},{3,0},{1,2},{2,1},{4,7},{7,4},{5,6},{6,5},{8,11},{11,8},{9,1... | collective-permute-start | bytes 884744 | tf_op jit(solution)/shard_map/ppermute | solution.py:746
  25.6 0.0 collective-permute-start.9
  25.6 0.0 copy-done.1
  25.6 0.0 copy-done.2
  25.6 6.2 %kept.1 = (bf16[144,128]{1,0:T(8,128)(2,1)S(1)}, bf16[144,128]{1,0:T(8,128)(2,1)S(1)}, bf16[144,128]{1,0:T(8,128)(2,1)S(1)}, bf16[144,128]{1,0:T(8,128)(2,1)S(1)}, bf16[16,64,2048]{2,1,0:T(8,128)(2,1)}) custom-call(s32[3,8]{1,0:T(4,128)S(1)} %bitcast.14, s32[2,8]{1,0:T(2,128)S(1)} %bitcast.20, s32[8]{0:T(128)S(1)} %copy-done.2, ...), custom_call_target="tpu_custom_call" | custom-call | flops 1 | bytes 1 | tf_op jit(solution)/shard_map/kept/pallas_call | solution.py:433
  31.9 1.7 %collective-permute-start.10 = (bf16[128,1024]{1,0:T(8,128)(2,1)S(1)}, bf16[128,1024]{1,0:T(8,128)(2,1)S(1)}, u32[]{:S(2)}, u32[]{:S(2)}) collective-permute-start(bf16[128,1024]{1,0:T(8,128)(2,1)S(1)} %carry.1), channel_id=1, source_target_pairs={{0,3},{3,0},{1,2},{2,1},{4,7},{7,4},{5,6},{6,5},{8,11},{11,8},{9,1... | collective-permute-start | bytes 786440 | tf_op jit(solution)/shard_map/ppermute | solution.py:746
  33.6 0.1 maximum_bitcast_fusion.frequency
  33.7 3.5 %collective-permute-done.4.near = bf16[128,1152]{1,0:T(8,128)(2,1)S(1)} collective-permute-done((bf16[128,1152]{1,0:T(8,128)(2,1)S(1)}, bf16[128,1152]{1,0:T(8,128)(2,1)S(1)}, u32[]{:S(2)}, u32[]{:S(2)}) %collective-permute-start.4) | collective-permute-done | bytes 294944 | tf_op jit(solution)/shard_map/ppermute | solution.py:746
  37.2 0.4 collective-permute-done.5.third
  37.7 1.5 %finish_keys.1 = (bf16[64,1024]{1,0:T(8,128)(2,1)S(1)}, bf16[64,1024]{1,0:T(8,128)(2,1)S(1)}, bf16[64,1024]{1,0:T(8,128)(2,1)S(1)}, bf16[64,1024]{1,0:T(8,128)(2...) custom-call(s32[3,8]{1,0:T(4,128)S(1)} %bitcast.15, ...), custom_call_target="tpu_custom_call" | custom-call | flops 1 | bytes 1 | tf_op jit(solution)/shard_map/finish_keys/pallas_call | solution.py:572
  39.2 0.1 collective-permute-start.8
  39.3 4.0 %collective-permute-done.9.near = bf16[128,1024]{1,0:T(8,128)(2,1)S(1)} collective-permute-done((bf16[128,1024]{1,0:T(8,128)(2,1)S(1)}, bf16[128,1024]{1,0:T(8,128)(2,1)S(1)}, u32[]{:S(2)}, u32[]{:S(2)}) %collective-permute-start.9) | collective-permute-done | bytes 262176 | tf_op jit(solution)/shard_map/ppermute | solution.py:746
  43.3 5.3 %collective-permute-done.10.third = bf16[128,1024]{1,0:T(8,128)(2,1)S(1)} collective-permute-done((bf16[128,1024]{1,0:T(8,128)(2,1)S(1)}, bf16[128,1024]{1,0:T(8,128)(2,1)S(1)}, u32[]{:S(2)}, u32[]{:S(2)}) %collective-permute-start.10) | collective-permute-done | bytes 262176 | tf_op jit(solution)/shard_map/ppermute | solution.py:746
  48.6 1.0 %finish_values.1 = (bf16[64,1024]{1,0:T(8,128)(2,1)S(1)}, bf16[64,1024]{1,0:T(8,128)(2,1)S(1)}, bf16[64,1024]{1,0:T(8,128)(2,1)S(1)}, bf16[64,1024]{1,0:T(8,128)...) custom-call(s32[3,8]{1,0:T(4,128)S(1)} %bitcast.16, ...), custom_call_target="tpu_custom_call" | custom-call | flops 1 | bytes 1 | tf_op jit(solution)/shard_map/finish_values/pallas_call | solution.py:595
  49.6 1.9 %collective-permute-start.14 = (bf16[176,128]{1,0:T(8,128)(2,1)S(1)}, bf16[176,128]{1,0:T(8,128)(2,1)S(1)}, u32[]{:S(2)}, u32[]{:S(2)}) collective-permute-start(bf16[176,128]{1,0:T(8,128)(2,1)S(1)} %get-tuple-element.67), channel_id=1, source_target_pairs={{0,1},{1,0},{2,3},{3,2},{4,5},{5,4},{6,7},{7,6},{8,9},{9,8},{10,11... | collective-permute-start | bytes 135176 | tf_op jit(solution)/shard_map/ppermute | solution.py:746
  51.5 2.3 %collective-permute-start.15 = (bf16[176,128]{1,0:T(8,128)(2,1)S(1)}, bf16[176,128]{1,0:T(8,128)(2,1)S(1)}, u32[]{:S(2)}, u32[]{:S(2)}) collective-permute-start(bf16[176,128]{1,0:T(8,128)(2,1)S(1)} %get-tuple-element.68), channel_id=1, source_target_pairs={{0,2},{1,3},{2,0},{3,1},{4,6},{5,7},{6,4},{7,5},{8,10},{9,11},{10,... | collective-permute-start | bytes 135176 | tf_op jit(solution)/shard_map/ppermute | solution.py:746
  53.8 0.3 collective-permute-start.16
  54.1 0.0 collective-permute-start.6
  54.1 0.0 collective-permute-done.14.refs_1_
  54.1 0.5 collective-permute-start.7
  54.6 2.2 %collective-permute-done.15.refs_2_ = bf16[176,128]{1,0:T(8,128)(2,1)S(1)} collective-permute-done((bf16[176,128]{1,0:T(8,128)(2,1)S(1)}, bf16[176,128]{1,0:T(8,128)(2,1)S(1)}, u32[]{:S(2)}, u32[]{:S(2)}) %collective-permute-start.15) | collective-permute-done | bytes 45088 | tf_op jit(solution)/shard_map/ppermute | solution.py:746
  56.7 0.0 collective-permute-start.11
  56.7 2.9 %collective-permute-done.16.refs_3_ = bf16[176,128]{1,0:T(8,128)(2,1)S(1)} collective-permute-done((bf16[176,128]{1,0:T(8,128)(2,1)S(1)}, bf16[176,128]{1,0:T(8,128)(2,1)S(1)}, u32[]{:S(2)}, u32[]{:S(2)}) %collective-permute-start.16) | collective-permute-done | bytes 45088 | tf_op jit(solution)/shard_map/ppermute | solution.py:746
  59.6 0.6 collective-permute-start.12
  60.2 0.0 collective-permute-done.8.rest_3_.refs_4_
  60.2 0.0 collective-permute-start.13
  60.2 0.9 %gather_parts.1 = (f32[128,128]{1,0:T(8,128)S(1)}, f32[128,128]{1,0:T(8,128)S(1)}, bf16[32,128]{1,0:T(8,128)(2,1)S(1)}, bf16[32,128]{1,0:T(8,128)(2,1)S(1)}, bf1...) custom-call(s32[3,8]{1,0:T(4,128)S(1)} %bitcast.17, bf16[176,128]{1,0:T(8,128)(2,1)S(1)} %get-tuple-element.66.refs_0_, ...), custom_call_target="tpu_custom_call" | custom-call | flops 1 | bytes 1 | tf_op jit(solution)/shard_map/gather_parts/pallas_call | solution.py:683
  61.0 0.0 collective-permute-done.6.rest_1_
  61.1 1.7 %collective-permute-start.17 = (bf16[32,128]{1,0:T(8,128)(2,1)S(1)}, bf16[32,128]{1,0:T(8,128)(2,1)S(1)}, u32[]{:S(2)}, u32[]{:S(2)}) collective-permute-start(bf16[32,128]{1,0:T(8,128)(2,1)S(1)} %get-tuple-element.73), channel_id=1, source_target_pairs={{0,4},{4,0},{8,12},{12,8},{1,5},{5,1},{9,13},{13,9},{2,6},{6,2},{1... | collective-permute-start | bytes 24584 | tf_op jit(solution)/shard_map/ppermute | solution.py:750
  62.7 0.0 collective-permute-done.7.rest_2_
  62.7 0.6 collective-permute-start.18
  63.3 0.0 collective-permute-done.11.rest_5_
  63.3 0.9 %collective-permute-start.19 = (bf16[32,128]{1,0:T(8,128)(2,1)S(1)}, bf16[32,128]{1,0:T(8,128)(2,1)S(1)}, u32[]{:S(2)}, u32[]{:S(2)}) collective-permute-start(bf16[32,128]{1,0:T(8,128)(2,1)S(1)} %get-tuple-element.75), channel_id=1, source_target_pairs={{0,12},{4,8},{8,4},{12,0},{1,13},{5,9},{9,5},{13,1},{2,14},{6,10},... | collective-permute-start | bytes 24584 | tf_op jit(solution)/shard_map/ppermute | solution.py:750
  64.1 1.8 %collective-permute-done.12.rest_6_ = bf16[64,1024]{1,0:T(8,128)(2,1)S(1)} collective-permute-done((bf16[64,1024]{1,0:T(8,128)(2,1)S(1)}, bf16[64,1024]{1,0:T(8,128)(2,1)S(1)}, u32[]{:S(2)}, u32[]{:S(2)}) %collective-permute-start.12) | collective-permute-done | bytes 131104 | tf_op jit(solution)/shard_map/ppermute | solution.py:750
  66.0 0.0 collective-permute-done.13.rest_7_
  66.0 1.5 %place_pages.1 = bf16[16,64,2048]{2,1,0:T(8,128)(2,1)} custom-call(s32[3,8]{1,0:T(4,128)S(1)} %bitcast.18, s32[2,8]{1,0:T(2,128)S(1)} %bitcast.21, bf16[16,64,2048]{2,1,0:T(8,128)(2,1)} %get-tuple-element.43.pool, bf16[64,1024]{1,0:T(8,128)(2,1)S(1)} %get-tuple-element.47.rest_0_, ...), custom_call_target="tpu_custom_call", output_to_operand_aliasing={{}: (2, {})} | custom-call | flops 1 | bytes 1 | tf_op jit(solution)/shard_map/place_pages/pallas_call | solution.py:637
  67.5 0.0 collective-permute-done.17.refs_1_
  67.5 0.1 collective-permute-done.18.refs_2_
  67.6 0.0 collective-permute-done.19.refs_3_
  67.6 1.6 %combine.1 = bf16[8,2048]{1,0:T(8,128)(2,1)} custom-call(s32[3,8]{1,0:T(4,128)S(1)} %bitcast.19, f32[128,128]{1,0:T(8,128)S(1)} %get-tuple-element.70.kept_out, f32[128,128]{1,0:T(8,128)S(1)} %get-tuple-element.71.kept_level, bf16[32,128]{1,0:T(8,128)(2,1)S(1)} %get-tuple-element.72.refs_0_, bf16[32,128]{1,0:T(8,128)(2,1)S(1)} %collective-permute-done.17.refs_1_, ...), custom_call_target="tpu_custom_call" | custom-call | flops 1 | bytes 1 | tf_op jit(solution)/shard_map/combine/pallas_call | solution.py:715
  (3 shorter events, 0.1 us)
Async XLA Ops:
  0.6 7.6 %copy-start.3 = (bf16[8,8192]{1,0:T(8,128)(2,1)S(1)}, bf16[8,8192]{1,0:T(8,128)(2,1)}, u32[]{:S(2)}) copy-start(bf16[8,8192]{1,0:T(8,128)(2,1)} %param.14) | copy-start | bytes 393220
  0.6 7.6 %copy-start = (s32[8,3]{0,1:T(4,128)S(1)}, s32[8,3]{0,1:T(4,128)}, u32[]{:S(2)}) copy-start(s32[8,3]{0,1:T(4,128)} %param.11) | copy-start | bytes 292
  5.1 18.2 %collective-permute-start.3 = (bf16[128,2176]{1,0:T(8,128)(2,1)S(1)}, bf16[128,2176]{1,0:T(8,128)(2,1)S(1)}, u32[]{:S(2)}, u32[]{:S(2)}) collective-permute-start(bf16[128,2176]{1,0:T(8,128)(2,1)S(1)} %project_first.1.after), channel_id=1, source_target_pairs={{0,1},{3,2},{1,3},{2,0},{4,5},{7,6},{5,7},{6,4},{8,9},{11,10},{9,1... | collective-permute-start | bytes 1671176 | tf_op jit(solution)/shard_map/ppermute | solution.py:746
  8.8 1.9 %collective-permute-start = (bf16[64,128]{1,0:T(8,128)(2,1)S(1)}, bf16[64,128]{1,0:T(8,128)(2,1)S(1)}, u32[]{:S(2)}, u32[]{:S(2)}) collective-permute-start(bf16[64,128]{1,0:T(8,128)(2,1)S(1)} %get-tuple-element.39), channel_id=1, source_target_pairs={{0,4},{4,0},{8,12},{12,8},{1,5},{5,1},{9,13},{13,9},{2,6},{6,2},{1... | collective-permute-start | bytes 49160 | tf_op jit(solution)/shard_map/ppermute | solution.py:750
  8.9 3.8 %collective-permute-start.1 = (bf16[64,128]{1,0:T(8,128)(2,1)S(1)}, bf16[64,128]{1,0:T(8,128)(2,1)S(1)}, u32[]{:S(2)}, u32[]{:S(2)}) collective-permute-start(bf16[64,128]{1,0:T(8,128)(2,1)S(1)} %get-tuple-element.40), channel_id=1, source_target_pairs={{0,8},{4,12},{8,0},{12,4},{1,9},{5,13},{9,1},{13,5},{2,10},{6,14},... | collective-permute-start | bytes 49160 | tf_op jit(solution)/shard_map/ppermute | solution.py:750
  10.5 3.2 %collective-permute-start.2 = (bf16[64,128]{1,0:T(8,128)(2,1)S(1)}, bf16[64,128]{1,0:T(8,128)(2,1)S(1)}, u32[]{:S(2)}, u32[]{:S(2)}) collective-permute-start(bf16[64,128]{1,0:T(8,128)(2,1)S(1)} %get-tuple-element.41), channel_id=1, source_target_pairs={{0,12},{4,8},{8,4},{12,0},{1,13},{5,9},{9,5},{13,1},{2,14},{6,10},... | collective-permute-start | bytes 49160 | tf_op jit(solution)/shard_map/ppermute | solution.py:750
  10.8 14.9 %copy-start.1 = (s32[8,2,1]{0,2,1:T(1,128)S(1)}, s32[8,2,1]{0,2,1:T(1,128)}, u32[]{:S(2)}) copy-start(s32[8,2,1]{0,2,1:T(1,128)} %param.12) | copy-start | bytes 196
  10.8 14.9 %copy-start.2 = (s32[8]{0:T(128)S(1)}, s32[8]{0:T(128)}, u32[]{:S(2)}) copy-start(s32[8]{0:T(128)} %lengths.1) | copy-start | bytes 100
  20.6 16.6 %collective-permute-start.4 = (bf16[128,1152]{1,0:T(8,128)(2,1)S(1)}, bf16[128,1152]{1,0:T(8,128)(2,1)S(1)}, u32[]{:S(2)}, u32[]{:S(2)}) collective-permute-start(bf16[128,1152]{1,0:T(8,128)(2,1)S(1)} %get-tuple-element.45), channel_id=1, source_target_pairs={{0,1},{1,0},{2,3},{3,2},{4,5},{5,4},{6,7},{7,6},{8,9},{9,8},{10,11... | collective-permute-start | bytes 884744 | tf_op jit(solution)/shard_map/ppermute | solution.py:746
  23.4 14.3 %collective-permute-start.5 = (bf16[128,1152]{1,0:T(8,128)(2,1)S(1)}, bf16[128,1152]{1,0:T(8,128)(2,1)S(1)}, u32[]{:S(2)}, u32[]{:S(2)}) collective-permute-start(bf16[128,1152]{1,0:T(8,128)(2,1)S(1)} %add_convert_fusion.after), channel_id=1, source_target_pairs={{0,3},{3,0},{1,2},{2,1},{4,7},{7,4},{5,6},{6,5},{8,11},{11,8},{9,1... | collective-permute-start | bytes 884744 | tf_op jit(solution)/shard_map/ppermute | solution.py:746
  25.6 17.6 %collective-permute-start.9 = (bf16[128,1024]{1,0:T(8,128)(2,1)S(1)}, bf16[128,1024]{1,0:T(8,128)(2,1)S(1)}, u32[]{:S(2)}, u32[]{:S(2)}) collective-permute-start(bf16[128,1024]{1,0:T(8,128)(2,1)S(1)} %get-tuple-element.52), channel_id=1, source_target_pairs={{0,1},{1,0},{2,3},{3,2},{4,5},{5,4},{6,7},{7,6},{8,9},{9,8},{10,11... | collective-permute-start | bytes 786440 | tf_op jit(solution)/shard_map/ppermute | solution.py:746
  31.9 16.7 %collective-permute-start.10 = (bf16[128,1024]{1,0:T(8,128)(2,1)S(1)}, bf16[128,1024]{1,0:T(8,128)(2,1)S(1)}, u32[]{:S(2)}, u32[]{:S(2)}) collective-permute-start(bf16[128,1024]{1,0:T(8,128)(2,1)S(1)} %carry.1), channel_id=1, source_target_pairs={{0,3},{3,0},{1,2},{2,1},{4,7},{7,4},{5,6},{6,5},{8,11},{11,8},{9,1... | collective-permute-start | bytes 786440 | tf_op jit(solution)/shard_map/ppermute | solution.py:746
  39.2 21.0 %collective-permute-start.8 = (bf16[64,1024]{1,0:T(8,128)(2,1)S(1)}, bf16[64,1024]{1,0:T(8,128)(2,1)S(1)}, u32[]{:S(2)}, u32[]{:S(2)}) collective-permute-start(bf16[64,1024]{1,0:T(8,128)(2,1)S(1)} %get-tuple-element.50), channel_id=1, source_target_pairs={{0,12},{4,8},{8,4},{12,0},{1,13},{5,9},{9,5},{13,1},{2,14},{6,10},... | collective-permute-start | bytes 393224 | tf_op jit(solution)/shard_map/ppermute | solution.py:750
  49.6 4.5 %collective-permute-start.14 = (bf16[176,128]{1,0:T(8,128)(2,1)S(1)}, bf16[176,128]{1,0:T(8,128)(2,1)S(1)}, u32[]{:S(2)}, u32[]{:S(2)}) collective-permute-start(bf16[176,128]{1,0:T(8,128)(2,1)S(1)} %get-tuple-element.67), channel_id=1, source_target_pairs={{0,1},{1,0},{2,3},{3,2},{4,5},{5,4},{6,7},{7,6},{8,9},{9,8},{10,11... | collective-permute-start | bytes 135176 | tf_op jit(solution)/shard_map/ppermute | solution.py:746
  51.5 5.2 %collective-permute-start.15 = (bf16[176,128]{1,0:T(8,128)(2,1)S(1)}, bf16[176,128]{1,0:T(8,128)(2,1)S(1)}, u32[]{:S(2)}, u32[]{:S(2)}) collective-permute-start(bf16[176,128]{1,0:T(8,128)(2,1)S(1)} %get-tuple-element.68), channel_id=1, source_target_pairs={{0,2},{1,3},{2,0},{3,1},{4,6},{5,7},{6,4},{7,5},{8,10},{9,11},{10,... | collective-permute-start | bytes 135176 | tf_op jit(solution)/shard_map/ppermute | solution.py:746
  53.8 5.8 %collective-permute-start.16 = (bf16[176,128]{1,0:T(8,128)(2,1)S(1)}, bf16[176,128]{1,0:T(8,128)(2,1)S(1)}, u32[]{:S(2)}, u32[]{:S(2)}) collective-permute-start(bf16[176,128]{1,0:T(8,128)(2,1)S(1)} %get-tuple-element.69), channel_id=1, source_target_pairs={{0,3},{1,2},{2,1},{3,0},{4,7},{5,6},{6,5},{7,4},{8,11},{9,10},{10,... | collective-permute-start | bytes 135176 | tf_op jit(solution)/shard_map/ppermute | solution.py:746
  54.1 7.0 %collective-permute-start.6 = (bf16[64,1024]{1,0:T(8,128)(2,1)S(1)}, bf16[64,1024]{1,0:T(8,128)(2,1)S(1)}, u32[]{:S(2)}, u32[]{:S(2)}) collective-permute-start(bf16[64,1024]{1,0:T(8,128)(2,1)S(1)} %get-tuple-element.48), channel_id=1, source_target_pairs={{0,4},{4,0},{8,12},{12,8},{1,5},{5,1},{9,13},{13,9},{2,6},{6,2},{1... | collective-permute-start | bytes 393224 | tf_op jit(solution)/shard_map/ppermute | solution.py:750
  54.1 8.6 %collective-permute-start.7 = (bf16[64,1024]{1,0:T(8,128)(2,1)S(1)}, bf16[64,1024]{1,0:T(8,128)(2,1)S(1)}, u32[]{:S(2)}, u32[]{:S(2)}) collective-permute-start(bf16[64,1024]{1,0:T(8,128)(2,1)S(1)} %get-tuple-element.49), channel_id=1, source_target_pairs={{0,8},{4,12},{8,0},{12,4},{1,9},{5,13},{9,1},{13,5},{2,10},{6,14},... | collective-permute-start | bytes 393224 | tf_op jit(solution)/shard_map/ppermute | solution.py:750
  56.7 6.5 %collective-permute-start.11 = (bf16[64,1024]{1,0:T(8,128)(2,1)S(1)}, bf16[64,1024]{1,0:T(8,128)(2,1)S(1)}, u32[]{:S(2)}, u32[]{:S(2)}) collective-permute-start(bf16[64,1024]{1,0:T(8,128)(2,1)S(1)} %get-tuple-element.63), channel_id=1, source_target_pairs={{0,4},{4,0},{8,12},{12,8},{1,5},{5,1},{9,13},{13,9},{2,6},{6,2},{1... | collective-permute-start | bytes 393224 | tf_op jit(solution)/shard_map/ppermute | solution.py:750
  59.6 6.4 %collective-permute-start.12 = (bf16[64,1024]{1,0:T(8,128)(2,1)S(1)}, bf16[64,1024]{1,0:T(8,128)(2,1)S(1)}, u32[]{:S(2)}, u32[]{:S(2)}) collective-permute-start(bf16[64,1024]{1,0:T(8,128)(2,1)S(1)} %get-tuple-element.64), channel_id=1, source_target_pairs={{0,8},{4,12},{8,0},{12,4},{1,9},{5,13},{9,1},{13,5},{2,10},{6,14},... | collective-permute-start | bytes 393224 | tf_op jit(solution)/shard_map/ppermute | solution.py:750
  60.2 5.8 %collective-permute-start.13 = (bf16[64,1024]{1,0:T(8,128)(2,1)S(1)}, bf16[64,1024]{1,0:T(8,128)(2,1)S(1)}, u32[]{:S(2)}, u32[]{:S(2)}) collective-permute-start(bf16[64,1024]{1,0:T(8,128)(2,1)S(1)} %get-tuple-element.65), channel_id=1, source_target_pairs={{0,12},{4,8},{8,4},{12,0},{1,13},{5,9},{9,5},{13,1},{2,14},{6,10},... | collective-permute-start | bytes 393224 | tf_op jit(solution)/shard_map/ppermute | solution.py:750
  61.1 6.5 %collective-permute-start.17 = (bf16[32,128]{1,0:T(8,128)(2,1)S(1)}, bf16[32,128]{1,0:T(8,128)(2,1)S(1)}, u32[]{:S(2)}, u32[]{:S(2)}) collective-permute-start(bf16[32,128]{1,0:T(8,128)(2,1)S(1)} %get-tuple-element.73), channel_id=1, source_target_pairs={{0,4},{4,0},{8,12},{12,8},{1,5},{5,1},{9,13},{13,9},{2,6},{6,2},{1... | collective-permute-start | bytes 24584 | tf_op jit(solution)/shard_map/ppermute | solution.py:750
  62.7 4.9 %collective-permute-start.18 = (bf16[32,128]{1,0:T(8,128)(2,1)S(1)}, bf16[32,128]{1,0:T(8,128)(2,1)S(1)}, u32[]{:S(2)}, u32[]{:S(2)}) collective-permute-start(bf16[32,128]{1,0:T(8,128)(2,1)S(1)} %get-tuple-element.74), channel_id=1, source_target_pairs={{0,8},{4,12},{8,0},{12,4},{1,9},{5,13},{9,1},{13,5},{2,10},{6,14},... | collective-permute-start | bytes 24584 | tf_op jit(solution)/shard_map/ppermute | solution.py:750
  63.3 4.4 %collective-permute-start.19 = (bf16[32,128]{1,0:T(8,128)(2,1)S(1)}, bf16[32,128]{1,0:T(8,128)(2,1)S(1)}, u32[]{:S(2)}, u32[]{:S(2)}) collective-permute-start(bf16[32,128]{1,0:T(8,128)(2,1)S(1)} %get-tuple-element.75), channel_id=1, source_target_pairs={{0,12},{4,8},{8,4},{12,0},{1,13},{5,9},{9,5},{13,1},{2,14},{6,10},... | collective-permute-start | bytes 24584 | tf_op jit(solution)/shard_map/ppermute | solution.py:750

commit v2 on v1

--- a/solution.py
+++ b/solution.py
@@ -148,6 +148,7 @@
 NEAR = [(0, 1), (1, 0), (2, 3), (3, 2)]
 THIRD = [(0, 3), (3, 0), (1, 2), (2, 1)]
 LANES = 128
+GROUP = 2
 BF16 = jnp.bfloat16
 F32 = jnp.float32
 SMEM = pltpu.SMEM
@@ -303,58 +304,103 @@
     return jnp.broadcast_to(line, (LANES, LANES)).T[:rows]
 
 
-def middle_kernel(hidden, gain, weight, *rest, after):
-    keys, values = rest[after : after + 3], rest[after + 3 : after + 6]
-    rows_in, gained, gain_in, tiles, row_sem, gain_sem, tile_sem = rest[after + 6 :]
+def project_keys_kernel(hidden, gain, weight, after, own, near, third, gained, rows_in, gain_in, tile, *sems):
+    row_sem, gain_sem, tile_sem = sems
     shard = lax.axis_index("shard")
+    rows = own.shape[0]
     half = weight.shape[1] // 2
-    rows = values[0].shape[0]
     inner_block, outer_block = far_blocks(shard)
     blocks = [shard, jnp.bitwise_xor(shard, 1), jnp.where(is_inner(shard), inner_block, outer_block)]
     rows_here = row_copies(hidden, blocks, rows_in, row_sem)
-    tiles_here = weight_copies(weight, tiles, tile_sem)
+    tile_copy = pltpu.make_async_copy(weight.at[:, pl.ds(0, half)], tile, tile_sem)
     gain_copy = pltpu.make_async_copy(gain, gain_in, gain_sem)
     gain_copy.start()
-    for copy in rows_here + tiles_here:
+    for copy in rows_here:
         copy.start()
+    tile_copy.start()
     gain_copy.wait()
     for copy in rows_here:
         copy.wait()
     scale_rows(rows_in, gained, gain_in, slice(None))
-    for place, ref in enumerate(keys):
+    for place, ref in enumerate((own, near, third)):
         span = slice(place * rows, (place + 1) * rows)
         put_squares(rows_in, span, ref, slice(half, half + LANES), 2 if place == 2 else 0)
-    for side, refs in enumerate((keys, values)):
-        tiles_here[side].wait()
-        product = jnp.dot(gained[...], tiles[side], preferred_element_type=F32).astype(BF16)
-        for place, ref in enumerate(refs):
-            ref[:, :half] = product[place * rows : (place + 1) * rows]
-
-
-def middle(hidden, gain, weight, after):
+    tile_copy.wait()
+    product = jnp.dot(gained[...], tile[...], preferred_element_type=F32).astype(BF16)
+    for place, ref in enumerate((own, near, third)):
+        ref[:, :half] = product[place * rows : (place + 1) * rows]
+
+
+def project_keys(hidden, gain, weight, after):
     stripes, blocks, page_len, features = hidden.shape
     half = weight.shape[1] // 2
     rows = stripes * page_len
-    keys = jax.ShapeDtypeStruct((rows, half + LANES), BF16)
-    values = jax.ShapeDtypeStruct((rows, half), BF16)
-    return pl.pallas_call(
-        functools.partial(middle_kernel, after=len(after)),
-        in_specs=[whole(pl.ANY)] * (3 + len(after)),
-        out_specs=[whole()] * 6,
-        out_shape=[keys] * 3 + [values] * 3,
+    return pl.pallas_call(
+        project_keys_kernel,
+        in_specs=[whole(pl.ANY)] * 4,
+        out_specs=[whole()] * 4,
+        out_shape=[jax.ShapeDtypeStruct((rows, half + LANES), BF16)] * 3
+        + [jax.ShapeDtypeStruct((3 * rows, features), BF16)],
         scratch_shapes=[
             pltpu.VMEM((3 * rows, features), BF16),
-            pltpu.VMEM((3 * rows, features), BF16),
             pltpu.VMEM((features,), BF16),
-            pltpu.VMEM((2, features, half), BF16),
+            pltpu.VMEM((features, half), BF16),
             pltpu.SemaphoreType.DMA((3 * stripes,)),
             pltpu.SemaphoreType.DMA,
-            pltpu.SemaphoreType.DMA((2,)),
+            pltpu.SemaphoreType.DMA,
         ],
         compiler_params=pltpu.CompilerParams(vmem_limit_bytes=LIMIT),
         cost_estimate=SMALL,
-        name="middle",
-    )(hidden, gain, weight, *after)
+        name="project_keys",
+    )(hidden, gain, weight, after)
+
+
+def project_values_kernel(gained, weight, *rest):
+    own, near, third, tile, sem = rest[-5:]
+    rows, half = own.shape
+    tile_copy = pltpu.make_async_copy(weight.at[:, pl.ds(half, half)], tile, sem)
+    tile_copy.start()
+    tile_copy.wait()
+    product = jnp.dot(gained[...], tile[...], preferred_element_type=F32).astype(BF16)
+    for place, ref in enumerate((own, near, third)):
+        ref[...] = product[place * rows : (place + 1) * rows]
+
+
+def project_values(gained, weight, after):
+    half = weight.shape[1] // 2
+    return pl.pallas_call(
+        project_values_kernel,
+        in_specs=[whole()] + [whole(pl.ANY)] * (1 + len(after)),
+        out_specs=[whole()] * 3,
+        out_shape=[jax.ShapeDtypeStruct((gained.shape[0] // 3, half), BF16)] * 3,
+        scratch_shapes=[pltpu.VMEM((weight.shape[0], half), BF16), pltpu.SemaphoreType.DMA],
+        compiler_params=pltpu.CompilerParams(vmem_limit_bytes=LIMIT),
+        cost_estimate=SMALL,
+        name="project_values",
+    )(gained, weight, *after)
+
+
+def carry_kernel(mine, first, *rest, start):
+    out = rest[-1]
+    inner = is_inner(lax.axis_index("shard"))
+    arrived = first[:, start : start + mine.shape[1]].astype(F32)
+    out[...] = (mine[...].astype(F32) + jnp.where(inner, arrived, 0.0)).astype(BF16)
+
+
+def carry(mine, first, after, start):
+    return pl.pallas_call(
+        functools.partial(carry_kernel, start=start),
+        in_specs=[whole(), whole()] + [whole(pl.ANY)] * len(after),
+        out_specs=whole(),
+        out_shape=jax.ShapeDtypeStruct(mine.shape, BF16),
+        compiler_params=pltpu.CompilerParams(vmem_limit_bytes=LIMIT),
+        cost_estimate=SMALL,
+        name="carry",
+    )(mine, first, *after)
+
+
+def rep_shapes(rows, width):
+    return [jax.ShapeDtypeStruct((rows, width), BF16)] * 4
 
 
 def ask_kernel(jobs, query, after, *outs):
@@ -367,15 +413,16 @@
         ask_kernel,
         in_specs=[whole(SMEM), whole(), whole(pl.ANY)],
         out_specs=[whole()] * 4,
-        out_shape=[jax.ShapeDtypeStruct(query.shape[1:], BF16)] * 4,
+        out_shape=rep_shapes(*query.shape[1:]),
         compiler_params=pltpu.CompilerParams(vmem_limit_bytes=LIMIT),
         cost_estimate=SMALL,
         name="ask",
     )(jobs, query, after)
 
 
-def kept_kernel(jobs, table, lengths, query, pool, after, *rest, shards):
-    outs, new_pool, pages, total, level, in_sem, out_sem = rest[:4], *rest[4:]
+def kept_kernel(jobs, table, lengths, query, pool, *rest, shards, after):
+    outs = rest[after : after + 4]
+    new_pool, pages, total, level, in_sem, out_sem = rest[after + 4 :]
     slots, heads, _ = query.shape
     here = heads // shards
     rows = slots * here
@@ -397,24 +444,31 @@
         for page in range(2):
             copy_in(context, page).start()
 
-    @pl.loop(0, slots)
-    def _(context):
-        for page in range(2):
-            copy_in(context, page).wait()
-            copy_out(context, page).start()
+    lane = lax.broadcasted_iota(jnp.int32, (heads, 2 * page_len), 1)
+    page_of = lane // page_len
+    position = (page_of * shards + shard) * page_len + lane % page_len
+
+    def context_part(context):
         gone = [jnp.int32(0), jnp.int32(0)]
         for job in range(jobs.shape[1]):
             hit = (jobs[0, job] == replica) & (jobs[1, job] == context)
             for page in range(2):
                 gone[page] = gone[page] | (hit & (jobs[2, job] == page)).astype(jnp.int32)
-        lane = lax.broadcasted_iota(jnp.int32, (heads, 2 * page_len), 1)
-        page = lane // page_len
-        position = (page * shards + shard) * page_len + lane % page_len
-        usable = (position < lengths[context]) & (jnp.where(page == 0, gone[0], gone[1]) == 0)
+        usable = (position < lengths[context]) & (jnp.where(page_of == 0, gone[0], gone[1]) == 0)
         both = pages[pl.ds(context * 2, 2)].reshape(2 * page_len, 2 * half)
-        result, logarithm = attend(query[context], both[:, :half], both[:, half:], usable)
-        total[context] = result
-        level[context] = jnp.broadcast_to(logarithm, result.shape)
+        return attend(query[context], both[:, :half], both[:, half:], usable)
+
+    @pl.loop(0, slots // GROUP)
+    def _(index):
+        contexts = [index * GROUP + member for member in range(GROUP)]
+        for context in contexts:
+            for page in range(2):
+                copy_in(context, page).wait()
+                copy_out(context, page).start()
+        results = [context_part(context) for context in contexts]
+        for context, (result, logarithm) in zip(contexts, results):
+            total[context] = result
+            level[context] = jnp.broadcast_to(logarithm, result.shape)
 
     for step, out in enumerate(outs):
         start = pl.multiple_of(jnp.bitwise_xor(shard, step) * here, here)
@@ -431,8 +485,8 @@
 def kept(jobs, table, lengths, query, pool, after, shards):
     slots, heads, size = query.shape
     return pl.pallas_call(
-        functools.partial(kept_kernel, shards=shards),
-        in_specs=[whole(SMEM)] * 3 + [whole()] + [whole(pl.ANY)] * 2,
+        functools.partial(kept_kernel, shards=shards, after=len(after)),
+        in_specs=[whole(SMEM)] * 3 + [whole()] + [whole(pl.ANY)] * (1 + len(after)),
         out_specs=[whole()] * 4 + [whole(pl.ANY)],
         out_shape=[jax.ShapeDtypeStruct((slots * heads // shards + 16, size), BF16)] * 4
         + [jax.ShapeDtypeStruct(pool.shape, pool.dtype)],
@@ -446,32 +500,7 @@
         compiler_params=pltpu.CompilerParams(vmem_limit_bytes=LIMIT),
         cost_estimate=SMALL,
         name="kept",
-    )(jobs, table, lengths, query, pool, after)
-
-
-def carry_kernel(mine, first, after, out):
-    start = first.shape[1] - mine.shape[1]
-    inner = is_inner(lax.axis_index("shard"))
-
-    @pl.when(inner)
-    def _():
-        out[...] = (mine[...].astype(F32) + first[:, start:].astype(F32)).astype(BF16)
-
-    @pl.when(jnp.logical_not(inner))
-    def _():
-        out[...] = mine[...]
-
-
-def carry(mine, first, after):
-    return pl.pallas_call(
-        carry_kernel,
-        in_specs=[whole(), whole(), whole(pl.ANY)],
-        out_specs=whole(),
-        out_shape=jax.ShapeDtypeStruct(mine.shape, BF16),
-        compiler_params=pltpu.CompilerParams(vmem_limit_bytes=LIMIT),
-        cost_estimate=SMALL,
-        name="carry",
-    )(mine, first, after)
+    )(jobs, table, lengths, query, pool, *after)
 
 
 def route(jobs, finished, outs):
@@ -536,12 +565,13 @@
         level[send] = jnp.broadcast_to(largest + jnp.log(total), level.shape[1:])
 
 
-def finish_values_kernel(jobs, own, near, first, third, scale, weights, share, level, *rest, shards):
-    kept_parts, outs, packed, finished, result = rest[:4], rest[4:8], rest[8:12], rest[12], rest[13]
+def finish_values_kernel(jobs, own, near, first, third, scale, weights, share, level, *rest, shards, after):
+    kept_parts, outs = rest[:4], rest[4 + after : 8 + after]
+    packed, finished, result = rest[8 + after : 12 + after], rest[12 + after], rest[13 + after]
     shard = lax.axis_index("shard")
     for head in range(own.shape[1] // LANES):
         columns = slice(head * LANES, (head + 1) * LANES)
-        start = own.shape[1] + LANES + head * LANES
+        start = first.shape[1] - own.shape[1] + head * LANES
         total = add_parts(own, near, first, third, columns, slice(start, start + LANES))
         finished[:, columns] = (total * scale[...]).astype(BF16)
     route(jobs, finished, outs)
@@ -573,7 +603,7 @@
         functools.partial(finish_keys_kernel, stripe=stripe),
         in_specs=[whole(SMEM)] + [whole()] * 9,
         out_specs=[whole()] * 8,
-        out_shape=[jax.ShapeDtypeStruct((page_len, width), BF16)] * 4
+        out_shape=rep_shapes(page_len, width)
         + [
             jax.ShapeDtypeStruct((rows, LANES), F32),
             jax.ShapeDtypeStruct((SENDS, heads, page_len), BF16),
@@ -587,22 +617,21 @@
     )(jobs, *parts, frequency, *asked)
 
 
-def finish_values(jobs, parts, scale, weights, share, level, kept_parts, shards):
+def finish_values(jobs, parts, scale, weights, share, level, kept_parts, after, shards):
     rows, width = parts[0].shape
     heads = level.shape[1]
     page_len = rows // SENDS
     packed = kept_parts[0].shape[0] + SENDS * heads // shards
     return pl.pallas_call(
-        functools.partial(finish_values_kernel, shards=shards),
-        in_specs=[whole(SMEM)] + [whole()] * 12,
+        functools.partial(finish_values_kernel, shards=shards, after=len(after)),
+        in_specs=[whole(SMEM)] + [whole()] * 12 + [whole(pl.ANY)] * len(after),
         out_specs=[whole()] * 8,
-        out_shape=[jax.ShapeDtypeStruct((page_len, width), BF16)] * 4
-        + [jax.ShapeDtypeStruct((packed, LANES), BF16)] * 4,
+        out_shape=rep_shapes(page_len, width) + [jax.ShapeDtypeStruct((packed, LANES), BF16)] * 4,
         scratch_shapes=[pltpu.VMEM((rows, width), BF16), pltpu.VMEM((SENDS, heads, LANES), F32)],
         compiler_params=pltpu.CompilerParams(vmem_limit_bytes=LIMIT),
         cost_estimate=SMALL,
         name="finish_values",
-    )(jobs, *parts, scale, weights, share, level, *kept_parts)
+    )(jobs, *parts, scale, weights, share, level, *kept_parts, *after)
 
 
 def job_from(jobs, step):
@@ -615,8 +644,10 @@
 
 
 def place_kernel(jobs, table, pool, *rest):
-    key_pages, value_pages, out, pages, sem = rest[:4], rest[4:8], rest[8], rest[9], rest[10]
-    half = key_pages[0].shape[1]
+    key_pages, value_pages = rest[:4], rest[4:8]
+    out, done, pages, sem = rest[8:]
+    half = rest[0].shape[1]
+    done[...] = jnp.zeros_like(done)
     for wait in (False, True):
         for step in range(4):
             hit, context, page = job_from(jobs, step)
@@ -637,8 +668,8 @@
     return pl.pallas_call(
         place_kernel,
         in_specs=[whole(SMEM)] * 2 + [whole(pl.ANY)] + [whole()] * 8,
-        out_specs=whole(pl.ANY),
-        out_shape=jax.ShapeDtypeStruct(pool.shape, pool.dtype),
+        out_specs=[whole(pl.ANY), whole()],
+        out_shape=[jax.ShapeDtypeStruct(pool.shape, pool.dtype), jax.ShapeDtypeStruct((16, LANES), BF16)],
         scratch_shapes=[pltpu.VMEM((4,) + pool.shape[1:], pool.dtype), pltpu.SemaphoreType.DMA((4,))],
         input_output_aliases={2: 0},
         compiler_params=pltpu.CompilerParams(vmem_limit_bytes=LIMIT),
@@ -656,44 +687,62 @@
 
 
 def gather_kernel(jobs, *refs, rows, count):
-    parts, after, kept_out, kept_level, outs = refs[:4], refs[4], refs[5], refs[6], refs[7:]
-    tails = [ref[rows + count :] for ref in parts]
+    parts, page, outs, page_out = refs[:4], refs[4], refs[5:9], refs[9]
+    page_out[...] = page[...]
     mixed, level = blend(
-        [ref[:rows].astype(F32) for ref in parts], [join_lines(tail, 0, rows) for tail in tails]
+        [ref[rows : rows + count].astype(F32) for ref in parts],
+        [join_lines(ref[rows + count :], 3, count) for ref in parts],
+    )
+    here = count // SENDS
+    replica = lax.axis_index("rep")
+    lane = lax.broadcasted_iota(jnp.int32, (here, LANES), 1)
+    for step, out in enumerate(outs):
+        chosen = jobs[0, replica * SENDS] == jnp.bitwise_xor(replica, step)
+        total = jnp.where(chosen, level[:here], level[here:])
+        high = total.astype(BF16).astype(F32)
+        middle_part = (total - high).astype(BF16).astype(F32)
+        low = total - high - middle_part
+        out[:, :LANES] = jnp.where(chosen, mixed[:here], mixed[here:]).astype(BF16)
+        out[:, LANES:] = jnp.where(
+            lane == 0, high, jnp.where(lane == 1, middle_part, jnp.where(lane == 2, low, 0.0))
+        ).astype(BF16)
+
+
+def gather_parts(jobs, parts, page, rows, count):
+    return pl.pallas_call(
+        functools.partial(gather_kernel, rows=rows, count=count),
+        in_specs=[whole(SMEM)] + [whole()] * 5,
+        out_specs=[whole()] * 5,
+        out_shape=rep_shapes(count // SENDS, 2 * LANES) + [jax.ShapeDtypeStruct(page.shape, BF16)],
+        compiler_params=pltpu.CompilerParams(vmem_limit_bytes=LIMIT),
+        cost_estimate=SMALL,
+        name="gather_parts",
+    )(jobs, *parts, page)
+
+
+def blend_kernel(*refs, rows, count):
+    parts, after, kept_out, kept_level = refs[:4], refs[4], refs[5], refs[6]
+    mixed, level = blend(
+        [ref[:rows].astype(F32) for ref in parts], [join_lines(ref[rows + count :], 0, rows) for ref in parts]
     )
     kept_out[...] = mixed
     kept_level[...] = level
-    mixed, level = blend(
-        [ref[rows : rows + count].astype(F32) for ref in parts], [join_lines(tail, 3, count) for tail in tails]
-    )
-    here = count // SENDS
-    replica = lax.axis_index("rep")
-    lines = [
-        jnp.concatenate([level[send * here : (send + 1) * here], jnp.zeros((LANES - here, LANES), F32)], axis=0).T[:16]
-        for send in range(SENDS)
-    ]
-    for step, out in enumerate(outs):
-        chosen = jobs[0, replica * SENDS] == jnp.bitwise_xor(replica, step)
-        out[:here] = jnp.where(chosen, mixed[:here], mixed[here:]).astype(BF16)
-        out[here:] = split_lines(jnp.where(chosen, lines[0], lines[1]), 0).astype(BF16)
-
-
-def gather_parts(jobs, parts, after, rows, count):
-    here = count // SENDS
-    return pl.pallas_call(
-        functools.partial(gather_kernel, rows=rows, count=count),
-        in_specs=[whole(SMEM)] + [whole()] * 4 + [whole(pl.ANY)],
-        out_specs=[whole()] * 6,
-        out_shape=[jax.ShapeDtypeStruct((rows, LANES), F32)] * 2
-        + [jax.ShapeDtypeStruct((here + 16, LANES), BF16)] * 4,
-        compiler_params=pltpu.CompilerParams(vmem_limit_bytes=LIMIT),
-        cost_estimate=SMALL,
-        name="gather_parts",
-    )(jobs, *parts, after)
+
+
+def blend_kept(parts, after, rows, count):
+    return pl.pallas_call(
+        functools.partial(blend_kernel, rows=rows, count=count),
+        in_specs=[whole()] * 4 + [whole(pl.ANY)],
+        out_specs=[whole()] * 2,
+        out_shape=[jax.ShapeDtypeStruct((rows, LANES), F32)] * 2,
+        compiler_params=pltpu.CompilerParams(vmem_limit_bytes=LIMIT),
+        cost_estimate=SMALL,
+        name="blend_kept",
+    )(*parts, after)
 
 
 def combine_kernel(jobs, kept_out, kept_level, *refs):
-    parts, out, mixed = refs[:4], refs[4], refs[5]
+    parts, out, mixed = refs[:4], refs[5], refs[6]
     slots, here, size = mixed.shape
     mixed[...] = kept_out[...].reshape(mixed.shape)
     for step, ref in enumerate(parts):
@@ -701,27 +750,28 @@
 
         @pl.when(hit)
         def _():
-            fresh_level = join_lines(ref[here:], 0, here)
+            fresh_level = jnp.sum(ref[:, LANES:].astype(F32), axis=1, keepdims=True)
+            fresh_level = jnp.broadcast_to(fresh_level, (here, LANES))
             old_level = kept_level[pl.ds(pl.multiple_of(context * here, here), here)]
-            blended, _ = blend([mixed[context], ref[:here].astype(F32)], [old_level, fresh_level])
+            blended, _ = blend([mixed[context], ref[:, :LANES].astype(F32)], [old_level, fresh_level])
             mixed[context] = blended
 
     for head in range(here):
         out[:, head * size : (head + 1) * size] = mixed[:, head, :].astype(BF16)
 
 
-def combine(jobs, kept_out, kept_level, parts, slots):
+def combine(jobs, kept_out, kept_level, parts, after, slots):
     here = kept_out.shape[0] // slots
     return pl.pallas_call(
         combine_kernel,
-        in_specs=[whole(SMEM)] + [whole()] * 6,
+        in_specs=[whole(SMEM)] + [whole()] * 6 + [whole(pl.ANY)],
         out_specs=whole(),
         out_shape=jax.ShapeDtypeStruct((slots, here * LANES), BF16),
         scratch_shapes=[pltpu.VMEM((slots, here, LANES), F32)],
         compiler_params=pltpu.CompilerParams(vmem_limit_bytes=LIMIT),
         cost_estimate=SMALL,
         name="combine",
-    )(jobs, kept_out, kept_level, *parts)
+    )(jobs, kept_out, kept_level, *parts, after)
 
 
 def on_device(
@@ -745,43 +795,51 @@
     def along(array, pairs):
         return lax.ppermute(array, "shard", pairs)
 
+    def across(array, step):
+        return lax.ppermute(array, "rep", [(i, i ^ step) for i in range(replicas)])
+
     def between(arrays):
-        return [arrays[0]] + [
-            lax.ppermute(arrays[step], "rep", [(i, i ^ step) for i in range(replicas)])
-            for step in range(1, replicas)
-        ]
+        return [arrays[0]] + [across(arrays[step], step) for step in range(1, replicas)]
 
     sent = project_first(blocks, gain, kv_weight)
     first = along(sent, FIRST)
-    asked = between(ask(jobs, query, sent))
-    key_0, key_1, key_2, value_0, value_1, value_2 = middle(blocks, gain, kv_weight, asked[1:])
+    key_0, key_1, key_2, gained = project_keys(blocks, gain, kv_weight, sent)
     key_near = along(key_1, NEAR)
+    asked = between(ask(jobs, query, key_1))
+    key_third = along(carry(key_2, first, asked[1:], 0), THIRD)
+    value_0, value_1, value_2 = project_values(gained, kv_weight, asked[1:])
     value_near = along(value_1, NEAR)
-    width = key_2.shape[1]
-    carried = jnp.where(is_inner(lax.axis_index("shard")), first[:, :width].astype(F32), 0.0)
-    key_sum = (key_2.astype(F32) + carried).astype(BF16)
-    key_third = along(key_sum, THIRD)
-    *kept_parts, new_pool = kept(jobs, table, context_lengths, query, kv_pool, key_sum, shards)
-    value_third = along(carry(value_2, first, kept_parts[0]), THIRD)
+    value_third = along(carry(value_2, first, [key_near, key_third], key_2.shape[1]), THIRD)
     frequency = THETA ** (-(jnp.arange(HD // 2, dtype=F32) * 2.0 / HD))
     frequency = jnp.concatenate([frequency, frequency])[None, :]
     *key_out, scale, weights, share, level = finish_keys(
         jobs, (key_0, key_near, first, key_third), frequency, asked, stripe
     )
     key_pages = between(key_out)
+    *kept_parts, new_pool = kept(jobs, table, context_lengths, query, kv_pool, [scale], shards)
     finished = finish_values(
-        jobs, (value_0, value_near, first, value_third), scale, weights, share, level, kept_parts, shards
-    )
-    value_pages = between(finished[:4])
+        jobs,
+        (value_0, value_near, first, value_third),
+        scale,
+        weights,
+        share,
+        level,
+        kept_parts,
+        key_pages[1:],
+        shards,
+    )
+    value_pages = [finished[0], None, across(finished[2], 2), across(finished[3], 3)]
     packed = finished[4:]
     parts = [packed[0]] + [
         along(packed[step], [(i, i ^ step) for i in range(shards)]) for step in range(1, shards)
     ]
     here = QH // shards
-    kept_out, kept_level, *fresh = gather_parts(jobs, parts, key_pages[3], slots * here, SENDS * here)
-    fresh = between(fresh)
-    new_pool = place_pages(jobs, table, new_pool, key_pages, value_pages)
-    return (new_pool, combine(jobs, kept_out, kept_level, fresh, slots))
+    *gathered, near_page = gather_parts(jobs, parts, finished[1], slots * here, SENDS * here)
+    fresh = between(gathered)
+    value_pages[1] = across(near_page, 1)
+    kept_out, kept_level = blend_kept(parts, gathered[0], slots * here, SENDS * here)
+    new_pool, placed = place_pages(jobs, table, new_pool, key_pages, value_pages)
+    return (new_pool, combine(jobs, kept_out, kept_level, fresh, placed, slots))
 
 
 def solution(mesh):

time: 69.9 us -> 65.9 us (0.943)
  waiting for transfers between devices: 23.1 us -> 15.9 us
  starting transfers between devices: 20.3 us -> 22.7 us
  Pallas kernels: 24.8 us -> 26.2 us
    ppermute x8, waiting for transfers between devices: 18.3 us -> 13.8 us  [along(): return lax.ppermute(array, 'shard', pairs)]
    ppermute x12, waiting for transfers between devices: 4.82 us -> 2.09 us  [across(): return lax.ppermute(array, 'rep', [(i, i ^ step) for i in range(replicas)])]
    pallas_call x5 -> x8, Pallas kernels: 15.9 us -> 17.4 us  [the longest x1 6 us: kept(): pl.pallas_call(functools.partial(kept_kernel, shards=shards, after=len(af...]
    ppermute x12, starting transfers between devices: 6.12 us -> 7.39 us  [across(): return lax.ppermute(array, 'rep', [(i, i ^ step) for i in range(replicas)])]
    ppermute x8, starting transfers between devices: 14.1 us -> 15.3 us  [along(): return lax.ppermute(array, 'shard', pairs)]
  transfers between devices with their start and end apart: 20 -> 20, of which waited for: 10 -> 8; matrix products, arithmetic and copies ran while one was open for 0% -> 0% of each run, Pallas kernels for 27% -> 29%
where the time goes in v2:
time: 65.9 us; the launch traced here: 65.7 us
  Pallas kernels  26.2 us (40%)
  starting transfers between devices  22.7 us (34%)
  waiting for transfers between devices  15.9 us (24%)
  between operations  0.86 us (1%)
    ppermute x8, starting transfers between devices, along(): return lax.ppermute(array, 'shard', pairs)  15.3 us
    ppermute x8, waiting for transfers between devices, along(): return lax.ppermute(array, 'shard', pairs)  13.8 us
    ppermute x12, starting transfers between devices, across(): return lax.ppermute(array, 'rep', [(i, i ^ step) for i in range(replicas)])  7.39 us
    pallas_call x1, Pallas kernels, kept(): pl.pallas_call(functools.partial(kept_kernel, shards=shards, after=len(af...  6 us
    pallas_call x1, Pallas kernels, project_keys(): pl.pallas_call(project_keys_kernel, in_specs=[whole(pl.ANY)] * 4, out_spe...  4.56 us
    pallas_call x1, Pallas kernels, project_first(): pl.pallas_call(first_kernel, in_specs=[whole(pl.ANY)] * 3, out_specs=whol...  4.41 us
    pallas_call x1, Pallas kernels, project_values(): pl.pallas_call(project_values_kernel, in_specs=[whole()] + [whole(pl.ANY)...  4 us
    ppermute x12, waiting for transfers between devices, across(): return lax.ppermute(array, 'rep', [(i, i ^ step) for i in range(replicas)])  2.09 us
  transfers between devices with their start and end apart: 20, of which 8 were waited for; matrix products, arithmetic and copies ran while one was open for 0% of the time, Pallas kernels for 29%

profile of v2, /device:TPU:0, one launch (start us, length us, event | category | flops | bytes accessed | tf_op | source)
XLA Modules:
  0.0 65.7 jit_solution(9971556790439544937)
XLA Ops:
  0.6 4.4 %project_first.1.after = bf16[128,2176]{1,0:T(8,128)(2,1)S(1)} custom-call(bf16[2,4,64,2048]{3,2,1,0:T(8,128)(2,1)} %bitcast.22, bf16[2048]{0:T(1024)(128)(2,1)} %gain.3, bf16[2048,2048]{1,0:T(8,128)(2,1)} %weight.5), custom_call_target="tpu_custom_call" | custom-call | flops 1 | bytes 1 | tf_op jit(solution)/shard_map/project_first/pallas_call | solution.py:239
  5.0 0.0 copy-start.3
  5.1 0.0 copy-start
  5.1 3.1 %collective-permute-start.1 = (bf16[128,2176]{1,0:T(8,128)(2,1)S(1)}, bf16[128,2176]{1,0:T(8,128)(2,1)S(1)}, u32[]{:S(2)}, u32[]{:S(2)}) collective-permute-start(bf16[128,2176]{1,0:T(8,128)(2,1)S(1)} %project_first.1.after), channel_id=1, source_target_pairs={{0,1},{3,2},{1,3},{2,0},{4,5},{7,6},{5,7},{6,4},{8,9},{11,10},{9,1... | collective-permute-start | bytes 1671176 | tf_op jit(solution)/shard_map/ppermute | solution.py:796
  8.1 4.6 %project_keys.1 = (bf16[128,1152]{1,0:T(8,128)(2,1)S(1)}, bf16[128,1152]{1,0:T(8,128)(2,1)S(1)}, bf16[128,1152]{1,0:T(8,128)(2,1)S(1)}, bf16[384,2048]{1,0:T(8,128)(2,1)S(1)}) custom-call(bf16[2,4,64,2048]{3,2,1,0:T(8,128)(2,1)} %bitcast.23, bf16[2048]{0:T(1024)(128)(2,1)} %gain.3, bf16[2048,2048]{1,0:T(8,128)(2,1)} %weight.5, ...), custom_call_target="tpu_custom_call" | custom-call | flops 1 | bytes 1 | tf_op jit(solution)/shard_map/project_keys/pallas_call | solution.py:338
  12.7 0.0 copy-done.3
  12.7 0.0 copy-done
  12.8 0.6 ask.1
  13.4 0.1 collective-permute-start.2
  13.4 1.6 %collective-permute-start.3 = (bf16[64,128]{1,0:T(8,128)(2,1)S(1)}, bf16[64,128]{1,0:T(8,128)(2,1)S(1)}, u32[]{:S(2)}, u32[]{:S(2)}) collective-permute-start(bf16[64,128]{1,0:T(8,128)(2,1)S(1)} %get-tuple-element.47), channel_id=1, source_target_pairs={{0,8},{4,12},{8,0},{12,4},{1,9},{5,13},{9,1},{13,5},{2,10},{6,14},... | collective-permute-start | bytes 49160 | tf_op jit(solution)/shard_map/ppermute | solution.py:799
  15.0 0.3 collective-permute-start.4
  15.3 2.6 %collective-permute-start = (bf16[128,1152]{1,0:T(8,128)(2,1)S(1)}, bf16[128,1152]{1,0:T(8,128)(2,1)S(1)}, u32[]{:S(2)}, u32[]{:S(2)}) collective-permute-start(bf16[128,1152]{1,0:T(8,128)(2,1)S(1)} %get-tuple-element.44.after), channel_id=1, source_target_pairs={{0,1},{1,0},{2,3},{3,2},{4,5},{5,4},{6,7},{7,6},{8,9},{9,8},{10,11... | collective-permute-start | bytes 884744 | tf_op jit(solution)/shard_map/ppermute | solution.py:796
  17.9 0.0 collective-permute-done.2.rest_0_.rest_1_
  17.9 0.0 collective-permute-done.3.rest_1_.rest_2_
  17.9 0.3 collective-permute-done.4.rest_2_.rest_3_
  18.2 3.7 %collective-permute-done.1.first = bf16[128,2176]{1,0:T(8,128)(2,1)S(1)} collective-permute-done((bf16[128,2176]{1,0:T(8,128)(2,1)S(1)}, bf16[128,2176]{1,0:T(8,128)(2,1)S(1)}, u32[]{:S(2)}, u32[]{:S(2)}) %collective-permute-start.1) | collective-permute-done | bytes 557088 | tf_op jit(solution)/shard_map/ppermute | solution.py:796
  21.9 0.1 carry.2
  22.0 3.7 %collective-permute-start.5 = (bf16[128,1152]{1,0:T(8,128)(2,1)S(1)}, bf16[128,1152]{1,0:T(8,128)(2,1)S(1)}, u32[]{:S(2)}, u32[]{:S(2)}) collective-permute-start(bf16[128,1152]{1,0:T(8,128)(2,1)S(1)} %carry.2), channel_id=1, source_target_pairs={{0,3},{3,0},{1,2},{2,1},{4,7},{7,4},{5,6},{6,5},{8,11},{11,8},{9,1... | collective-permute-start | bytes 884744 | tf_op jit(solution)/shard_map/ppermute | solution.py:796
  25.7 0.0 copy-start.1
  25.7 0.0 copy-start.2
  25.7 4.0 %project_values.1 = (bf16[128,1024]{1,0:T(8,128)(2,1)S(1)}, bf16[128,1024]{1,0:T(8,128)(2,1)S(1)}, bf16[128,1024]{1,0:T(8,128)(2,1)S(1)}) custom-call(bf16[384,2048]{1,0:T(8,128)(2,1)S(1)} %get-tuple-element.56.gained, bf16[2048,2048]{1,0:T(8,128)(2,1)} %weight.5, bf16[64,128]{1,0:T(8,128)(2,1)S(1)} %collective-permute-done.2.rest_0_.rest_1_, ...), custom_call_target="tpu_custom_call" | custom-call | flops 1 | bytes 1 | tf_op jit(solution)/shard_map/project_values/pallas_call | solution.py:371
  29.7 0.1 collective-permute-start.9
  29.8 0.0 collective-permute-done.near.rest_0_
  29.8 7.0 %collective-permute-done.5.third.rest_1_ = bf16[128,1152]{1,0:T(8,128)(2,1)S(1)} collective-permute-done((bf16[128,1152]{1,0:T(8,128)(2,1)S(1)}, bf16[128,1152]{1,0:T(8,128)(2,1)S(1)}, u32[]{:S(2)}, u32[]{:S(2)}) %collective-permute-start.5) | collective-permute-done | bytes 294944 | tf_op jit(solution)/shard_map/ppermute | solution.py:796
  36.9 0.1 carry.3
  36.9 1.4 %collective-permute-start.10 = (bf16[128,1024]{1,0:T(8,128)(2,1)S(1)}, bf16[128,1024]{1,0:T(8,128)(2,1)S(1)}, u32[]{:S(2)}, u32[]{:S(2)}) collective-permute-start(bf16[128,1024]{1,0:T(8,128)(2,1)S(1)} %carry.3), channel_id=1, source_target_pairs={{0,3},{3,0},{1,2},{2,1},{4,7},{7,4},{5,6},{6,5},{8,11},{11,8},{9,1... | collective-permute-start | bytes 786440 | tf_op jit(solution)/shard_map/ppermute | solution.py:796
  38.3 0.1 maximum_bitcast_fusion.frequency
  38.4 1.5 %finish_keys.1 = (bf16[64,1024]{1,0:T(8,128)(2,1)S(1)}, bf16[64,1024]{1,0:T(8,128)(2,1)S(1)}, bf16[64,1024]{1,0:T(8,128)(2,1)S(1)}, bf16[64,1024]{1,0:T(8,128)(2...) custom-call(s32[3,8]{1,0:T(4,128)S(1)} %bitcast.14, ...), custom_call_target="tpu_custom_call" | custom-call | flops 1 | bytes 1 | tf_op jit(solution)/shard_map/finish_keys/pallas_call | solution.py:602
  39.9 0.1 collective-permute-start.6
  40.0 1.5 %collective-permute-start.7 = (bf16[64,1024]{1,0:T(8,128)(2,1)S(1)}, bf16[64,1024]{1,0:T(8,128)(2,1)S(1)}, u32[]{:S(2)}, u32[]{:S(2)}) collective-permute-start(bf16[64,1024]{1,0:T(8,128)(2,1)S(1)} %get-tuple-element.54), channel_id=1, source_target_pairs={{0,8},{4,12},{8,0},{12,4},{1,9},{5,13},{9,1},{13,5},{2,10},{6,14},... | collective-permute-start | bytes 393224 | tf_op jit(solution)/shard_map/ppermute | solution.py:799
  41.6 0.3 collective-permute-start.8
  41.9 0.0 copy-done.1
  41.9 0.0 copy-done.2
  41.9 6.0 %kept.1 = (bf16[144,128]{1,0:T(8,128)(2,1)S(1)}, bf16[144,128]{1,0:T(8,128)(2,1)S(1)}, bf16[144,128]{1,0:T(8,128)(2,1)S(1)}, bf16[144,128]{1,0:T(8,128)(2,1)S(1)}, bf16[16,64,2048]{2,1,0:T(8,128)(2,1)}) custom-call(s32[3,8]{1,0:T(4,128)S(1)} %bitcast.15, s32[2,8]{1,0:T(2,128)S(1)} %bitcast.20, s32[8]{0:T(128)S(1)} %copy-done.2, ...), custom_call_target="tpu_custom_call" | custom-call | flops 1 | bytes 1 | tf_op jit(solution)/shard_map/kept/pallas_call | solution.py:487
  47.9 0.0 collective-permute-done.9.near
  47.9 0.0 collective-permute-done.6.rest_4_.rest_1_
  47.9 0.0 collective-permute-done.7.rest_5_.rest_2_
  47.9 0.4 collective-permute-done.8.rest_6_.rest_3_
  48.3 0.0 collective-permute-done.10.third
  48.3 1.0 %finish_values.1 = (bf16[64,1024]{1,0:T(8,128)(2,1)S(1)}, bf16[64,1024]{1,0:T(8,128)(2,1)S(1)}, bf16[64,1024]{1,0:T(8,128)(2,1)S(1)}, bf16[64,1024]{1,0:T(8,128)...) custom-call(s32[3,8]{1,0:T(4,128)S(1)} %bitcast.16, ...), custom_call_target="tpu_custom_call" | custom-call | flops 1 | bytes 1 | tf_op jit(solution)/shard_map/finish_values/pallas_call | solution.py:625
  49.3 0.5 collective-permute-start.11
  49.9 2.6 %collective-permute-start.12 = (bf16[176,128]{1,0:T(8,128)(2,1)S(1)}, bf16[176,128]{1,0:T(8,128)(2,1)S(1)}, u32[]{:S(2)}, u32[]{:S(2)}) collective-permute-start(bf16[176,128]{1,0:T(8,128)(2,1)S(1)} %get-tuple-element.70), channel_id=1, source_target_pairs={{0,2},{1,3},{2,0},{3,1},{4,6},{5,7},{6,4},{7,5},{8,10},{9,11},{10,... | collective-permute-start | bytes 135176 | tf_op jit(solution)/shard_map/ppermute | solution.py:796
  52.5 1.3 %collective-permute-start.13 = (bf16[176,128]{1,0:T(8,128)(2,1)S(1)}, bf16[176,128]{1,0:T(8,128)(2,1)S(1)}, u32[]{:S(2)}, u32[]{:S(2)}) collective-permute-start(bf16[176,128]{1,0:T(8,128)(2,1)S(1)} %get-tuple-element.71), channel_id=1, source_target_pairs={{0,3},{1,2},{2,1},{3,0},{4,7},{5,6},{6,5},{7,4},{8,11},{9,10},{10,... | collective-permute-start | bytes 135176 | tf_op jit(solution)/shard_map/ppermute | solution.py:796
  53.8 1.5 %collective-permute-start.15 = (bf16[64,1024]{1,0:T(8,128)(2,1)S(1)}, bf16[64,1024]{1,0:T(8,128)(2,1)S(1)}, u32[]{:S(2)}, u32[]{:S(2)}) collective-permute-start(bf16[64,1024]{1,0:T(8,128)(2,1)S(1)} %get-tuple-element.74), channel_id=1, source_target_pairs={{0,8},{4,12},{8,0},{12,4},{1,9},{5,13},{9,1},{13,5},{2,10},{6,14},... | collective-permute-start | bytes 393224 | tf_op jit(solution)/shard_map/ppermute | solution.py:799
  55.3 0.0 collective-permute-start.16
  55.3 0.0 collective-permute-done.11.refs_1_
  55.3 0.8 %collective-permute-done.12.refs_2_ = bf16[176,128]{1,0:T(8,128)(2,1)S(1)} collective-permute-done((bf16[176,128]{1,0:T(8,128)(2,1)S(1)}, bf16[176,128]{1,0:T(8,128)(2,1)S(1)}, u32[]{:S(2)}, u32[]{:S(2)}) %collective-permute-start.12) | collective-permute-done | bytes 45088 | tf_op jit(solution)/shard_map/ppermute | solution.py:796
  56.1 2.3 %collective-permute-done.13.refs_3_ = bf16[176,128]{1,0:T(8,128)(2,1)S(1)} collective-permute-done((bf16[176,128]{1,0:T(8,128)(2,1)S(1)}, bf16[176,128]{1,0:T(8,128)(2,1)S(1)}, u32[]{:S(2)}, u32[]{:S(2)}) %collective-permute-start.13) | collective-permute-done | bytes 45088 | tf_op jit(solution)/shard_map/ppermute | solution.py:796
  58.3 0.7 %gather_parts.1 = (bf16[16,256]{1,0:T(8,128)(2,1)S(1)}, bf16[16,256]{1,0:T(8,128)(2,1)S(1)}, bf16[16,256]{1,0:T(8,128)(2,1)S(1)}, bf16[16,256]{1,0:T(8,128)(2,1)S(1)}, bf16[64,1024]{1,0:T(8,128)(2,1)S(1)}) custom-call(s32[3,8]{1,0:T(4,128)S(1)} %bitcast.17, bf16[176,128]{1,0:T(8,128)(2,1)S(1)} %get-tuple-element.68.refs_0_, ...), custom_call_target="tpu_custom_call" | custom-call | flops 1 | bytes 1 | tf_op jit(solution)/shard_map/gather_parts/pallas_call | solution.py:712
  59.1 0.1 collective-permute-start.14
  59.1 0.5 collective-permute-start.17
  59.6 1.5 %collective-permute-start.18 = (bf16[16,256]{1,0:T(8,128)(2,1)S(1)}, bf16[16,256]{1,0:T(8,128)(2,1)S(1)}, u32[]{:S(2)}, u32[]{:S(2)}) collective-permute-start(bf16[16,256]{1,0:T(8,128)(2,1)S(1)} %get-tuple-element.81), channel_id=1, source_target_pairs={{0,8},{4,12},{8,0},{12,4},{1,9},{5,13},{9,1},{13,5},{2,10},{6,14},... | collective-permute-start | bytes 24584 | tf_op jit(solution)/shard_map/ppermute | solution.py:799
  61.1 0.0 collective-permute-done.15.rest_6_
  61.1 0.0 collective-permute-start.19
  61.1 0.2 blend_kept.1
  61.3 0.0 collective-permute-done.16.rest_7_
  61.3 0.0 collective-permute-done.14.rest_5_
  61.3 1.4 %place_pages.1 = (bf16[16,64,2048]{2,1,0:T(8,128)(2,1)}, bf16[16,128]{1,0:T(8,128)(2,1)S(1)}) custom-call(s32[3,8]{1,0:T(4,128)S(1)} %bitcast.18, s32[2,8]{1,0:T(2,128)S(1)} %bitcast.21, bf16[16,64,2048]{2,1,0:T(8,128)(2,1)} %get-tuple-element.51.pool, bf16[64,1024]{1,0:T(8,128)(2,1)S(1)} %get-tuple-element.52.rest_0_, ...), custom_call_target="tpu_custom_call", output_to_operand_aliasing={{0}: (2, {})} | custom-call | flops 1 | bytes 1 | tf_op jit(solution)/shard_map/place_pages/pallas_call | solution.py:668
  62.8 0.0 collective-permute-done.17.refs_1_
  62.8 0.5 collective-permute-done.18.refs_2_
  63.3 1.0 %collective-permute-done.19.refs_3_ = bf16[16,256]{1,0:T(8,128)(2,1)S(1)} collective-permute-done((bf16[16,256]{1,0:T(8,128)(2,1)S(1)}, bf16[16,256]{1,0:T(8,128)(2,1)S(1)}, u32[]{:S(2)}, u32[]{:S(2)}) %collective-permute-start.19) | collective-permute-done | bytes 8224 | tf_op jit(solution)/shard_map/ppermute | solution.py:799
  64.3 1.5 %combine.1 = bf16[8,2048]{1,0:T(8,128)(2,1)} custom-call(s32[3,8]{1,0:T(4,128)S(1)} %bitcast.19, f32[128,128]{1,0:T(8,128)S(1)} %get-tuple-element.78.kept_out, f32[128,128]{1,0:T(8,128)S(1)} %get-tuple-element.79.kept_level, bf16[16,256]{1,0:T(8,128)(2,1)S(1)} %get-tuple-element.77.refs_4_.refs_0_, bf16[16,256]{1,0:T(8,128)(2,1)S(1)} %collective-permute-done.17.refs_1_, ...), custom_call_target="tpu_custom_call" | custom-call | flops 1 | bytes 1 | tf_op jit(solution)/shard_map/combine/pallas_call | solution.py:765
  (2 shorter events, 0.0 us)
Async XLA Ops:
  5.0 7.7 %copy-start.3 = (bf16[8,8192]{1,0:T(8,128)(2,1)S(1)}, bf16[8,8192]{1,0:T(8,128)(2,1)}, u32[]{:S(2)}) copy-start(bf16[8,8192]{1,0:T(8,128)(2,1)} %param.14) | copy-start | bytes 393220
  5.1 7.7 %copy-start = (s32[8,3]{0,1:T(4,128)S(1)}, s32[8,3]{0,1:T(4,128)}, u32[]{:S(2)}) copy-start(s32[8,3]{0,1:T(4,128)} %param.11) | copy-start | bytes 292
  5.1 16.8 %collective-permute-start.1 = (bf16[128,2176]{1,0:T(8,128)(2,1)S(1)}, bf16[128,2176]{1,0:T(8,128)(2,1)S(1)}, u32[]{:S(2)}, u32[]{:S(2)}) collective-permute-start(bf16[128,2176]{1,0:T(8,128)(2,1)S(1)} %project_first.1.after), channel_id=1, source_target_pairs={{0,1},{3,2},{1,3},{2,0},{4,5},{7,6},{5,7},{6,4},{8,9},{11,10},{9,1... | collective-permute-start | bytes 1671176 | tf_op jit(solution)/shard_map/ppermute | solution.py:796
  13.4 4.5 %collective-permute-start.2 = (bf16[64,128]{1,0:T(8,128)(2,1)S(1)}, bf16[64,128]{1,0:T(8,128)(2,1)S(1)}, u32[]{:S(2)}, u32[]{:S(2)}) collective-permute-start(bf16[64,128]{1,0:T(8,128)(2,1)S(1)} %get-tuple-element.46), channel_id=1, source_target_pairs={{0,4},{4,0},{8,12},{12,8},{1,5},{5,1},{9,13},{13,9},{2,6},{6,2},{1... | collective-permute-start | bytes 49160 | tf_op jit(solution)/shard_map/ppermute | solution.py:799
  13.4 4.5 %collective-permute-start.3 = (bf16[64,128]{1,0:T(8,128)(2,1)S(1)}, bf16[64,128]{1,0:T(8,128)(2,1)S(1)}, u32[]{:S(2)}, u32[]{:S(2)}) collective-permute-start(bf16[64,128]{1,0:T(8,128)(2,1)S(1)} %get-tuple-element.47), channel_id=1, source_target_pairs={{0,8},{4,12},{8,0},{12,4},{1,9},{5,13},{9,1},{13,5},{2,10},{6,14},... | collective-permute-start | bytes 49160 | tf_op jit(solution)/shard_map/ppermute | solution.py:799
  15.0 3.2 %collective-permute-start.4 = (bf16[64,128]{1,0:T(8,128)(2,1)S(1)}, bf16[64,128]{1,0:T(8,128)(2,1)S(1)}, u32[]{:S(2)}, u32[]{:S(2)}) collective-permute-start(bf16[64,128]{1,0:T(8,128)(2,1)S(1)} %get-tuple-element.48), channel_id=1, source_target_pairs={{0,12},{4,8},{8,4},{12,0},{1,13},{5,9},{9,5},{13,1},{2,14},{6,10},... | collective-permute-start | bytes 49160 | tf_op jit(solution)/shard_map/ppermute | solution.py:799
  15.3 14.5 %collective-permute-start = (bf16[128,1152]{1,0:T(8,128)(2,1)S(1)}, bf16[128,1152]{1,0:T(8,128)(2,1)S(1)}, u32[]{:S(2)}, u32[]{:S(2)}) collective-permute-start(bf16[128,1152]{1,0:T(8,128)(2,1)S(1)} %get-tuple-element.44.after), channel_id=1, source_target_pairs={{0,1},{1,0},{2,3},{3,2},{4,5},{5,4},{6,7},{7,6},{8,9},{9,8},{10,11... | collective-permute-start | bytes 884744 | tf_op jit(solution)/shard_map/ppermute | solution.py:796
  22.0 14.9 %collective-permute-start.5 = (bf16[128,1152]{1,0:T(8,128)(2,1)S(1)}, bf16[128,1152]{1,0:T(8,128)(2,1)S(1)}, u32[]{:S(2)}, u32[]{:S(2)}) collective-permute-start(bf16[128,1152]{1,0:T(8,128)(2,1)S(1)} %carry.2), channel_id=1, source_target_pairs={{0,3},{3,0},{1,2},{2,1},{4,7},{7,4},{5,6},{6,5},{8,11},{11,8},{9,1... | collective-permute-start | bytes 884744 | tf_op jit(solution)/shard_map/ppermute | solution.py:796
  25.7 16.2 %copy-start.1 = (s32[8,2,1]{0,2,1:T(1,128)S(1)}, s32[8,2,1]{0,2,1:T(1,128)}, u32[]{:S(2)}) copy-start(s32[8,2,1]{0,2,1:T(1,128)} %param.12) | copy-start | bytes 196
  25.7 16.2 %copy-start.2 = (s32[8]{0:T(128)S(1)}, s32[8]{0:T(128)}, u32[]{:S(2)}) copy-start(s32[8]{0:T(128)} %lengths.1) | copy-start | bytes 100
  29.7 18.2 %collective-permute-start.9 = (bf16[128,1024]{1,0:T(8,128)(2,1)S(1)}, bf16[128,1024]{1,0:T(8,128)(2,1)S(1)}, u32[]{:S(2)}, u32[]{:S(2)}) collective-permute-start(bf16[128,1024]{1,0:T(8,128)(2,1)S(1)} %get-tuple-element.58), channel_id=1, source_target_pairs={{0,1},{1,0},{2,3},{3,2},{4,5},{5,4},{6,7},{7,6},{8,9},{9,8},{10,11... | collective-permute-start | bytes 786440 | tf_op jit(solution)/shard_map/ppermute | solution.py:796
  36.9 11.3 %collective-permute-start.10 = (bf16[128,1024]{1,0:T(8,128)(2,1)S(1)}, bf16[128,1024]{1,0:T(8,128)(2,1)S(1)}, u32[]{:S(2)}, u32[]{:S(2)}) collective-permute-start(bf16[128,1024]{1,0:T(8,128)(2,1)S(1)} %carry.3), channel_id=1, source_target_pairs={{0,3},{3,0},{1,2},{2,1},{4,7},{7,4},{5,6},{6,5},{8,11},{11,8},{9,1... | collective-permute-start | bytes 786440 | tf_op jit(solution)/shard_map/ppermute | solution.py:796
  39.9 8.0 %collective-permute-start.6 = (bf16[64,1024]{1,0:T(8,128)(2,1)S(1)}, bf16[64,1024]{1,0:T(8,128)(2,1)S(1)}, u32[]{:S(2)}, u32[]{:S(2)}) collective-permute-start(bf16[64,1024]{1,0:T(8,128)(2,1)S(1)} %get-tuple-element.53), channel_id=1, source_target_pairs={{0,4},{4,0},{8,12},{12,8},{1,5},{5,1},{9,13},{13,9},{2,6},{6,2},{1... | collective-permute-start | bytes 393224 | tf_op jit(solution)/shard_map/ppermute | solution.py:799
  40.0 7.9 %collective-permute-start.7 = (bf16[64,1024]{1,0:T(8,128)(2,1)S(1)}, bf16[64,1024]{1,0:T(8,128)(2,1)S(1)}, u32[]{:S(2)}, u32[]{:S(2)}) collective-permute-start(bf16[64,1024]{1,0:T(8,128)(2,1)S(1)} %get-tuple-element.54), channel_id=1, source_target_pairs={{0,8},{4,12},{8,0},{12,4},{1,9},{5,13},{9,1},{13,5},{2,10},{6,14},... | collective-permute-start | bytes 393224 | tf_op jit(solution)/shard_map/ppermute | solution.py:799
  41.6 6.7 %collective-permute-start.8 = (bf16[64,1024]{1,0:T(8,128)(2,1)S(1)}, bf16[64,1024]{1,0:T(8,128)(2,1)S(1)}, u32[]{:S(2)}, u32[]{:S(2)}) collective-permute-start(bf16[64,1024]{1,0:T(8,128)(2,1)S(1)} %get-tuple-element.55), channel_id=1, source_target_pairs={{0,12},{4,8},{8,4},{12,0},{1,13},{5,9},{9,5},{13,1},{2,14},{6,10},... | collective-permute-start | bytes 393224 | tf_op jit(solution)/shard_map/ppermute | solution.py:799
  49.3 5.9 %collective-permute-start.11 = (bf16[176,128]{1,0:T(8,128)(2,1)S(1)}, bf16[176,128]{1,0:T(8,128)(2,1)S(1)}, u32[]{:S(2)}, u32[]{:S(2)}) collective-permute-start(bf16[176,128]{1,0:T(8,128)(2,1)S(1)} %get-tuple-element.69), channel_id=1, source_target_pairs={{0,1},{1,0},{2,3},{3,2},{4,5},{5,4},{6,7},{7,6},{8,9},{9,8},{10,11... | collective-permute-start | bytes 135176 | tf_op jit(solution)/shard_map/ppermute | solution.py:796
  49.9 6.2 %collective-permute-start.12 = (bf16[176,128]{1,0:T(8,128)(2,1)S(1)}, bf16[176,128]{1,0:T(8,128)(2,1)S(1)}, u32[]{:S(2)}, u32[]{:S(2)}) collective-permute-start(bf16[176,128]{1,0:T(8,128)(2,1)S(1)} %get-tuple-element.70), channel_id=1, source_target_pairs={{0,2},{1,3},{2,0},{3,1},{4,6},{5,7},{6,4},{7,5},{8,10},{9,11},{10,... | collective-permute-start | bytes 135176 | tf_op jit(solution)/shard_map/ppermute | solution.py:796
  52.5 5.8 %collective-permute-start.13 = (bf16[176,128]{1,0:T(8,128)(2,1)S(1)}, bf16[176,128]{1,0:T(8,128)(2,1)S(1)}, u32[]{:S(2)}, u32[]{:S(2)}) collective-permute-start(bf16[176,128]{1,0:T(8,128)(2,1)S(1)} %get-tuple-element.71), channel_id=1, source_target_pairs={{0,3},{1,2},{2,1},{3,0},{4,7},{5,6},{6,5},{7,4},{8,11},{9,10},{10,... | collective-permute-start | bytes 135176 | tf_op jit(solution)/shard_map/ppermute | solution.py:796
  53.8 7.3 %collective-permute-start.15 = (bf16[64,1024]{1,0:T(8,128)(2,1)S(1)}, bf16[64,1024]{1,0:T(8,128)(2,1)S(1)}, u32[]{:S(2)}, u32[]{:S(2)}) collective-permute-start(bf16[64,1024]{1,0:T(8,128)(2,1)S(1)} %get-tuple-element.74), channel_id=1, source_target_pairs={{0,8},{4,12},{8,0},{12,4},{1,9},{5,13},{9,1},{13,5},{2,10},{6,14},... | collective-permute-start | bytes 393224 | tf_op jit(solution)/shard_map/ppermute | solution.py:799
  55.3 6.0 %collective-permute-start.16 = (bf16[64,1024]{1,0:T(8,128)(2,1)S(1)}, bf16[64,1024]{1,0:T(8,128)(2,1)S(1)}, u32[]{:S(2)}, u32[]{:S(2)}) collective-permute-start(bf16[64,1024]{1,0:T(8,128)(2,1)S(1)} %get-tuple-element.75), channel_id=1, source_target_pairs={{0,12},{4,8},{8,4},{12,0},{1,13},{5,9},{9,5},{13,1},{2,14},{6,10},... | collective-permute-start | bytes 393224 | tf_op jit(solution)/shard_map/ppermute | solution.py:799
  59.1 2.3 %collective-permute-start.14 = (bf16[64,1024]{1,0:T(8,128)(2,1)S(1)}, bf16[64,1024]{1,0:T(8,128)(2,1)S(1)}, u32[]{:S(2)}, u32[]{:S(2)}) collective-permute-start(bf16[64,1024]{1,0:T(8,128)(2,1)S(1)} %get-tuple-element.73), channel_id=1, source_target_pairs={{0,4},{4,0},{8,12},{12,8},{1,5},{5,1},{9,13},{13,9},{2,6},{6,2},{1... | collective-permute-start | bytes 393224 | tf_op jit(solution)/shard_map/ppermute | solution.py:799
  59.1 3.7 %collective-permute-start.17 = (bf16[16,256]{1,0:T(8,128)(2,1)S(1)}, bf16[16,256]{1,0:T(8,128)(2,1)S(1)}, u32[]{:S(2)}, u32[]{:S(2)}) collective-permute-start(bf16[16,256]{1,0:T(8,128)(2,1)S(1)} %get-tuple-element.80), channel_id=1, source_target_pairs={{0,4},{4,0},{8,12},{12,8},{1,5},{5,1},{9,13},{13,9},{2,6},{6,2},{1... | collective-permute-start | bytes 24584 | tf_op jit(solution)/shard_map/ppermute | solution.py:799
  59.6 3.7 %collective-permute-start.18 = (bf16[16,256]{1,0:T(8,128)(2,1)S(1)}, bf16[16,256]{1,0:T(8,128)(2,1)S(1)}, u32[]{:S(2)}, u32[]{:S(2)}) collective-permute-start(bf16[16,256]{1,0:T(8,128)(2,1)S(1)} %get-tuple-element.81), channel_id=1, source_target_pairs={{0,8},{4,12},{8,0},{12,4},{1,9},{5,13},{9,1},{13,5},{2,10},{6,14},... | collective-permute-start | bytes 24584 | tf_op jit(solution)/shard_map/ppermute | solution.py:799
  61.1 3.1 %collective-permute-start.19 = (bf16[16,256]{1,0:T(8,128)(2,1)S(1)}, bf16[16,256]{1,0:T(8,128)(2,1)S(1)}, u32[]{:S(2)}, u32[]{:S(2)}) collective-permute-start(bf16[16,256]{1,0:T(8,128)(2,1)S(1)} %get-tuple-element.82), channel_id=1, source_target_pairs={{0,12},{4,8},{8,4},{12,0},{1,13},{5,9},{9,5},{13,1},{2,14},{6,10},... | collective-permute-start | bytes 24584 | tf_op jit(solution)/shard_map/ppermute | solution.py:799

commit v3 on v2

--- a/solution.py
+++ b/solution.py
@@ -181,14 +181,6 @@
     ]
 
 
-def weight_copies(weight, tiles, sem):
-    half = weight.shape[1] // 2
-    return [
-        pltpu.make_async_copy(weight.at[:, pl.ds(side * half, half)], tiles.at[side], sem.at[side])
-        for side in range(2)
-    ]
-
-
 def scale_rows(rows_in, gained, gain_in, span):
     wide_gain = gain_in[...].astype(F32).reshape(1, gain_in.shape[0])
     gained[span] = (rows_in[span].astype(F32) * wide_gain).astype(BF16)
@@ -212,106 +204,11 @@
     return jnp.where(lower, 2, 1), jnp.where(lower, 3, 0)
 
 
-def first_kernel(hidden, gain, weight, out, rows_in, gained, gain_in, tiles, row_sem, gain_sem, tile_sem):
+def first_kernel(hidden, gain, weight, out, gained, tile, rows_in, gain_in, row_sem, gain_sem, tile_sem):
     shard = lax.axis_index("shard")
     half = weight.shape[1] // 2
     inner_block, outer_block = far_blocks(shard)
     rows_here = row_copies(hidden, [jnp.where(is_inner(shard), outer_block, inner_block)], rows_in, row_sem)
-    tiles_here = weight_copies(weight, tiles, tile_sem)
-    gain_copy = pltpu.make_async_copy(gain, gain_in, gain_sem)
-    gain_copy.start()
-    for copy in rows_here + tiles_here:
-        copy.start()
-    gain_copy.wait()
-    for copy in rows_here:
-        copy.wait()
-    scale_rows(rows_in, gained, gain_in, slice(None))
-    put_squares(rows_in, slice(None), out, slice(half, half + LANES), 0)
-    for side, columns in enumerate((slice(0, half), slice(half + LANES, 2 * half + LANES))):
-        tiles_here[side].wait()
-        out[:, columns] = jnp.dot(gained[...], tiles[side], preferred_element_type=F32).astype(BF16)
-
-
-def project_first(hidden, gain, weight):
-    stripes, blocks, page_len, features = hidden.shape
-    half = weight.shape[1] // 2
-    rows = stripes * page_len
-    return pl.pallas_call(
-        first_kernel,
-        in_specs=[whole(pl.ANY)] * 3,
-        out_specs=whole(),
-        out_shape=jax.ShapeDtypeStruct((rows, 2 * half + LANES), BF16),
-        scratch_shapes=[
-            pltpu.VMEM((rows, features), BF16),
-            pltpu.VMEM((rows, features), BF16),
-            pltpu.VMEM((features,), BF16),
-            pltpu.VMEM((2, features, half), BF16),
-            pltpu.SemaphoreType.DMA((stripes,)),
-            pltpu.SemaphoreType.DMA,
-            pltpu.SemaphoreType.DMA((2,)),
-        ],
-        compiler_params=pltpu.CompilerParams(vmem_limit_bytes=LIMIT),
-        cost_estimate=SMALL,
-        name="project_first",
-    )(hidden, gain, weight)
-
-
-def head_spread(query, width):
-    heads = query.shape[0]
-    group = heads // (width // LANES)
-    head = lax.broadcasted_iota(jnp.int32, (heads, LANES), 0)
-    pieces = [jnp.where(head // group == g, query, jnp.zeros_like(query)) for g in range(width // LANES)]
-    return jnp.concatenate(pieces, axis=1)
-
-
-def head_pick(products):
-    heads, width = products.shape
-    group = heads // (width // LANES)
-    head = lax.broadcasted_iota(jnp.int32, (heads, LANES), 0)
-    picked = products[:, :LANES]
-    for g in range(1, width // LANES):
-        picked = jnp.where(head // group == g, products[:, g * LANES : (g + 1) * LANES], picked)
-    return picked
-
-
-def score(query, key_rows):
-    spread = head_spread(query, key_rows.shape[1])
-    scores = lax.dot_general(spread, key_rows, (((1,), (1,)), ((), ())), preferred_element_type=F32)
-    return scores * (1.0 / math.sqrt(LANES))
-
-
-def attend(query, key_rows, value_rows, usable):
-    scores = jnp.where(usable, score(query, key_rows), FLOOR_SCORE)
-    largest = jnp.max(scores, axis=1, keepdims=True)
-    weights = jnp.where(usable, jnp.exp(scores - largest), 0.0)
-    total = jnp.sum(weights, axis=1, keepdims=True)
-    picked = head_pick(jnp.dot(weights.astype(BF16), value_rows, preferred_element_type=F32))
-    some = total > 0.0
-    safe = jnp.where(some, total, 1.0)
-    return picked / safe, jnp.where(some, largest + jnp.log(safe), FLOOR_SCORE)
-
-
-def split_lines(lines, first):
-    high = lines.astype(BF16).astype(F32)
-    middle_part = (lines - high).astype(BF16).astype(F32)
-    low = lines - high - middle_part
-    place = lax.broadcasted_iota(jnp.int32, lines.shape, 0) - first
-    return jnp.where(place == 0, high, jnp.where(place == 1, middle_part, jnp.where(place == 2, low, 0.0)))
-
-
-def join_lines(tail, first, rows):
-    line = jnp.sum(tail[first : first + 3].astype(F32), axis=0, keepdims=True)
-    return jnp.broadcast_to(line, (LANES, LANES)).T[:rows]
-
-
-def project_keys_kernel(hidden, gain, weight, after, own, near, third, gained, rows_in, gain_in, tile, *sems):
-    row_sem, gain_sem, tile_sem = sems
-    shard = lax.axis_index("shard")
-    rows = own.shape[0]
-    half = weight.shape[1] // 2
-    inner_block, outer_block = far_blocks(shard)
-    blocks = [shard, jnp.bitwise_xor(shard, 1), jnp.where(is_inner(shard), inner_block, outer_block)]
-    rows_here = row_copies(hidden, blocks, rows_in, row_sem)
     tile_copy = pltpu.make_async_copy(weight.at[:, pl.ds(0, half)], tile, tile_sem)
     gain_copy = pltpu.make_async_copy(gain, gain_in, gain_sem)
     gain_copy.start()
@@ -322,29 +219,130 @@
     for copy in rows_here:
         copy.wait()
     scale_rows(rows_in, gained, gain_in, slice(None))
+    put_squares(rows_in, slice(None), out, slice(half, half + LANES), 0)
+    tile_copy.wait()
+    out[:, :half] = jnp.dot(gained[...], tile[...], preferred_element_type=F32).astype(BF16)
+
+
+def project_first(hidden, gain, weight):
+    stripes, blocks, page_len, features = hidden.shape
+    half = weight.shape[1] // 2
+    rows = stripes * page_len
+    return pl.pallas_call(
+        first_kernel,
+        in_specs=[whole(pl.ANY)] * 3,
+        out_specs=[whole()] * 3,
+        out_shape=[
+            jax.ShapeDtypeStruct((rows, half + LANES), BF16),
+            jax.ShapeDtypeStruct((rows, features), BF16),
+            jax.ShapeDtypeStruct((features, half), BF16),
+        ],
+        scratch_shapes=[
+            pltpu.VMEM((rows, features), BF16),
+            pltpu.VMEM((features,), BF16),
+            pltpu.SemaphoreType.DMA((stripes,)),
+            pltpu.SemaphoreType.DMA,
+            pltpu.SemaphoreType.DMA,
+        ],
+        compiler_params=pltpu.CompilerParams(vmem_limit_bytes=LIMIT),
+        cost_estimate=SMALL,
+        name="project_first",
+    )(hidden, gain, weight)
+
+
+def head_spread(query, width):
+    heads = query.shape[0]
+    group = heads // (width // LANES)
+    head = lax.broadcasted_iota(jnp.int32, (heads, LANES), 0)
+    pieces = [jnp.where(head // group == g, query, jnp.zeros_like(query)) for g in range(width // LANES)]
+    return jnp.concatenate(pieces, axis=1)
+
+
+def head_pick(products):
+    heads, width = products.shape
+    group = heads // (width // LANES)
+    head = lax.broadcasted_iota(jnp.int32, (heads, LANES), 0)
+    picked = products[:, :LANES]
+    for g in range(1, width // LANES):
+        picked = jnp.where(head // group == g, products[:, g * LANES : (g + 1) * LANES], picked)
+    return picked
+
+
+def score(query, key_rows):
+    spread = head_spread(query, key_rows.shape[1])
+    scores = lax.dot_general(spread, key_rows, (((1,), (1,)), ((), ())), preferred_element_type=F32)
+    return scores * (1.0 / math.sqrt(LANES))
+
+
+def attend(query, key_rows, value_rows, usable):
+    scores = jnp.where(usable, score(query, key_rows), FLOOR_SCORE)
+    largest = jnp.max(scores, axis=1, keepdims=True)
+    weights = jnp.where(usable, jnp.exp(scores - largest), 0.0)
+    total = jnp.sum(weights, axis=1, keepdims=True)
+    picked = head_pick(jnp.dot(weights.astype(BF16), value_rows, preferred_element_type=F32))
+    some = total > 0.0
+    safe = jnp.where(some, total, 1.0)
+    return picked / safe, jnp.where(some, largest + jnp.log(safe), FLOOR_SCORE)
+
+
+def split_lines(lines, first):
+    high = lines.astype(BF16).astype(F32)
+    middle_part = (lines - high).astype(BF16).astype(F32)
+    low = lines - high - middle_part
+    place = lax.broadcasted_iota(jnp.int32, lines.shape, 0) - first
+    return jnp.where(place == 0, high, jnp.where(place == 1, middle_part, jnp.where(place == 2, low, 0.0)))
+
+
+def join_lines(tail, first, rows):
+    line = jnp.sum(tail[first : first + 3].astype(F32), axis=0, keepdims=True)
+    return jnp.broadcast_to(line, (LANES, LANES)).T[:rows]
+
+
+def project_keys_kernel(hidden, gain, weight, sent, key_tile, *rest):
+    own, near, third, values, gained, value_tile = rest[:6]
+    rows_in, gain_in, row_sem, gain_sem, tile_sem = rest[6:]
+    shard = lax.axis_index("shard")
+    rows = own.shape[0]
+    half = weight.shape[1] // 2
+    inner_block, outer_block = far_blocks(shard)
+    blocks = [shard, jnp.bitwise_xor(shard, 1), jnp.where(is_inner(shard), inner_block, outer_block)]
+    rows_here = row_copies(hidden, blocks, rows_in, row_sem)
+    tile_copy = pltpu.make_async_copy(weight.at[:, pl.ds(half, half)], value_tile, tile_sem)
+    gain_copy = pltpu.make_async_copy(gain, gain_in, gain_sem)
+    gain_copy.start()
+    for copy in rows_here + [tile_copy]:
+        copy.start()
+    gain_copy.wait()
+    for copy in rows_here:
+        copy.wait()
+    scale_rows(rows_in, gained, gain_in, slice(None))
     for place, ref in enumerate((own, near, third)):
         span = slice(place * rows, (place + 1) * rows)
         put_squares(rows_in, span, ref, slice(half, half + LANES), 2 if place == 2 else 0)
-    tile_copy.wait()
-    product = jnp.dot(gained[...], tile[...], preferred_element_type=F32).astype(BF16)
+    product = jnp.dot(gained[...], key_tile[...], preferred_element_type=F32).astype(BF16)
     for place, ref in enumerate((own, near, third)):
         ref[:, :half] = product[place * rows : (place + 1) * rows]
-
-
-def project_keys(hidden, gain, weight, after):
+    tile_copy.wait()
+    values[...] = jnp.dot(sent[...], value_tile[...], preferred_element_type=F32).astype(BF16)
+
+
+def project_keys(hidden, gain, weight, sent, tile):
     stripes, blocks, page_len, features = hidden.shape
     half = weight.shape[1] // 2
     rows = stripes * page_len
     return pl.pallas_call(
         project_keys_kernel,
-        in_specs=[whole(pl.ANY)] * 4,
-        out_specs=[whole()] * 4,
+        in_specs=[whole(pl.ANY)] * 3 + [whole()] * 2,
+        out_specs=[whole()] * 6,
         out_shape=[jax.ShapeDtypeStruct((rows, half + LANES), BF16)] * 3
-        + [jax.ShapeDtypeStruct((3 * rows, features), BF16)],
+        + [
+            jax.ShapeDtypeStruct((rows, half), BF16),
+            jax.ShapeDtypeStruct((3 * rows, features), BF16),
+            jax.ShapeDtypeStruct((features, half), BF16),
+        ],
         scratch_shapes=[
             pltpu.VMEM((3 * rows, features), BF16),
             pltpu.VMEM((features,), BF16),
-            pltpu.VMEM((features, half), BF16),
             pltpu.SemaphoreType.DMA((3 * stripes,)),
             pltpu.SemaphoreType.DMA,
             pltpu.SemaphoreType.DMA,
@@ -352,44 +350,37 @@
         compiler_params=pltpu.CompilerParams(vmem_limit_bytes=LIMIT),
         cost_estimate=SMALL,
         name="project_keys",
-    )(hidden, gain, weight, after)
-
-
-def project_values_kernel(gained, weight, *rest):
-    own, near, third, tile, sem = rest[-5:]
-    rows, half = own.shape
-    tile_copy = pltpu.make_async_copy(weight.at[:, pl.ds(half, half)], tile, sem)
-    tile_copy.start()
-    tile_copy.wait()
+    )(hidden, gain, weight, sent, tile)
+
+
+def project_values_kernel(gained, tile, *rest):
     product = jnp.dot(gained[...], tile[...], preferred_element_type=F32).astype(BF16)
-    for place, ref in enumerate((own, near, third)):
+    rows = rest[-1].shape[0]
+    for place, ref in enumerate(rest[-3:]):
         ref[...] = product[place * rows : (place + 1) * rows]
 
 
-def project_values(gained, weight, after):
-    half = weight.shape[1] // 2
+def project_values(gained, tile, after):
     return pl.pallas_call(
         project_values_kernel,
-        in_specs=[whole()] + [whole(pl.ANY)] * (1 + len(after)),
+        in_specs=[whole()] * 2 + [whole(pl.ANY)] * len(after),
         out_specs=[whole()] * 3,
-        out_shape=[jax.ShapeDtypeStruct((gained.shape[0] // 3, half), BF16)] * 3,
-        scratch_shapes=[pltpu.VMEM((weight.shape[0], half), BF16), pltpu.SemaphoreType.DMA],
+        out_shape=[jax.ShapeDtypeStruct((gained.shape[0] // 3, tile.shape[1]), BF16)] * 3,
         compiler_params=pltpu.CompilerParams(vmem_limit_bytes=LIMIT),
         cost_estimate=SMALL,
         name="project_values",
-    )(gained, weight, *after)
-
-
-def carry_kernel(mine, first, *rest, start):
-    out = rest[-1]
+    )(gained, tile, *after)
+
+
+def carry_kernel(mine, first, *rest):
     inner = is_inner(lax.axis_index("shard"))
-    arrived = first[:, start : start + mine.shape[1]].astype(F32)
-    out[...] = (mine[...].astype(F32) + jnp.where(inner, arrived, 0.0)).astype(BF16)
-
-
-def carry(mine, first, after, start):
-    return pl.pallas_call(
-        functools.partial(carry_kernel, start=start),
+    arrived = jnp.where(inner, first[...].astype(F32), 0.0)
+    rest[-1][...] = (mine[...].astype(F32) + arrived).astype(BF16)
+
+
+def carry(mine, first, after):
+    return pl.pallas_call(
+        carry_kernel,
         in_specs=[whole(), whole()] + [whole(pl.ANY)] * len(after),
         out_specs=whole(),
         out_shape=jax.ShapeDtypeStruct(mine.shape, BF16),
@@ -403,21 +394,21 @@
     return [jax.ShapeDtypeStruct((rows, width), BF16)] * 4
 
 
-def ask_kernel(jobs, query, after, *outs):
-    for step, out in enumerate(outs):
+def ask_kernel(jobs, query, *rest):
+    for step, out in enumerate(rest[-4:]):
         out[...] = query[job_from(jobs, step)[1]]
 
 
 def ask(jobs, query, after):
     return pl.pallas_call(
         ask_kernel,
-        in_specs=[whole(SMEM), whole(), whole(pl.ANY)],
+        in_specs=[whole(SMEM), whole()] + [whole(pl.ANY)] * len(after),
         out_specs=[whole()] * 4,
         out_shape=rep_shapes(*query.shape[1:]),
         compiler_params=pltpu.CompilerParams(vmem_limit_bytes=LIMIT),
         cost_estimate=SMALL,
         name="ask",
-    )(jobs, query, after)
+    )(jobs, query, *after)
 
 
 def kept_kernel(jobs, table, lengths, query, pool, *rest, shards, after):
@@ -518,8 +509,8 @@
             out[...] = finished[page_len:]
 
 
-def add_parts(own, near, first, third, columns, first_columns):
-    direct = jnp.where(is_inner(lax.axis_index("shard")), 0.0, first[:, first_columns].astype(F32))
+def add_parts(own, near, first, third, columns):
+    direct = jnp.where(is_inner(lax.axis_index("shard")), 0.0, first[:, columns].astype(F32))
     return (own[:, columns].astype(F32) + near[:, columns].astype(F32)) + (third[:, columns].astype(F32) + direct)
 
 
@@ -533,7 +524,7 @@
     width = own.shape[1] - LANES
 
     def added(columns):
-        return add_parts(own, near, first, third, columns, columns)
+        return add_parts(own, near, first, third, columns)
 
     squares = jnp.sum(added(slice(width, width + LANES)), axis=1, keepdims=True)
     inverse = jnp.broadcast_to(lax.rsqrt(squares / D + EPS), (rows, LANES))
@@ -571,8 +562,7 @@
     shard = lax.axis_index("shard")
     for head in range(own.shape[1] // LANES):
         columns = slice(head * LANES, (head + 1) * LANES)
-        start = first.shape[1] - own.shape[1] + head * LANES
-        total = add_parts(own, near, first, third, columns, slice(start, start + LANES))
+        total = add_parts(own, near, first, third, columns)
         finished[:, columns] = (total * scale[...]).astype(BF16)
     route(jobs, finished, outs)
     page_len = own.shape[0] // SENDS
@@ -801,25 +791,29 @@
     def between(arrays):
         return [arrays[0]] + [across(arrays[step], step) for step in range(1, replicas)]
 
-    sent = project_first(blocks, gain, kv_weight)
-    first = along(sent, FIRST)
-    key_0, key_1, key_2, gained = project_keys(blocks, gain, kv_weight, sent)
+    key_sent, gained_sent, key_tile = project_first(blocks, gain, kv_weight)
+    key_first = along(key_sent, FIRST)
+    key_0, key_1, key_2, value_sent, gained, tile = project_keys(
+        blocks, gain, kv_weight, gained_sent, key_tile
+    )
+    value_first = along(value_sent, FIRST)
     key_near = along(key_1, NEAR)
-    asked = between(ask(jobs, query, key_1))
-    key_third = along(carry(key_2, first, asked[1:], 0), THIRD)
-    value_0, value_1, value_2 = project_values(gained, kv_weight, asked[1:])
+    key_2 = carry(key_2, key_first, [])
+    key_third = along(key_2, THIRD)
+    *kept_parts, new_pool = kept(jobs, table, context_lengths, query, kv_pool, [key_2], shards)
+    asked = between(ask(jobs, query, [value_first, kept_parts[0]]))
+    value_0, value_1, value_2 = project_values(gained, tile, asked[1:])
     value_near = along(value_1, NEAR)
-    value_third = along(carry(value_2, first, [key_near, key_third], key_2.shape[1]), THIRD)
+    value_third = along(carry(value_2, value_first, []), THIRD)
     frequency = THETA ** (-(jnp.arange(HD // 2, dtype=F32) * 2.0 / HD))
     frequency = jnp.concatenate([frequency, frequency])[None, :]
     *key_out, scale, weights, share, level = finish_keys(
-        jobs, (key_0, key_near, first, key_third), frequency, asked, stripe
+        jobs, (key_0, key_near, key_first, key_third), frequency, asked, stripe
     )
     key_pages = between(key_out)
-    *kept_parts, new_pool = kept(jobs, table, context_lengths, query, kv_pool, [scale], shards)
     finished = finish_values(
         jobs,
-        (value_0, value_near, first, value_third),
+        (value_0, value_near, value_first, value_third),
         scale,
         weights,
         share,

time: 65.9 us -> 64.3 us (0.976)
  Pallas kernels: 26.2 us -> 22.4 us
  waiting for transfers between devices: 15.9 us -> 19.3 us
  starting transfers between devices: 22.7 us -> 21.5 us
    pallas_call x6, Pallas kernels: 13.7 us -> 10.1 us  [the longest x1 4.16 us: project_keys(): pl.pallas_call(project_keys_kernel, in_specs=[whole(pl.ANY)] * 3 + [whole...]
    ppermute x12, waiting for transfers between devices: 2.09 us -> 4.03 us  [across(): return lax.ppermute(array, 'rep', [(i, i ^ step) for i in range(replicas)])]
    ppermute x8 -> x9, waiting for transfers between devices: 13.8 us -> 15.3 us  [along(): return lax.ppermute(array, 'shard', pairs)]
    ppermute x12, starting transfers between devices: 7.39 us -> 6.44 us  [across(): return lax.ppermute(array, 'rep', [(i, i ^ step) for i in range(replicas)])]
    ppermute x8 -> x9, starting transfers between devices: 15.3 us -> 15.1 us  [along(): return lax.ppermute(array, 'shard', pairs)]
  transfers between devices with their start and end apart: 20 -> 21, of which waited for: 8 -> 10; matrix products, arithmetic and copies ran while one was open for 0% -> 0% of each run, Pallas kernels for 29% -> 26%
where the time goes in v3:
time: 64.3 us; the launch traced here: 64.1 us
  Pallas kernels  22.4 us (35%)
  starting transfers between devices  21.5 us (33%)
  waiting for transfers between devices  19.3 us (30%)
  between operations  0.84 us (1%)
    ppermute x9, waiting for transfers between devices, along(): return lax.ppermute(array, 'shard', pairs)  15.3 us
    ppermute x9, starting transfers between devices, along(): return lax.ppermute(array, 'shard', pairs)  15.1 us
    ppermute x12, starting transfers between devices, across(): return lax.ppermute(array, 'rep', [(i, i ^ step) for i in range(replicas)])  6.44 us
    pallas_call x1, Pallas kernels, kept(): pl.pallas_call(functools.partial(kept_kernel, shards=shards, after=len(af...  6.01 us
    pallas_call x1, Pallas kernels, project_keys(): pl.pallas_call(project_keys_kernel, in_specs=[whole(pl.ANY)] * 3 + [whole...  4.16 us
    ppermute x12, waiting for transfers between devices, across(): return lax.ppermute(array, 'rep', [(i, i ^ step) for i in range(replicas)])  4.03 us
    pallas_call x1, Pallas kernels, project_first(): pl.pallas_call(first_kernel, in_specs=[whole(pl.ANY)] * 3, out_specs=[who...  3.36 us
    pallas_call x1, Pallas kernels, project_values(): pl.pallas_call(project_values_kernel, in_specs=[whole()] * 2 + [whole(pl....  1.78 us
  transfers between devices with their start and end apart: 21, of which 10 were waited for; matrix products, arithmetic and copies ran while one was open for 0% of the time, Pallas kernels for 26%

profile of v3, /device:TPU:0, one launch (start us, length us, event | category | flops | bytes accessed | tf_op | source)
XLA Modules:
  0.0 64.1 jit_solution(5622877848116533007)
XLA Ops:
  0.6 3.4 %project_first.1 = (bf16[128,1152]{1,0:T(8,128)(2,1)S(1)}, bf16[128,2048]{1,0:T(8,128)(2,1)S(1)}, bf16[2048,1024]{1,0:T(8,128)(2,1)S(1)}) custom-call(bf16[2,4,64,2048]{3,2,1,0:T(8,128)(2,1)} %bitcast.22, bf16[2048]{0:T(1024)(128)(2,1)} %gain.3, bf16[2048,2048]{1,0:T(8,128)(2,1)} %weight.3), custom_call_target="tpu_custom_call" | custom-call | flops 1 | bytes 1 | tf_op jit(solution)/shard_map/project_first/pallas_call | solution.py:231
  4.0 3.1 %collective-permute-start = (bf16[128,1152]{1,0:T(8,128)(2,1)S(1)}, bf16[128,1152]{1,0:T(8,128)(2,1)S(1)}, u32[]{:S(2)}, u32[]{:S(2)}) collective-permute-start(bf16[128,1152]{1,0:T(8,128)(2,1)S(1)} %get-tuple-element.51), channel_id=1, source_target_pairs={{0,1},{3,2},{1,3},{2,0},{4,5},{7,6},{5,7},{6,4},{8,9},{11,10},{9,1... | collective-permute-start | bytes 884744 | tf_op jit(solution)/shard_map/ppermute | solution.py:786
  7.1 0.0 copy-start.3
  7.1 0.0 copy-start
  7.1 0.0 copy-start.1
  7.1 0.0 copy-start.2
  7.1 4.2 %project_keys.1 = (bf16[128,1152]{1,0:T(8,128)(2,1)S(1)}, bf16[128,1152]{1,0:T(8,128)(2,1)S(1)}, bf16[128,1152]{1,0:T(8,128)(2,1)S(1)}, bf16[128,1024]{1,0:T(8,1...) custom-call(bf16[2,4,64,2048]{3,2,1,0:T(8,128)(2,1)} %bitcast.23, bf16[2048]{0:T(1024)(128)(2,1)} %gain.3, ...), custom_call_target="tpu_custom_call" | custom-call | flops 1 | bytes 1 | tf_op jit(solution)/shard_map/project_keys/pallas_call | solution.py:333
  11.2 2.6 %collective-permute-start.3 = (bf16[128,1024]{1,0:T(8,128)(2,1)S(1)}, bf16[128,1024]{1,0:T(8,128)(2,1)S(1)}, u32[]{:S(2)}, u32[]{:S(2)}) collective-permute-start(bf16[128,1024]{1,0:T(8,128)(2,1)S(1)} %get-tuple-element.55), channel_id=1, source_target_pairs={{0,1},{3,2},{1,3},{2,0},{4,5},{7,6},{5,7},{6,4},{8,9},{11,10},{9,1... | collective-permute-start | bytes 786440 | tf_op jit(solution)/shard_map/ppermute | solution.py:786
  13.9 0.5 collective-permute-start.1
  14.3 1.4 %collective-permute-done.first = bf16[128,1152]{1,0:T(8,128)(2,1)S(1)} collective-permute-done((bf16[128,1152]{1,0:T(8,128)(2,1)S(1)}, bf16[128,1152]{1,0:T(8,128)(2,1)S(1)}, u32[]{:S(2)}, u32[]{:S(2)}) %collective-permute-start) | collective-permute-done | bytes 294944 | tf_op jit(solution)/shard_map/ppermute | solution.py:786
  15.8 0.1 carry.2.rest_0_
  15.9 4.3 %collective-permute-start.2 = (bf16[128,1152]{1,0:T(8,128)(2,1)S(1)}, bf16[128,1152]{1,0:T(8,128)(2,1)S(1)}, u32[]{:S(2)}, u32[]{:S(2)}) collective-permute-start(bf16[128,1152]{1,0:T(8,128)(2,1)S(1)} %carry.2.rest_0_), channel_id=1, source_target_pairs={{0,3},{3,0},{1,2},{2,1},{4,7},{7,4},{5,6},{6,5},{8,11},{11,8},{9,1... | collective-permute-start | bytes 884744 | tf_op jit(solution)/shard_map/ppermute | solution.py:786
  20.1 0.0 copy-done.3
  20.2 0.0 copy-done
  20.2 0.0 copy-done.1
  20.2 0.0 copy-done.2
  20.2 6.0 %kept.1 = (bf16[144,128]{1,0:T(8,128)(2,1)S(1)}, bf16[144,128]{1,0:T(8,128)(2,1)S(1)}, bf16[144,128]{1,0:T(8,128)(2,1)S(1)}, bf16[144,128]{1,0:T(8,128)(2,1)S(1)}, bf16[16,64,2048]{2,1,0:T(8,128)(2,1)}) custom-call(s32[3,8]{1,0:T(4,128)S(1)} %bitcast.13, s32[2,8]{1,0:T(2,128)S(1)} %bitcast.20, s32[8]{0:T(128)S(1)} %copy-done.2, ...), custom_call_target="tpu_custom_call" | custom-call | flops 1 | bytes 1 | tf_op jit(solution)/shard_map/kept/pallas_call | solution.py:478
  26.2 0.0 collective-permute-done.3.rest_0_.first
  26.2 0.6 ask.1
  26.8 0.1 collective-permute-start.4
  26.9 1.6 %collective-permute-start.5 = (bf16[64,128]{1,0:T(8,128)(2,1)S(1)}, bf16[64,128]{1,0:T(8,128)(2,1)S(1)}, u32[]{:S(2)}, u32[]{:S(2)}) collective-permute-start(bf16[64,128]{1,0:T(8,128)(2,1)S(1)} %get-tuple-element.59), channel_id=1, source_target_pairs={{0,8},{4,12},{8,0},{12,4},{1,9},{5,13},{9,1},{13,5},{2,10},{6,14},... | collective-permute-start | bytes 49160 | tf_op jit(solution)/shard_map/ppermute | solution.py:789
  28.5 0.3 collective-permute-start.6
  28.8 0.0 collective-permute-done.4.rest_1_.rest_0_
  28.8 1.9 %collective-permute-done.5.rest_2_.rest_1_ = bf16[64,128]{1,0:T(8,128)(2,1)S(1)} collective-permute-done((bf16[64,128]{1,0:T(8,128)(2,1)S(1)}, bf16[64,128]{1,0:T(8,128)(2,1)S(1)}, u32[]{:S(2)}, u32[]{:S(2)}) %collective-permute-start.5) | collective-permute-done | bytes 16416 | tf_op jit(solution)/shard_map/ppermute | solution.py:789
  30.7 0.9 %collective-permute-done.6.rest_3_.rest_2_ = bf16[64,128]{1,0:T(8,128)(2,1)S(1)} collective-permute-done((bf16[64,128]{1,0:T(8,128)(2,1)S(1)}, bf16[64,128]{1,0:T(8,128)(2,1)S(1)}, u32[]{:S(2)}, u32[]{:S(2)}) %collective-permute-start.6) | collective-permute-done | bytes 16416 | tf_op jit(solution)/shard_map/ppermute | solution.py:789
  31.6 1.8 %project_values.1 = (bf16[128,1024]{1,0:T(8,128)(2,1)S(1)}, bf16[128,1024]{1,0:T(8,128)(2,1)S(1)}, bf16[128,1024]{1,0:T(8,128)(2,1)S(1)}) custom-call(bf16[384,2048]{1,0:T(8,128)(2,1)S(1)} %get-tuple-element.65.gained, bf16[2048,1024]{1,0:T(8,128)(2,1)S(1)} %get-tuple-element.66.tile, bf16[64,128]{1,0:T(8,128)(2,1)S(1)} %collective-permute-done.4.rest_1_.rest_0_, ...), custom_call_target="tpu_custom_call" | custom-call | flops 1 | bytes 1 | tf_op jit(solution)/shard_map/project_values/pallas_call | solution.py:364
  33.4 0.1 collective-permute-start.10
  33.5 0.1 carry.3
  33.6 0.1 collective-permute-start.11
  33.7 0.1 maximum_bitcast_fusion.frequency
  33.8 0.0 collective-permute-done.1.near
  33.8 0.7 %collective-permute-done.2.third = bf16[128,1152]{1,0:T(8,128)(2,1)S(1)} collective-permute-done((bf16[128,1152]{1,0:T(8,128)(2,1)S(1)}, bf16[128,1152]{1,0:T(8,128)(2,1)S(1)}, u32[]{:S(2)}, u32[]{:S(2)}) %collective-permute-start.2) | collective-permute-done | bytes 294944 | tf_op jit(solution)/shard_map/ppermute | solution.py:786
  34.5 1.5 %finish_keys.1 = (bf16[64,1024]{1,0:T(8,128)(2,1)S(1)}, bf16[64,1024]{1,0:T(8,128)(2,1)S(1)}, bf16[64,1024]{1,0:T(8,128)(2,1)S(1)}, bf16[64,1024]{1,0:T(8,128)(2...) custom-call(s32[3,8]{1,0:T(4,128)S(1)} %bitcast.15, ...), custom_call_target="tpu_custom_call" | custom-call | flops 1 | bytes 1 | tf_op jit(solution)/shard_map/finish_keys/pallas_call | solution.py:592
  36.1 0.1 collective-permute-start.7
  36.1 2.1 %collective-permute-start.8 = (bf16[64,1024]{1,0:T(8,128)(2,1)S(1)}, bf16[64,1024]{1,0:T(8,128)(2,1)S(1)}, u32[]{:S(2)}, u32[]{:S(2)}) collective-permute-start(bf16[64,1024]{1,0:T(8,128)(2,1)S(1)} %get-tuple-element.63), channel_id=1, source_target_pairs={{0,8},{4,12},{8,0},{12,4},{1,9},{5,13},{9,1},{13,5},{2,10},{6,14},... | collective-permute-start | bytes 393224 | tf_op jit(solution)/shard_map/ppermute | solution.py:789
  38.3 0.1 collective-permute-start.9
  38.3 9.5 %collective-permute-done.10.near = bf16[128,1024]{1,0:T(8,128)(2,1)S(1)} collective-permute-done((bf16[128,1024]{1,0:T(8,128)(2,1)S(1)}, bf16[128,1024]{1,0:T(8,128)(2,1)S(1)}, u32[]{:S(2)}, u32[]{:S(2)}) %collective-permute-start.10) | collective-permute-done | bytes 262176 | tf_op jit(solution)/shard_map/ppermute | solution.py:786
  47.8 0.0 collective-permute-done.11.third
  47.8 0.0 collective-permute-done.7.rest_4_.rest_1_
  47.8 0.0 collective-permute-done.8.rest_5_.rest_2_
  47.8 0.0 collective-permute-done.9.rest_6_.rest_3_
  47.8 1.1 %finish_values.1 = (bf16[64,1024]{1,0:T(8,128)(2,1)S(1)}, bf16[64,1024]{1,0:T(8,128)(2,1)S(1)}, bf16[64,1024]{1,0:T(8,128)(2,1)S(1)}, bf16[64,1024]{1,0:T(8,128)...) custom-call(s32[3,8]{1,0:T(4,128)S(1)} %bitcast.16, ...), custom_call_target="tpu_custom_call" | custom-call | flops 1 | bytes 1 | tf_op jit(solution)/shard_map/finish_values/pallas_call | solution.py:615
  48.9 2.0 %collective-permute-start.12 = (bf16[176,128]{1,0:T(8,128)(2,1)S(1)}, bf16[176,128]{1,0:T(8,128)(2,1)S(1)}, u32[]{:S(2)}, u32[]{:S(2)}) collective-permute-start(bf16[176,128]{1,0:T(8,128)(2,1)S(1)} %get-tuple-element.79), channel_id=1, source_target_pairs={{0,1},{1,0},{2,3},{3,2},{4,5},{5,4},{6,7},{7,6},{8,9},{9,8},{10,11... | collective-permute-start | bytes 135176 | tf_op jit(solution)/shard_map/ppermute | solution.py:786
  50.8 0.9 %collective-permute-start.13 = (bf16[176,128]{1,0:T(8,128)(2,1)S(1)}, bf16[176,128]{1,0:T(8,128)(2,1)S(1)}, u32[]{:S(2)}, u32[]{:S(2)}) collective-permute-start(bf16[176,128]{1,0:T(8,128)(2,1)S(1)} %get-tuple-element.80), channel_id=1, source_target_pairs={{0,2},{1,3},{2,0},{3,1},{4,6},{5,7},{6,4},{7,5},{8,10},{9,11},{10,... | collective-permute-start | bytes 135176 | tf_op jit(solution)/shard_map/ppermute | solution.py:786
  51.7 1.6 %collective-permute-start.14 = (bf16[176,128]{1,0:T(8,128)(2,1)S(1)}, bf16[176,128]{1,0:T(8,128)(2,1)S(1)}, u32[]{:S(2)}, u32[]{:S(2)}) collective-permute-start(bf16[176,128]{1,0:T(8,128)(2,1)S(1)} %get-tuple-element.81), channel_id=1, source_target_pairs={{0,3},{1,2},{2,1},{3,0},{4,7},{5,6},{6,5},{7,4},{8,11},{9,10},{10,... | collective-permute-start | bytes 135176 | tf_op jit(solution)/shard_map/ppermute | solution.py:786
  53.3 0.5 collective-permute-start.16
  53.9 0.0 collective-permute-start.17
  53.9 0.0 collective-permute-done.12.refs_1_
  53.9 2.4 %collective-permute-done.13.refs_2_ = bf16[176,128]{1,0:T(8,128)(2,1)S(1)} collective-permute-done((bf16[176,128]{1,0:T(8,128)(2,1)S(1)}, bf16[176,128]{1,0:T(8,128)(2,1)S(1)}, u32[]{:S(2)}, u32[]{:S(2)}) %collective-permute-start.13) | collective-permute-done | bytes 45088 | tf_op jit(solution)/shard_map/ppermute | solution.py:786
  56.3 1.2 %collective-permute-done.14.refs_3_ = bf16[176,128]{1,0:T(8,128)(2,1)S(1)} collective-permute-done((bf16[176,128]{1,0:T(8,128)(2,1)S(1)}, bf16[176,128]{1,0:T(8,128)(2,1)S(1)}, u32[]{:S(2)}, u32[]{:S(2)}) %collective-permute-start.14) | collective-permute-done | bytes 45088 | tf_op jit(solution)/shard_map/ppermute | solution.py:786
  57.5 0.7 %gather_parts.1 = (bf16[16,256]{1,0:T(8,128)(2,1)S(1)}, bf16[16,256]{1,0:T(8,128)(2,1)S(1)}, bf16[16,256]{1,0:T(8,128)(2,1)S(1)}, bf16[16,256]{1,0:T(8,128)(2,1)S(1)}, bf16[64,1024]{1,0:T(8,128)(2,1)S(1)}) custom-call(s32[3,8]{1,0:T(4,128)S(1)} %bitcast.17, bf16[176,128]{1,0:T(8,128)(2,1)S(1)} %get-tuple-element.78.refs_0_, ...), custom_call_target="tpu_custom_call" | custom-call | flops 1 | bytes 1 | tf_op jit(solution)/shard_map/gather_parts/pallas_call | solution.py:702
  58.3 0.1 collective-permute-start.15
  58.3 0.5 collective-permute-start.18
  58.8 0.5 collective-permute-start.19
  59.4 0.3 collective-permute-done.16.rest_6_
  59.7 0.6 collective-permute-start.20
  60.3 0.2 blend_kept.1
  60.5 0.0 collective-permute-done.17.rest_7_
  60.5 0.0 collective-permute-done.15.rest_5_
  60.5 1.4 %place_pages.1 = (bf16[16,64,2048]{2,1,0:T(8,128)(2,1)}, bf16[16,128]{1,0:T(8,128)(2,1)S(1)}) custom-call(s32[3,8]{1,0:T(4,128)S(1)} %bitcast.18, s32[2,8]{1,0:T(2,128)S(1)} %bitcast.21, bf16[16,64,2048]{2,1,0:T(8,128)(2,1)} %get-tuple-element.52.pool, bf16[64,1024]{1,0:T(8,128)(2,1)S(1)} %get-tuple-element.61.rest_0_, ...), custom_call_target="tpu_custom_call", output_to_operand_aliasing={{0}: (2, {})} | custom-call | flops 1 | bytes 1 | tf_op jit(solution)/shard_map/place_pages/pallas_call | solution.py:658
  61.9 0.0 collective-permute-done.18.refs_1_
  61.9 0.6 collective-permute-done.19.refs_2_
  62.5 0.3 collective-permute-done.20.refs_3_
  62.7 1.4 %combine.1 = bf16[8,2048]{1,0:T(8,128)(2,1)} custom-call(s32[3,8]{1,0:T(4,128)S(1)} %bitcast.19, f32[128,128]{1,0:T(8,128)S(1)} %get-tuple-element.88.kept_out, f32[128,128]{1,0:T(8,128)S(1)} %get-tuple-element.89.kept_level, bf16[16,256]{1,0:T(8,128)(2,1)S(1)} %get-tuple-element.87.refs_4_.refs_0_, bf16[16,256]{1,0:T(8,128)(2,1)S(1)} %collective-permute-done.18.refs_1_, ...), custom_call_target="tpu_custom_call" | custom-call | flops 1 | bytes 1 | tf_op jit(solution)/shard_map/combine/pallas_call | solution.py:755
  (2 shorter events, 0.0 us)
Async XLA Ops:
  4.0 11.8 %collective-permute-start = (bf16[128,1152]{1,0:T(8,128)(2,1)S(1)}, bf16[128,1152]{1,0:T(8,128)(2,1)S(1)}, u32[]{:S(2)}, u32[]{:S(2)}) collective-permute-start(bf16[128,1152]{1,0:T(8,128)(2,1)S(1)} %get-tuple-element.51), channel_id=1, source_target_pairs={{0,1},{3,2},{1,3},{2,0},{4,5},{7,6},{5,7},{6,4},{8,9},{11,10},{9,1... | collective-permute-start | bytes 884744 | tf_op jit(solution)/shard_map/ppermute | solution.py:786
  7.1 13.1 %copy-start.3 = (bf16[8,8192]{1,0:T(8,128)(2,1)S(1)}, bf16[8,8192]{1,0:T(8,128)(2,1)}, u32[]{:S(2)}) copy-start(bf16[8,8192]{1,0:T(8,128)(2,1)} %param.14) | copy-start | bytes 393220
  7.1 13.1 %copy-start = (s32[8,3]{0,1:T(4,128)S(1)}, s32[8,3]{0,1:T(4,128)}, u32[]{:S(2)}) copy-start(s32[8,3]{0,1:T(4,128)} %param.11) | copy-start | bytes 292
  7.1 13.1 %copy-start.1 = (s32[8,2,1]{0,2,1:T(1,128)S(1)}, s32[8,2,1]{0,2,1:T(1,128)}, u32[]{:S(2)}) copy-start(s32[8,2,1]{0,2,1:T(1,128)} %param.12) | copy-start | bytes 196
  7.1 13.1 %copy-start.2 = (s32[8]{0:T(128)S(1)}, s32[8]{0:T(128)}, u32[]{:S(2)}) copy-start(s32[8]{0:T(128)} %lengths.1) | copy-start | bytes 100
  11.2 15.0 %collective-permute-start.3 = (bf16[128,1024]{1,0:T(8,128)(2,1)S(1)}, bf16[128,1024]{1,0:T(8,128)(2,1)S(1)}, u32[]{:S(2)}, u32[]{:S(2)}) collective-permute-start(bf16[128,1024]{1,0:T(8,128)(2,1)S(1)} %get-tuple-element.55), channel_id=1, source_target_pairs={{0,1},{3,2},{1,3},{2,0},{4,5},{7,6},{5,7},{6,4},{8,9},{11,10},{9,1... | collective-permute-start | bytes 786440 | tf_op jit(solution)/shard_map/ppermute | solution.py:786
  13.9 19.9 %collective-permute-start.1 = (bf16[128,1152]{1,0:T(8,128)(2,1)S(1)}, bf16[128,1152]{1,0:T(8,128)(2,1)S(1)}, u32[]{:S(2)}, u32[]{:S(2)}) collective-permute-start(bf16[128,1152]{1,0:T(8,128)(2,1)S(1)} %get-tuple-element.54), channel_id=1, source_target_pairs={{0,1},{1,0},{2,3},{3,2},{4,5},{5,4},{6,7},{7,6},{8,9},{9,8},{10,11... | collective-permute-start | bytes 884744 | tf_op jit(solution)/shard_map/ppermute | solution.py:786
  15.9 18.7 %collective-permute-start.2 = (bf16[128,1152]{1,0:T(8,128)(2,1)S(1)}, bf16[128,1152]{1,0:T(8,128)(2,1)S(1)}, u32[]{:S(2)}, u32[]{:S(2)}) collective-permute-start(bf16[128,1152]{1,0:T(8,128)(2,1)S(1)} %carry.2.rest_0_), channel_id=1, source_target_pairs={{0,3},{3,0},{1,2},{2,1},{4,7},{7,4},{5,6},{6,5},{8,11},{11,8},{9,1... | collective-permute-start | bytes 884744 | tf_op jit(solution)/shard_map/ppermute | solution.py:786
  26.8 1.9 %collective-permute-start.4 = (bf16[64,128]{1,0:T(8,128)(2,1)S(1)}, bf16[64,128]{1,0:T(8,128)(2,1)S(1)}, u32[]{:S(2)}, u32[]{:S(2)}) collective-permute-start(bf16[64,128]{1,0:T(8,128)(2,1)S(1)} %get-tuple-element.58), channel_id=1, source_target_pairs={{0,4},{4,0},{8,12},{12,8},{1,5},{5,1},{9,13},{13,9},{2,6},{6,2},{1... | collective-permute-start | bytes 49160 | tf_op jit(solution)/shard_map/ppermute | solution.py:789
  26.9 3.8 %collective-permute-start.5 = (bf16[64,128]{1,0:T(8,128)(2,1)S(1)}, bf16[64,128]{1,0:T(8,128)(2,1)S(1)}, u32[]{:S(2)}, u32[]{:S(2)}) collective-permute-start(bf16[64,128]{1,0:T(8,128)(2,1)S(1)} %get-tuple-element.59), channel_id=1, source_target_pairs={{0,8},{4,12},{8,0},{12,4},{1,9},{5,13},{9,1},{13,5},{2,10},{6,14},... | collective-permute-start | bytes 49160 | tf_op jit(solution)/shard_map/ppermute | solution.py:789
  28.5 3.2 %collective-permute-start.6 = (bf16[64,128]{1,0:T(8,128)(2,1)S(1)}, bf16[64,128]{1,0:T(8,128)(2,1)S(1)}, u32[]{:S(2)}, u32[]{:S(2)}) collective-permute-start(bf16[64,128]{1,0:T(8,128)(2,1)S(1)} %get-tuple-element.60), channel_id=1, source_target_pairs={{0,12},{4,8},{8,4},{12,0},{1,13},{5,9},{9,5},{13,1},{2,14},{6,10},... | collective-permute-start | bytes 49160 | tf_op jit(solution)/shard_map/ppermute | solution.py:789
  33.4 14.4 %collective-permute-start.10 = (bf16[128,1024]{1,0:T(8,128)(2,1)S(1)}, bf16[128,1024]{1,0:T(8,128)(2,1)S(1)}, u32[]{:S(2)}, u32[]{:S(2)}) collective-permute-start(bf16[128,1024]{1,0:T(8,128)(2,1)S(1)} %get-tuple-element.68), channel_id=1, source_target_pairs={{0,1},{1,0},{2,3},{3,2},{4,5},{5,4},{6,7},{7,6},{8,9},{9,8},{10,11... | collective-permute-start | bytes 786440 | tf_op jit(solution)/shard_map/ppermute | solution.py:786
  33.6 14.2 %collective-permute-start.11 = (bf16[128,1024]{1,0:T(8,128)(2,1)S(1)}, bf16[128,1024]{1,0:T(8,128)(2,1)S(1)}, u32[]{:S(2)}, u32[]{:S(2)}) collective-permute-start(bf16[128,1024]{1,0:T(8,128)(2,1)S(1)} %carry.3), channel_id=1, source_target_pairs={{0,3},{3,0},{1,2},{2,1},{4,7},{7,4},{5,6},{6,5},{8,11},{11,8},{9,1... | collective-permute-start | bytes 786440 | tf_op jit(solution)/shard_map/ppermute | solution.py:786
  36.1 11.7 %collective-permute-start.7 = (bf16[64,1024]{1,0:T(8,128)(2,1)S(1)}, bf16[64,1024]{1,0:T(8,128)(2,1)S(1)}, u32[]{:S(2)}, u32[]{:S(2)}) collective-permute-start(bf16[64,1024]{1,0:T(8,128)(2,1)S(1)} %get-tuple-element.62), channel_id=1, source_target_pairs={{0,4},{4,0},{8,12},{12,8},{1,5},{5,1},{9,13},{13,9},{2,6},{6,2},{1... | collective-permute-start | bytes 393224 | tf_op jit(solution)/shard_map/ppermute | solution.py:789
  36.1 11.7 %collective-permute-start.8 = (bf16[64,1024]{1,0:T(8,128)(2,1)S(1)}, bf16[64,1024]{1,0:T(8,128)(2,1)S(1)}, u32[]{:S(2)}, u32[]{:S(2)}) collective-permute-start(bf16[64,1024]{1,0:T(8,128)(2,1)S(1)} %get-tuple-element.63), channel_id=1, source_target_pairs={{0,8},{4,12},{8,0},{12,4},{1,9},{5,13},{9,1},{13,5},{2,10},{6,14},... | collective-permute-start | bytes 393224 | tf_op jit(solution)/shard_map/ppermute | solution.py:789
  38.3 9.5 %collective-permute-start.9 = (bf16[64,1024]{1,0:T(8,128)(2,1)S(1)}, bf16[64,1024]{1,0:T(8,128)(2,1)S(1)}, u32[]{:S(2)}, u32[]{:S(2)}) collective-permute-start(bf16[64,1024]{1,0:T(8,128)(2,1)S(1)} %get-tuple-element.64), channel_id=1, source_target_pairs={{0,12},{4,8},{8,4},{12,0},{1,13},{5,9},{9,5},{13,1},{2,14},{6,10},... | collective-permute-start | bytes 393224 | tf_op jit(solution)/shard_map/ppermute | solution.py:789
  48.9 5.0 %collective-permute-start.12 = (bf16[176,128]{1,0:T(8,128)(2,1)S(1)}, bf16[176,128]{1,0:T(8,128)(2,1)S(1)}, u32[]{:S(2)}, u32[]{:S(2)}) collective-permute-start(bf16[176,128]{1,0:T(8,128)(2,1)S(1)} %get-tuple-element.79), channel_id=1, source_target_pairs={{0,1},{1,0},{2,3},{3,2},{4,5},{5,4},{6,7},{7,6},{8,9},{9,8},{10,11... | collective-permute-start | bytes 135176 | tf_op jit(solution)/shard_map/ppermute | solution.py:786
  50.8 5.5 %collective-permute-start.13 = (bf16[176,128]{1,0:T(8,128)(2,1)S(1)}, bf16[176,128]{1,0:T(8,128)(2,1)S(1)}, u32[]{:S(2)}, u32[]{:S(2)}) collective-permute-start(bf16[176,128]{1,0:T(8,128)(2,1)S(1)} %get-tuple-element.80), channel_id=1, source_target_pairs={{0,2},{1,3},{2,0},{3,1},{4,6},{5,7},{6,4},{7,5},{8,10},{9,11},{10,... | collective-permute-start | bytes 135176 | tf_op jit(solution)/shard_map/ppermute | solution.py:786
  51.7 5.8 %collective-permute-start.14 = (bf16[176,128]{1,0:T(8,128)(2,1)S(1)}, bf16[176,128]{1,0:T(8,128)(2,1)S(1)}, u32[]{:S(2)}, u32[]{:S(2)}) collective-permute-start(bf16[176,128]{1,0:T(8,128)(2,1)S(1)} %get-tuple-element.81), channel_id=1, source_target_pairs={{0,3},{1,2},{2,1},{3,0},{4,7},{5,6},{6,5},{7,4},{8,11},{9,10},{10,... | collective-permute-start | bytes 135176 | tf_op jit(solution)/shard_map/ppermute | solution.py:786
  53.3 6.3 %collective-permute-start.16 = (bf16[64,1024]{1,0:T(8,128)(2,1)S(1)}, bf16[64,1024]{1,0:T(8,128)(2,1)S(1)}, u32[]{:S(2)}, u32[]{:S(2)}) collective-permute-start(bf16[64,1024]{1,0:T(8,128)(2,1)S(1)} %get-tuple-element.84), channel_id=1, source_target_pairs={{0,8},{4,12},{8,0},{12,4},{1,9},{5,13},{9,1},{13,5},{2,10},{6,14},... | collective-permute-start | bytes 393224 | tf_op jit(solution)/shard_map/ppermute | solution.py:789
  53.9 6.6 %collective-permute-start.17 = (bf16[64,1024]{1,0:T(8,128)(2,1)S(1)}, bf16[64,1024]{1,0:T(8,128)(2,1)S(1)}, u32[]{:S(2)}, u32[]{:S(2)}) collective-permute-start(bf16[64,1024]{1,0:T(8,128)(2,1)S(1)} %get-tuple-element.85), channel_id=1, source_target_pairs={{0,12},{4,8},{8,4},{12,0},{1,13},{5,9},{9,5},{13,1},{2,14},{6,10},... | collective-permute-start | bytes 393224 | tf_op jit(solution)/shard_map/ppermute | solution.py:789
  58.3 2.2 %collective-permute-start.15 = (bf16[64,1024]{1,0:T(8,128)(2,1)S(1)}, bf16[64,1024]{1,0:T(8,128)(2,1)S(1)}, u32[]{:S(2)}, u32[]{:S(2)}) collective-permute-start(bf16[64,1024]{1,0:T(8,128)(2,1)S(1)} %get-tuple-element.83), channel_id=1, source_target_pairs={{0,4},{4,0},{8,12},{12,8},{1,5},{5,1},{9,13},{13,9},{2,6},{6,2},{1... | collective-permute-start | bytes 393224 | tf_op jit(solution)/shard_map/ppermute | solution.py:789
  58.3 3.5 %collective-permute-start.18 = (bf16[16,256]{1,0:T(8,128)(2,1)S(1)}, bf16[16,256]{1,0:T(8,128)(2,1)S(1)}, u32[]{:S(2)}, u32[]{:S(2)}) collective-permute-start(bf16[16,256]{1,0:T(8,128)(2,1)S(1)} %get-tuple-element.90), channel_id=1, source_target_pairs={{0,4},{4,0},{8,12},{12,8},{1,5},{5,1},{9,13},{13,9},{2,6},{6,2},{1... | collective-permute-start | bytes 24584 | tf_op jit(solution)/shard_map/ppermute | solution.py:789
  58.8 3.7 %collective-permute-start.19 = (bf16[16,256]{1,0:T(8,128)(2,1)S(1)}, bf16[16,256]{1,0:T(8,128)(2,1)S(1)}, u32[]{:S(2)}, u32[]{:S(2)}) collective-permute-start(bf16[16,256]{1,0:T(8,128)(2,1)S(1)} %get-tuple-element.91), channel_id=1, source_target_pairs={{0,8},{4,12},{8,0},{12,4},{1,9},{5,13},{9,1},{13,5},{2,10},{6,14},... | collective-permute-start | bytes 24584 | tf_op jit(solution)/shard_map/ppermute | solution.py:789
  59.7 3.1 %collective-permute-start.20 = (bf16[16,256]{1,0:T(8,128)(2,1)S(1)}, bf16[16,256]{1,0:T(8,128)(2,1)S(1)}, u32[]{:S(2)}, u32[]{:S(2)}) collective-permute-start(bf16[16,256]{1,0:T(8,128)(2,1)S(1)} %get-tuple-element.92), channel_id=1, source_target_pairs={{0,12},{4,8},{8,4},{12,0},{1,13},{5,9},{9,5},{13,1},{2,14},{6,10},... | collective-permute-start | bytes 24584 | tf_op jit(solution)/shard_map/ppermute | solution.py:789

commit v4 on v3

--- a/solution.py
+++ b/solution.py
@@ -148,6 +148,7 @@
 NEAR = [(0, 1), (1, 0), (2, 3), (3, 2)]
 THIRD = [(0, 3), (3, 0), (1, 2), (2, 1)]
 LANES = 128
+LINES = 8
 GROUP = 2
 BF16 = jnp.bfloat16
 F32 = jnp.float32
@@ -159,13 +160,6 @@
 
 def whole(space=VMEM):
     return pl.BlockSpec(memory_space=space)
-
-
-def split_sum(total, offset):
-    high = total.astype(BF16).astype(F32)
-    low = total - high
-    lane = lax.broadcasted_iota(jnp.int32, (total.shape[0], LANES), 1)
-    return jnp.where(lane == offset, high, jnp.where(lane == offset + 1, low, 0.0)).astype(BF16)
 
 
 def row_copies(hidden, blocks, rows_in, sem):
@@ -186,13 +180,18 @@
     gained[span] = (rows_in[span].astype(F32) * wide_gain).astype(BF16)
 
 
-def put_squares(rows_in, span, out, columns, offset):
-    squares = jnp.zeros((out.shape[0], LANES), F32)
+def put_squares(rows_in, span, out, first):
+    rows = out.shape[0] - LINES
+    squares = jnp.zeros((rows, LANES), F32)
     for lane in range(rows_in.shape[1] // LANES):
         part = rows_in[span, lane * LANES : (lane + 1) * LANES].astype(F32)
         squares = squares + part * part
-    total = jnp.sum(squares, axis=1, keepdims=True)
-    out[:, columns] = split_sum(total, offset)
+    total = jnp.sum(squares.T, axis=0, keepdims=True)
+    high = total.astype(BF16).astype(F32)
+    place = lax.broadcasted_iota(jnp.int32, (LINES, LANES), 0) - first
+    lines = jnp.where(place == 0, high, jnp.where(place == 1, total - high, 0.0))
+    rest = jnp.zeros((LINES, out.shape[1] - LANES), F32)
+    out[rows:] = jnp.concatenate([lines, rest], axis=1).astype(BF16)
 
 
 def is_inner(shard):
@@ -209,19 +208,25 @@
     half = weight.shape[1] // 2
     inner_block, outer_block = far_blocks(shard)
     rows_here = row_copies(hidden, [jnp.where(is_inner(shard), outer_block, inner_block)], rows_in, row_sem)
-    tile_copy = pltpu.make_async_copy(weight.at[:, pl.ds(0, half)], tile, tile_sem)
+    piece = half // 2
+    pieces = [slice(index * piece, (index + 1) * piece) for index in range(2)]
+    tile_copies = [
+        pltpu.make_async_copy(weight.at[:, columns], tile.at[:, columns], tile_sem.at[index])
+        for index, columns in enumerate(pieces)
+    ]
     gain_copy = pltpu.make_async_copy(gain, gain_in, gain_sem)
     gain_copy.start()
-    for copy in rows_here:
+    for copy in rows_here + tile_copies:
         copy.start()
-    tile_copy.start()
     gain_copy.wait()
     for copy in rows_here:
         copy.wait()
     scale_rows(rows_in, gained, gain_in, slice(None))
-    put_squares(rows_in, slice(None), out, slice(half, half + LANES), 0)
-    tile_copy.wait()
-    out[:, :half] = jnp.dot(gained[...], tile[...], preferred_element_type=F32).astype(BF16)
+    put_squares(rows_in, slice(None), out, 0)
+    for copy, columns in zip(tile_copies, pieces):
+        copy.wait()
+        product = jnp.dot(gained[...], tile[:, columns], preferred_element_type=F32)
+        out[: gained.shape[0], columns] = product.astype(BF16)
 
 
 def project_first(hidden, gain, weight):
@@ -233,7 +238,7 @@
         in_specs=[whole(pl.ANY)] * 3,
         out_specs=[whole()] * 3,
         out_shape=[
-            jax.ShapeDtypeStruct((rows, half + LANES), BF16),
+            jax.ShapeDtypeStruct((rows + LINES, half), BF16),
             jax.ShapeDtypeStruct((rows, features), BF16),
             jax.ShapeDtypeStruct((features, half), BF16),
         ],
@@ -242,7 +247,7 @@
             pltpu.VMEM((features,), BF16),
             pltpu.SemaphoreType.DMA((stripes,)),
             pltpu.SemaphoreType.DMA,
-            pltpu.SemaphoreType.DMA,
+            pltpu.SemaphoreType.DMA((2,)),
         ],
         compiler_params=pltpu.CompilerParams(vmem_limit_bytes=LIMIT),
         cost_estimate=SMALL,
@@ -302,7 +307,7 @@
     own, near, third, values, gained, value_tile = rest[:6]
     rows_in, gain_in, row_sem, gain_sem, tile_sem = rest[6:]
     shard = lax.axis_index("shard")
-    rows = own.shape[0]
+    rows = values.shape[0]
     half = weight.shape[1] // 2
     inner_block, outer_block = far_blocks(shard)
     blocks = [shard, jnp.bitwise_xor(shard, 1), jnp.where(is_inner(shard), inner_block, outer_block)]
@@ -318,10 +323,10 @@
     scale_rows(rows_in, gained, gain_in, slice(None))
     for place, ref in enumerate((own, near, third)):
         span = slice(place * rows, (place + 1) * rows)
-        put_squares(rows_in, span, ref, slice(half, half + LANES), 2 if place == 2 else 0)
+        put_squares(rows_in, span, ref, 2 if place == 2 else 0)
     product = jnp.dot(gained[...], key_tile[...], preferred_element_type=F32).astype(BF16)
     for place, ref in enumerate((own, near, third)):
-        ref[:, :half] = product[place * rows : (place + 1) * rows]
+        ref[:rows] = product[place * rows : (place + 1) * rows]
     tile_copy.wait()
     values[...] = jnp.dot(sent[...], value_tile[...], preferred_element_type=F32).astype(BF16)
 
@@ -334,7 +339,7 @@
         project_keys_kernel,
         in_specs=[whole(pl.ANY)] * 3 + [whole()] * 2,
         out_specs=[whole()] * 6,
-        out_shape=[jax.ShapeDtypeStruct((rows, half + LANES), BF16)] * 3
+        out_shape=[jax.ShapeDtypeStruct((rows + LINES, half), BF16)] * 3
         + [
             jax.ShapeDtypeStruct((rows, half), BF16),
             jax.ShapeDtypeStruct((3 * rows, features), BF16),
@@ -509,9 +514,10 @@
             out[...] = finished[page_len:]
 
 
-def add_parts(own, near, first, third, columns):
-    direct = jnp.where(is_inner(lax.axis_index("shard")), 0.0, first[:, columns].astype(F32))
-    return (own[:, columns].astype(F32) + near[:, columns].astype(F32)) + (third[:, columns].astype(F32) + direct)
+def add_parts(own, near, first, third, rows, columns):
+    direct = jnp.where(is_inner(lax.axis_index("shard")), 0.0, first[rows, columns].astype(F32))
+    parts = [ref[rows, columns].astype(F32) for ref in (own, near, third)]
+    return (parts[0] + parts[1]) + (parts[2] + direct)
 
 
 def finish_keys_kernel(jobs, own, near, first, third, frequency, *rest, stripe):
@@ -519,15 +525,15 @@
     scale, weights_out, share, level, finished = rest[8:]
     replica = lax.axis_index("rep")
     shard = lax.axis_index("shard")
-    rows = own.shape[0]
+    rows, width = finished.shape
     page_len = rows // SENDS
-    width = own.shape[1] - LANES
-
-    def added(columns):
-        return add_parts(own, near, first, third, columns)
-
-    squares = jnp.sum(added(slice(width, width + LANES)), axis=1, keepdims=True)
-    inverse = jnp.broadcast_to(lax.rsqrt(squares / D + EPS), (rows, LANES))
+
+    def added(span, columns):
+        return add_parts(own, near, first, third, span, columns)
+
+    squares = jnp.sum(added(slice(rows, rows + LINES), slice(0, LANES)), axis=0, keepdims=True)
+    squares = jnp.broadcast_to(squares, (LANES, LANES)).T[:rows]
+    inverse = lax.rsqrt(squares / D + EPS)
     scale[...] = inverse
     row = lax.broadcasted_iota(jnp.int32, (rows, LANES), 0)
     lane = lax.broadcasted_iota(jnp.int32, (rows, LANES), 1)
@@ -538,7 +544,7 @@
     sine_part = jnp.where(lane < LANES // 2, -jnp.sin(angle), jnp.sin(angle)) * inverse
     for head in range(width // LANES):
         columns = slice(head * LANES, (head + 1) * LANES)
-        value = added(columns)
+        value = added(slice(0, rows), columns)
         turned = value * cosine + pltpu.roll(value, LANES // 2, 1) * sine_part
         finished[:, columns] = turned.astype(BF16)
     route(jobs, finished, outs)
@@ -562,7 +568,7 @@
     shard = lax.axis_index("shard")
     for head in range(own.shape[1] // LANES):
         columns = slice(head * LANES, (head + 1) * LANES)
-        total = add_parts(own, near, first, third, columns)
+        total = add_parts(own, near, first, third, slice(None), columns)
         finished[:, columns] = (total * scale[...]).astype(BF16)
     route(jobs, finished, outs)
     page_len = own.shape[0] // SENDS
@@ -585,8 +591,7 @@
 
 
 def finish_keys(jobs, parts, frequency, asked, stripe):
-    rows = parts[0].shape[0]
-    width = parts[0].shape[1] - LANES
+    rows, width = parts[0].shape[0] - LINES, parts[0].shape[1]
     heads = asked[0].shape[0]
     page_len = rows // SENDS
     return pl.pallas_call(
@@ -800,11 +805,11 @@
     key_near = along(key_1, NEAR)
     key_2 = carry(key_2, key_first, [])
     key_third = along(key_2, THIRD)
-    *kept_parts, new_pool = kept(jobs, table, context_lengths, query, kv_pool, [key_2], shards)
-    asked = between(ask(jobs, query, [value_first, kept_parts[0]]))
-    value_0, value_1, value_2 = project_values(gained, tile, asked[1:])
+    asked = between(ask(jobs, query, [key_2]))
+    value_0, value_1, value_2 = project_values(gained, tile, [asked[0], value_first])
     value_near = along(value_1, NEAR)
-    value_third = along(carry(value_2, value_first, []), THIRD)
+    *kept_parts, new_pool = kept(jobs, table, context_lengths, query, kv_pool, [value_1] + asked[1:], shards)
+    value_third = along(carry(value_2, value_first, [kept_parts[0]]), THIRD)
     frequency = THETA ** (-(jnp.arange(HD // 2, dtype=F32) * 2.0 / HD))
     frequency = jnp.concatenate([frequency, frequency])[None, :]
     *key_out, scale, weights, share, level = finish_keys(
@@ -825,7 +830,7 @@
     value_pages = [finished[0], None, across(finished[2], 2), across(finished[3], 3)]
     packed = finished[4:]
     parts = [packed[0]] + [
-        along(packed[step], [(i, i ^ step) for i in range(shards)]) for step in range(1, shards)
+        along(packed[step], [(i, i ^ step) for i in range(shards)]) for step in range(shards - 1, 0, -1)
     ]
     here = QH // shards
     *gathered, near_page = gather_parts(jobs, parts, finished[1], slots * here, SENDS * here)

time: 64.3 us -> 61.1 us (0.950)
  waiting for transfers between devices: 19.3 us -> 11 us
  starting transfers between devices: 21.5 us -> 26.7 us
    ppermute x9, waiting for transfers between devices: 15.3 us -> 9.63 us  [along(): return lax.ppermute(array, 'shard', pairs)]
    ppermute x9, starting transfers between devices: 15.1 us -> 19.4 us  [along(): return lax.ppermute(array, 'shard', pairs)]
    ppermute x12, waiting for transfers between devices: 4.03 us -> 1.4 us  [across(): return lax.ppermute(array, 'rep', [(i, i ^ step) for i in range(replicas)])]
    ppermute x12, starting transfers between devices: 6.44 us -> 7.35 us  [across(): return lax.ppermute(array, 'rep', [(i, i ^ step) for i in range(replicas)])]
  transfers between devices with their start and end apart: 21 -> 21, of which waited for: 10 -> 8; matrix products, arithmetic and copies ran while one was open for 0% -> 0% of each run, Pallas kernels for 26% -> 27%
where the time goes in v4:
time: 61.1 us; the launch traced here: 60.9 us
  starting transfers between devices  26.7 us (44%)
  Pallas kernels  22.2 us (36%)
  waiting for transfers between devices  11 us (18%)
  between operations  0.82 us (1%)
    ppermute x9, starting transfers between devices, along(): return lax.ppermute(array, 'shard', pairs)  19.4 us
    ppermute x9, waiting for transfers between devices, along(): return lax.ppermute(array, 'shard', pairs)  9.63 us
    ppermute x12, starting transfers between devices, across(): return lax.ppermute(array, 'rep', [(i, i ^ step) for i in range(replicas)])  7.35 us
    pallas_call x1, Pallas kernels, kept(): pl.pallas_call(functools.partial(kept_kernel, shards=shards, after=len(af...  6 us
    pallas_call x1, Pallas kernels, project_keys(): pl.pallas_call(project_keys_kernel, in_specs=[whole(pl.ANY)] * 3 + [whole...  4.13 us
    pallas_call x1, Pallas kernels, project_first(): pl.pallas_call(first_kernel, in_specs=[whole(pl.ANY)] * 3, out_specs=[who...  2.95 us
    pallas_call x1, Pallas kernels, project_values(): pl.pallas_call(project_values_kernel, in_specs=[whole()] * 2 + [whole(pl....  1.78 us
    pallas_call x1, Pallas kernels, combine(): pl.pallas_call(combine_kernel, in_specs=[whole(SMEM)] + [whole()] * 6 + [...  1.56 us
  transfers between devices with their start and end apart: 21, of which 8 were waited for; matrix products, arithmetic and copies ran while one was open for 0% of the time, Pallas kernels for 27%

profile of v4, /device:TPU:0, one launch (start us, length us, event | category | flops | bytes accessed | tf_op | source)
XLA Modules:
  0.0 60.9 jit_solution(7106390722981236817)
XLA Ops:
  0.6 3.0 %project_first.1 = (bf16[136,1024]{1,0:T(8,128)(2,1)S(1)}, bf16[128,2048]{1,0:T(8,128)(2,1)S(1)}, bf16[2048,1024]{1,0:T(8,128)(2,1)S(1)}) custom-call(bf16[2,4,64,2048]{3,2,1,0:T(8,128)(2,1)} %bitcast.22, bf16[2048]{0:T(1024)(128)(2,1)} %gain.3, bf16[2048,2048]{1,0:T(8,128)(2,1)} %weight.3), custom_call_target="tpu_custom_call" | custom-call | flops 1 | bytes 1 | tf_op jit(solution)/shard_map/project_first/pallas_call | solution.py:236
  3.6 3.1 %collective-permute-start = (bf16[136,1024]{1,0:T(8,128)(2,1)S(1)}, bf16[136,1024]{1,0:T(8,128)(2,1)S(1)}, u32[]{:S(2)}, u32[]{:S(2)}) collective-permute-start(bf16[136,1024]{1,0:T(8,128)(2,1)S(1)} %get-tuple-element.53), channel_id=1, source_target_pairs={{0,1},{3,2},{1,3},{2,0},{4,5},{7,6},{5,7},{6,4},{8,9},{11,10},{9,1... | collective-permute-start | bytes 835592 | tf_op jit(solution)/shard_map/ppermute | solution.py:791
  6.6 0.0 copy-start.3
  6.6 0.0 copy-start
  6.6 4.1 %project_keys.1 = (bf16[136,1024]{1,0:T(8,128)(2,1)S(1)}, bf16[136,1024]{1,0:T(8,128)(2,1)S(1)}, bf16[136,1024]{1,0:T(8,128)(2,1)S(1)}, bf16[128,1024]{1,0:T(8,1...) custom-call(bf16[2,4,64,2048]{3,2,1,0:T(8,128)(2,1)} %bitcast.23, bf16[2048]{0:T(1024)(128)(2,1)} %gain.3, ...), custom_call_target="tpu_custom_call" | custom-call | flops 1 | bytes 1 | tf_op jit(solution)/shard_map/project_keys/pallas_call | solution.py:338
  10.8 0.0 copy-start.1
  10.8 0.0 copy-start.2
  10.8 2.7 %collective-permute-start.1 = (bf16[128,1024]{1,0:T(8,128)(2,1)S(1)}, bf16[128,1024]{1,0:T(8,128)(2,1)S(1)}, u32[]{:S(2)}, u32[]{:S(2)}) collective-permute-start(bf16[128,1024]{1,0:T(8,128)(2,1)S(1)} %get-tuple-element.55), channel_id=1, source_target_pairs={{0,1},{3,2},{1,3},{2,0},{4,5},{7,6},{5,7},{6,4},{8,9},{11,10},{9,1... | collective-permute-start | bytes 786440 | tf_op jit(solution)/shard_map/ppermute | solution.py:791
  13.5 0.4 collective-permute-start.5
  13.9 0.7 %collective-permute-done.first = bf16[136,1024]{1,0:T(8,128)(2,1)S(1)} collective-permute-done((bf16[136,1024]{1,0:T(8,128)(2,1)S(1)}, bf16[136,1024]{1,0:T(8,128)(2,1)S(1)}, u32[]{:S(2)}, u32[]{:S(2)}) %collective-permute-start) | collective-permute-done | bytes 278560 | tf_op jit(solution)/shard_map/ppermute | solution.py:791
  14.6 0.1 carry.2.rest_0_
  14.7 4.6 %collective-permute-start.6 = (bf16[136,1024]{1,0:T(8,128)(2,1)S(1)}, bf16[136,1024]{1,0:T(8,128)(2,1)S(1)}, u32[]{:S(2)}, u32[]{:S(2)}) collective-permute-start(bf16[136,1024]{1,0:T(8,128)(2,1)S(1)} %carry.2.rest_0_), channel_id=1, source_target_pairs={{0,3},{3,0},{1,2},{2,1},{4,7},{7,4},{5,6},{6,5},{8,11},{11,8},{9,1... | collective-permute-start | bytes 835592 | tf_op jit(solution)/shard_map/ppermute | solution.py:791
  19.4 0.0 copy-done.3
  19.4 0.0 copy-done
  19.4 0.6 ask.1
  20.0 0.1 collective-permute-start.2
  20.1 1.5 %collective-permute-start.3 = (bf16[64,128]{1,0:T(8,128)(2,1)S(1)}, bf16[64,128]{1,0:T(8,128)(2,1)S(1)}, u32[]{:S(2)}, u32[]{:S(2)}) collective-permute-start(bf16[64,128]{1,0:T(8,128)(2,1)S(1)} %get-tuple-element.58), channel_id=1, source_target_pairs={{0,8},{4,12},{8,0},{12,4},{1,9},{5,13},{9,1},{13,5},{2,10},{6,14},... | collective-permute-start | bytes 49160 | tf_op jit(solution)/shard_map/ppermute | solution.py:794
  21.6 0.0 collective-permute-done.1.rest_1_.first
  21.7 0.3 collective-permute-start.4
  22.0 1.8 %project_values.1 = (bf16[128,1024]{1,0:T(8,128)(2,1)S(1)}, bf16[128,1024]{1,0:T(8,128)(2,1)S(1)}, bf16[128,1024]{1,0:T(8,128)(2,1)S(1)}) custom-call(bf16[384,2048]{1,0:T(8,128)(2,1)S(1)} %get-tuple-element.50.gained, bf16[2048,1024]{1,0:T(8,128)(2,1)S(1)} %get-tuple-element.51.tile, bf16[64,128]{1,0:T(8,128)(2,1)S(1)} %get-tuple-element.54.rest_0_, ...), custom_call_target="tpu_custom_call" | custom-call | flops 1 | bytes 1 | tf_op jit(solution)/shard_map/project_values/pallas_call | solution.py:369
  23.8 0.0 collective-permute-done.2.rest_1_
  23.8 0.8 %collective-permute-start.10 = (bf16[128,1024]{1,0:T(8,128)(2,1)S(1)}, bf16[128,1024]{1,0:T(8,128)(2,1)S(1)}, u32[]{:S(2)}, u32[]{:S(2)}) collective-permute-start(bf16[128,1024]{1,0:T(8,128)(2,1)S(1)} %get-tuple-element.56.rest_0_), channel_id=1, source_target_pairs={{0,1},{1,0},{2,3},{3,2},{4,5},{5,4},{6,7},{7,6},{8,9},{9,8},{10,11... | collective-permute-start | bytes 786440 | tf_op jit(solution)/shard_map/ppermute | solution.py:791
  24.6 0.0 collective-permute-done.3.rest_2_
  24.6 0.2 collective-permute-done.4.rest_3_
  24.8 0.0 copy-done.1
  24.8 0.0 copy-done.2
  24.8 6.0 %kept.1 = (bf16[144,128]{1,0:T(8,128)(2,1)S(1)}, bf16[144,128]{1,0:T(8,128)(2,1)S(1)}, bf16[144,128]{1,0:T(8,128)(2,1)S(1)}, bf16[144,128]{1,0:T(8,128)(2,1)S(1)}, bf16[16,64,2048]{2,1,0:T(8,128)(2,1)}) custom-call(s32[3,8]{1,0:T(4,128)S(1)} %bitcast.14, s32[2,8]{1,0:T(2,128)S(1)} %bitcast.20, s32[8]{0:T(128)S(1)} %copy-done.2, ...), custom_call_target="tpu_custom_call" | custom-call | flops 1 | bytes 1 | tf_op jit(solution)/shard_map/kept/pallas_call | solution.py:483
  30.8 0.1 carry.3
  30.9 3.3 %collective-permute-start.11 = (bf16[128,1024]{1,0:T(8,128)(2,1)S(1)}, bf16[128,1024]{1,0:T(8,128)(2,1)S(1)}, u32[]{:S(2)}, u32[]{:S(2)}) collective-permute-start(bf16[128,1024]{1,0:T(8,128)(2,1)S(1)} %carry.3), channel_id=1, source_target_pairs={{0,3},{3,0},{1,2},{2,1},{4,7},{7,4},{5,6},{6,5},{8,11},{11,8},{9,1... | collective-permute-start | bytes 786440 | tf_op jit(solution)/shard_map/ppermute | solution.py:791
  34.3 0.1 maximum_bitcast_fusion.frequency
  34.4 0.0 collective-permute-done.5.near
  34.4 0.0 collective-permute-done.6.third
  34.4 1.5 %finish_keys.1 = (bf16[64,1024]{1,0:T(8,128)(2,1)S(1)}, bf16[64,1024]{1,0:T(8,128)(2,1)S(1)}, bf16[64,1024]{1,0:T(8,128)(2,1)S(1)}, bf16[64,1024]{1,0:T(8,128)(2...) custom-call(s32[3,8]{1,0:T(4,128)S(1)} %bitcast.15, ...), custom_call_target="tpu_custom_call" | custom-call | flops 1 | bytes 1 | tf_op jit(solution)/shard_map/finish_keys/pallas_call | solution.py:597
  35.9 0.1 collective-permute-start.7
  36.0 1.4 %collective-permute-start.8 = (bf16[64,1024]{1,0:T(8,128)(2,1)S(1)}, bf16[64,1024]{1,0:T(8,128)(2,1)S(1)}, u32[]{:S(2)}, u32[]{:S(2)}) collective-permute-start(bf16[64,1024]{1,0:T(8,128)(2,1)S(1)} %get-tuple-element.65), channel_id=1, source_target_pairs={{0,8},{4,12},{8,0},{12,4},{1,9},{5,13},{9,1},{13,5},{2,10},{6,14},... | collective-permute-start | bytes 393224 | tf_op jit(solution)/shard_map/ppermute | solution.py:794
  37.4 0.5 collective-permute-start.9
  37.9 0.8 %collective-permute-done.10.near = bf16[128,1024]{1,0:T(8,128)(2,1)S(1)} collective-permute-done((bf16[128,1024]{1,0:T(8,128)(2,1)S(1)}, bf16[128,1024]{1,0:T(8,128)(2,1)S(1)}, u32[]{:S(2)}, u32[]{:S(2)}) %collective-permute-start.10) | collective-permute-done | bytes 262176 | tf_op jit(solution)/shard_map/ppermute | solution.py:791
  38.7 5.7 %collective-permute-done.11.third = bf16[128,1024]{1,0:T(8,128)(2,1)S(1)} collective-permute-done((bf16[128,1024]{1,0:T(8,128)(2,1)S(1)}, bf16[128,1024]{1,0:T(8,128)(2,1)S(1)}, u32[]{:S(2)}, u32[]{:S(2)}) %collective-permute-start.11) | collective-permute-done | bytes 262176 | tf_op jit(solution)/shard_map/ppermute | solution.py:791
  44.4 0.0 collective-permute-done.7.rest_4_.rest_1_
  44.4 0.0 collective-permute-done.8.rest_5_.rest_2_
  44.4 0.0 collective-permute-done.9.rest_6_.rest_3_
  44.4 1.1 %finish_values.1 = (bf16[64,1024]{1,0:T(8,128)(2,1)S(1)}, bf16[64,1024]{1,0:T(8,128)(2,1)S(1)}, bf16[64,1024]{1,0:T(8,128)(2,1)S(1)}, bf16[64,1024]{1,0:T(8,128)...) custom-call(s32[3,8]{1,0:T(4,128)S(1)} %bitcast.16, ...), custom_call_target="tpu_custom_call" | custom-call | flops 1 | bytes 1 | tf_op jit(solution)/shard_map/finish_values/pallas_call | solution.py:620
  45.5 2.5 %collective-permute-start.12 = (bf16[176,128]{1,0:T(8,128)(2,1)S(1)}, bf16[176,128]{1,0:T(8,128)(2,1)S(1)}, u32[]{:S(2)}, u32[]{:S(2)}) collective-permute-start(bf16[176,128]{1,0:T(8,128)(2,1)S(1)} %get-tuple-element.79), channel_id=1, source_target_pairs={{0,3},{1,2},{2,1},{3,0},{4,7},{5,6},{6,5},{7,4},{8,11},{9,10},{10,... | collective-permute-start | bytes 135176 | tf_op jit(solution)/shard_map/ppermute | solution.py:791
  47.9 1.3 %collective-permute-start.13 = (bf16[176,128]{1,0:T(8,128)(2,1)S(1)}, bf16[176,128]{1,0:T(8,128)(2,1)S(1)}, u32[]{:S(2)}, u32[]{:S(2)}) collective-permute-start(bf16[176,128]{1,0:T(8,128)(2,1)S(1)} %get-tuple-element.80), channel_id=1, source_target_pairs={{0,2},{1,3},{2,0},{3,1},{4,6},{5,7},{6,4},{7,5},{8,10},{9,11},{10,... | collective-permute-start | bytes 135176 | tf_op jit(solution)/shard_map/ppermute | solution.py:791
  49.3 0.7 %collective-permute-start.14 = (bf16[176,128]{1,0:T(8,128)(2,1)S(1)}, bf16[176,128]{1,0:T(8,128)(2,1)S(1)}, u32[]{:S(2)}, u32[]{:S(2)}) collective-permute-start(bf16[176,128]{1,0:T(8,128)(2,1)S(1)} %get-tuple-element.81), channel_id=1, source_target_pairs={{0,1},{1,0},{2,3},{3,2},{4,5},{5,4},{6,7},{7,6},{8,9},{9,8},{10,11... | collective-permute-start | bytes 135176 | tf_op jit(solution)/shard_map/ppermute | solution.py:791
  49.9 1.5 %collective-permute-start.16 = (bf16[64,1024]{1,0:T(8,128)(2,1)S(1)}, bf16[64,1024]{1,0:T(8,128)(2,1)S(1)}, u32[]{:S(2)}, u32[]{:S(2)}) collective-permute-start(bf16[64,1024]{1,0:T(8,128)(2,1)S(1)} %get-tuple-element.84), channel_id=1, source_target_pairs={{0,8},{4,12},{8,0},{12,4},{1,9},{5,13},{9,1},{13,5},{2,10},{6,14},... | collective-permute-start | bytes 393224 | tf_op jit(solution)/shard_map/ppermute | solution.py:794
  51.4 0.0 collective-permute-start.17
  51.4 0.0 collective-permute-done.12.refs_1_
  51.4 2.0 %collective-permute-done.13.refs_2_ = bf16[176,128]{1,0:T(8,128)(2,1)S(1)} collective-permute-done((bf16[176,128]{1,0:T(8,128)(2,1)S(1)}, bf16[176,128]{1,0:T(8,128)(2,1)S(1)}, u32[]{:S(2)}, u32[]{:S(2)}) %collective-permute-start.13) | collective-permute-done | bytes 45088 | tf_op jit(solution)/shard_map/ppermute | solution.py:791
  53.5 0.3 collective-permute-done.14.refs_3_
  53.8 0.7 %gather_parts.1 = (bf16[16,256]{1,0:T(8,128)(2,1)S(1)}, bf16[16,256]{1,0:T(8,128)(2,1)S(1)}, bf16[16,256]{1,0:T(8,128)(2,1)S(1)}, bf16[16,256]{1,0:T(8,128)(2,1)S(1)}, bf16[64,1024]{1,0:T(8,128)(2,1)S(1)}) custom-call(s32[3,8]{1,0:T(4,128)S(1)} %bitcast.17, bf16[176,128]{1,0:T(8,128)(2,1)S(1)} %get-tuple-element.78.refs_0_, ...), custom_call_target="tpu_custom_call" | custom-call | flops 1 | bytes 1 | tf_op jit(solution)/shard_map/gather_parts/pallas_call | solution.py:707
  54.5 0.1 collective-permute-start.15
  54.6 0.5 collective-permute-start.18
  55.1 1.2 %collective-permute-start.19 = (bf16[16,256]{1,0:T(8,128)(2,1)S(1)}, bf16[16,256]{1,0:T(8,128)(2,1)S(1)}, u32[]{:S(2)}, u32[]{:S(2)}) collective-permute-start(bf16[16,256]{1,0:T(8,128)(2,1)S(1)} %get-tuple-element.91), channel_id=1, source_target_pairs={{0,8},{4,12},{8,0},{12,4},{1,9},{5,13},{9,1},{13,5},{2,10},{6,14},... | collective-permute-start | bytes 24584 | tf_op jit(solution)/shard_map/ppermute | solution.py:794
  56.3 0.0 collective-permute-done.16.rest_6_
  56.3 0.2 collective-permute-start.20
  56.5 0.2 blend_kept.1
  56.7 0.5 collective-permute-done.17.rest_7_
  57.2 0.0 collective-permute-done.15.rest_5_
  57.2 1.5 %place_pages.1 = (bf16[16,64,2048]{2,1,0:T(8,128)(2,1)}, bf16[16,128]{1,0:T(8,128)(2,1)S(1)}) custom-call(s32[3,8]{1,0:T(4,128)S(1)} %bitcast.18, s32[2,8]{1,0:T(2,128)S(1)} %bitcast.21, bf16[16,64,2048]{2,1,0:T(8,128)(2,1)} %get-tuple-element.60.pool, bf16[64,1024]{1,0:T(8,128)(2,1)S(1)} %get-tuple-element.63.rest_0_, ...), custom_call_target="tpu_custom_call", output_to_operand_aliasing={{0}: (2, {})} | custom-call | flops 1 | bytes 1 | tf_op jit(solution)/shard_map/place_pages/pallas_call | solution.py:663
  58.7 0.0 collective-permute-done.18.refs_1_
  58.7 0.0 collective-permute-done.19.refs_2_
  58.7 0.6 %collective-permute-done.20.refs_3_ = bf16[16,256]{1,0:T(8,128)(2,1)S(1)} collective-permute-done((bf16[16,256]{1,0:T(8,128)(2,1)S(1)}, bf16[16,256]{1,0:T(8,128)(2,1)S(1)}, u32[]{:S(2)}, u32[]{:S(2)}) %collective-permute-start.20) | collective-permute-done | bytes 8224 | tf_op jit(solution)/shard_map/ppermute | solution.py:794
  59.4 1.6 %combine.1 = bf16[8,2048]{1,0:T(8,128)(2,1)} custom-call(s32[3,8]{1,0:T(4,128)S(1)} %bitcast.19, f32[128,128]{1,0:T(8,128)S(1)} %get-tuple-element.88.kept_out, f32[128,128]{1,0:T(8,128)S(1)} %get-tuple-element.89.kept_level, bf16[16,256]{1,0:T(8,128)(2,1)S(1)} %get-tuple-element.87.refs_4_.refs_0_, bf16[16,256]{1,0:T(8,128)(2,1)S(1)} %collective-permute-done.18.refs_1_, ...), custom_call_target="tpu_custom_call" | custom-call | flops 1 | bytes 1 | tf_op jit(solution)/shard_map/combine/pallas_call | solution.py:760
  (2 shorter events, 0.0 us)
Async XLA Ops:
  3.6 11.1 %collective-permute-start = (bf16[136,1024]{1,0:T(8,128)(2,1)S(1)}, bf16[136,1024]{1,0:T(8,128)(2,1)S(1)}, u32[]{:S(2)}, u32[]{:S(2)}) collective-permute-start(bf16[136,1024]{1,0:T(8,128)(2,1)S(1)} %get-tuple-element.53), channel_id=1, source_target_pairs={{0,1},{3,2},{1,3},{2,0},{4,5},{7,6},{5,7},{6,4},{8,9},{11,10},{9,1... | collective-permute-start | bytes 835592 | tf_op jit(solution)/shard_map/ppermute | solution.py:791
  6.6 12.7 %copy-start.3 = (bf16[8,8192]{1,0:T(8,128)(2,1)S(1)}, bf16[8,8192]{1,0:T(8,128)(2,1)}, u32[]{:S(2)}) copy-start(bf16[8,8192]{1,0:T(8,128)(2,1)} %param.14) | copy-start | bytes 393220
  6.6 12.8 %copy-start = (s32[8,3]{0,1:T(4,128)S(1)}, s32[8,3]{0,1:T(4,128)}, u32[]{:S(2)}) copy-start(s32[8,3]{0,1:T(4,128)} %param.11) | copy-start | bytes 292
  10.8 14.0 %copy-start.1 = (s32[8,2,1]{0,2,1:T(1,128)S(1)}, s32[8,2,1]{0,2,1:T(1,128)}, u32[]{:S(2)}) copy-start(s32[8,2,1]{0,2,1:T(1,128)} %param.12) | copy-start | bytes 196
  10.8 14.0 %copy-start.2 = (s32[8]{0:T(128)S(1)}, s32[8]{0:T(128)}, u32[]{:S(2)}) copy-start(s32[8]{0:T(128)} %lengths.1) | copy-start | bytes 100
  10.8 10.8 %collective-permute-start.1 = (bf16[128,1024]{1,0:T(8,128)(2,1)S(1)}, bf16[128,1024]{1,0:T(8,128)(2,1)S(1)}, u32[]{:S(2)}, u32[]{:S(2)}) collective-permute-start(bf16[128,1024]{1,0:T(8,128)(2,1)S(1)} %get-tuple-element.55), channel_id=1, source_target_pairs={{0,1},{3,2},{1,3},{2,0},{4,5},{7,6},{5,7},{6,4},{8,9},{11,10},{9,1... | collective-permute-start | bytes 786440 | tf_op jit(solution)/shard_map/ppermute | solution.py:791
  13.5 20.9 %collective-permute-start.5 = (bf16[136,1024]{1,0:T(8,128)(2,1)S(1)}, bf16[136,1024]{1,0:T(8,128)(2,1)S(1)}, u32[]{:S(2)}, u32[]{:S(2)}) collective-permute-start(bf16[136,1024]{1,0:T(8,128)(2,1)S(1)} %get-tuple-element.62), channel_id=1, source_target_pairs={{0,1},{1,0},{2,3},{3,2},{4,5},{5,4},{6,7},{7,6},{8,9},{9,8},{10,11... | collective-permute-start | bytes 835592 | tf_op jit(solution)/shard_map/ppermute | solution.py:791
  14.7 19.6 %collective-permute-start.6 = (bf16[136,1024]{1,0:T(8,128)(2,1)S(1)}, bf16[136,1024]{1,0:T(8,128)(2,1)S(1)}, u32[]{:S(2)}, u32[]{:S(2)}) collective-permute-start(bf16[136,1024]{1,0:T(8,128)(2,1)S(1)} %carry.2.rest_0_), channel_id=1, source_target_pairs={{0,3},{3,0},{1,2},{2,1},{4,7},{7,4},{5,6},{6,5},{8,11},{11,8},{9,1... | collective-permute-start | bytes 835592 | tf_op jit(solution)/shard_map/ppermute | solution.py:791
  20.0 3.7 %collective-permute-start.2 = (bf16[64,128]{1,0:T(8,128)(2,1)S(1)}, bf16[64,128]{1,0:T(8,128)(2,1)S(1)}, u32[]{:S(2)}, u32[]{:S(2)}) collective-permute-start(bf16[64,128]{1,0:T(8,128)(2,1)S(1)} %get-tuple-element.57), channel_id=1, source_target_pairs={{0,4},{4,0},{8,12},{12,8},{1,5},{5,1},{9,13},{13,9},{2,6},{6,2},{1... | collective-permute-start | bytes 49160 | tf_op jit(solution)/shard_map/ppermute | solution.py:794
  20.1 4.5 %collective-permute-start.3 = (bf16[64,128]{1,0:T(8,128)(2,1)S(1)}, bf16[64,128]{1,0:T(8,128)(2,1)S(1)}, u32[]{:S(2)}, u32[]{:S(2)}) collective-permute-start(bf16[64,128]{1,0:T(8,128)(2,1)S(1)} %get-tuple-element.58), channel_id=1, source_target_pairs={{0,8},{4,12},{8,0},{12,4},{1,9},{5,13},{9,1},{13,5},{2,10},{6,14},... | collective-permute-start | bytes 49160 | tf_op jit(solution)/shard_map/ppermute | solution.py:794
  21.7 3.2 %collective-permute-start.4 = (bf16[64,128]{1,0:T(8,128)(2,1)S(1)}, bf16[64,128]{1,0:T(8,128)(2,1)S(1)}, u32[]{:S(2)}, u32[]{:S(2)}) collective-permute-start(bf16[64,128]{1,0:T(8,128)(2,1)S(1)} %get-tuple-element.59), channel_id=1, source_target_pairs={{0,12},{4,8},{8,4},{12,0},{1,13},{5,9},{9,5},{13,1},{2,14},{6,10},... | collective-permute-start | bytes 49160 | tf_op jit(solution)/shard_map/ppermute | solution.py:794
  23.8 14.9 %collective-permute-start.10 = (bf16[128,1024]{1,0:T(8,128)(2,1)S(1)}, bf16[128,1024]{1,0:T(8,128)(2,1)S(1)}, u32[]{:S(2)}, u32[]{:S(2)}) collective-permute-start(bf16[128,1024]{1,0:T(8,128)(2,1)S(1)} %get-tuple-element.56.rest_0_), channel_id=1, source_target_pairs={{0,1},{1,0},{2,3},{3,2},{4,5},{5,4},{6,7},{7,6},{8,9},{9,8},{10,11... | collective-permute-start | bytes 786440 | tf_op jit(solution)/shard_map/ppermute | solution.py:791
  30.9 13.5 %collective-permute-start.11 = (bf16[128,1024]{1,0:T(8,128)(2,1)S(1)}, bf16[128,1024]{1,0:T(8,128)(2,1)S(1)}, u32[]{:S(2)}, u32[]{:S(2)}) collective-permute-start(bf16[128,1024]{1,0:T(8,128)(2,1)S(1)} %carry.3), channel_id=1, source_target_pairs={{0,3},{3,0},{1,2},{2,1},{4,7},{7,4},{5,6},{6,5},{8,11},{11,8},{9,1... | collective-permute-start | bytes 786440 | tf_op jit(solution)/shard_map/ppermute | solution.py:791
  35.9 8.5 %collective-permute-start.7 = (bf16[64,1024]{1,0:T(8,128)(2,1)S(1)}, bf16[64,1024]{1,0:T(8,128)(2,1)S(1)}, u32[]{:S(2)}, u32[]{:S(2)}) collective-permute-start(bf16[64,1024]{1,0:T(8,128)(2,1)S(1)} %get-tuple-element.64), channel_id=1, source_target_pairs={{0,4},{4,0},{8,12},{12,8},{1,5},{5,1},{9,13},{13,9},{2,6},{6,2},{1... | collective-permute-start | bytes 393224 | tf_op jit(solution)/shard_map/ppermute | solution.py:794
  36.0 8.4 %collective-permute-start.8 = (bf16[64,1024]{1,0:T(8,128)(2,1)S(1)}, bf16[64,1024]{1,0:T(8,128)(2,1)S(1)}, u32[]{:S(2)}, u32[]{:S(2)}) collective-permute-start(bf16[64,1024]{1,0:T(8,128)(2,1)S(1)} %get-tuple-element.65), channel_id=1, source_target_pairs={{0,8},{4,12},{8,0},{12,4},{1,9},{5,13},{9,1},{13,5},{2,10},{6,14},... | collective-permute-start | bytes 393224 | tf_op jit(solution)/shard_map/ppermute | solution.py:794
  37.4 7.0 %collective-permute-start.9 = (bf16[64,1024]{1,0:T(8,128)(2,1)S(1)}, bf16[64,1024]{1,0:T(8,128)(2,1)S(1)}, u32[]{:S(2)}, u32[]{:S(2)}) collective-permute-start(bf16[64,1024]{1,0:T(8,128)(2,1)S(1)} %get-tuple-element.66), channel_id=1, source_target_pairs={{0,12},{4,8},{8,4},{12,0},{1,13},{5,9},{9,5},{13,1},{2,14},{6,10},... | collective-permute-start | bytes 393224 | tf_op jit(solution)/shard_map/ppermute | solution.py:794
  45.5 6.0 %collective-permute-start.12 = (bf16[176,128]{1,0:T(8,128)(2,1)S(1)}, bf16[176,128]{1,0:T(8,128)(2,1)S(1)}, u32[]{:S(2)}, u32[]{:S(2)}) collective-permute-start(bf16[176,128]{1,0:T(8,128)(2,1)S(1)} %get-tuple-element.79), channel_id=1, source_target_pairs={{0,3},{1,2},{2,1},{3,0},{4,7},{5,6},{6,5},{7,4},{8,11},{9,10},{10,... | collective-permute-start | bytes 135176 | tf_op jit(solution)/shard_map/ppermute | solution.py:791
  47.9 5.5 %collective-permute-start.13 = (bf16[176,128]{1,0:T(8,128)(2,1)S(1)}, bf16[176,128]{1,0:T(8,128)(2,1)S(1)}, u32[]{:S(2)}, u32[]{:S(2)}) collective-permute-start(bf16[176,128]{1,0:T(8,128)(2,1)S(1)} %get-tuple-element.80), channel_id=1, source_target_pairs={{0,2},{1,3},{2,0},{3,1},{4,6},{5,7},{6,4},{7,5},{8,10},{9,11},{10,... | collective-permute-start | bytes 135176 | tf_op jit(solution)/shard_map/ppermute | solution.py:791
  49.3 4.5 %collective-permute-start.14 = (bf16[176,128]{1,0:T(8,128)(2,1)S(1)}, bf16[176,128]{1,0:T(8,128)(2,1)S(1)}, u32[]{:S(2)}, u32[]{:S(2)}) collective-permute-start(bf16[176,128]{1,0:T(8,128)(2,1)S(1)} %get-tuple-element.81), channel_id=1, source_target_pairs={{0,1},{1,0},{2,3},{3,2},{4,5},{5,4},{6,7},{7,6},{8,9},{9,8},{10,11... | collective-permute-start | bytes 135176 | tf_op jit(solution)/shard_map/ppermute | solution.py:791
  49.9 6.3 %collective-permute-start.16 = (bf16[64,1024]{1,0:T(8,128)(2,1)S(1)}, bf16[64,1024]{1,0:T(8,128)(2,1)S(1)}, u32[]{:S(2)}, u32[]{:S(2)}) collective-permute-start(bf16[64,1024]{1,0:T(8,128)(2,1)S(1)} %get-tuple-element.84), channel_id=1, source_target_pairs={{0,8},{4,12},{8,0},{12,4},{1,9},{5,13},{9,1},{13,5},{2,10},{6,14},... | collective-permute-start | bytes 393224 | tf_op jit(solution)/shard_map/ppermute | solution.py:794
  51.4 5.8 %collective-permute-start.17 = (bf16[64,1024]{1,0:T(8,128)(2,1)S(1)}, bf16[64,1024]{1,0:T(8,128)(2,1)S(1)}, u32[]{:S(2)}, u32[]{:S(2)}) collective-permute-start(bf16[64,1024]{1,0:T(8,128)(2,1)S(1)} %get-tuple-element.85), channel_id=1, source_target_pairs={{0,12},{4,8},{8,4},{12,0},{1,13},{5,9},{9,5},{13,1},{2,14},{6,10},... | collective-permute-start | bytes 393224 | tf_op jit(solution)/shard_map/ppermute | solution.py:794
  54.5 2.7 %collective-permute-start.15 = (bf16[64,1024]{1,0:T(8,128)(2,1)S(1)}, bf16[64,1024]{1,0:T(8,128)(2,1)S(1)}, u32[]{:S(2)}, u32[]{:S(2)}) collective-permute-start(bf16[64,1024]{1,0:T(8,128)(2,1)S(1)} %get-tuple-element.83), channel_id=1, source_target_pairs={{0,4},{4,0},{8,12},{12,8},{1,5},{5,1},{9,13},{13,9},{2,6},{6,2},{1... | collective-permute-start | bytes 393224 | tf_op jit(solution)/shard_map/ppermute | solution.py:794
  54.6 4.2 %collective-permute-start.18 = (bf16[16,256]{1,0:T(8,128)(2,1)S(1)}, bf16[16,256]{1,0:T(8,128)(2,1)S(1)}, u32[]{:S(2)}, u32[]{:S(2)}) collective-permute-start(bf16[16,256]{1,0:T(8,128)(2,1)S(1)} %get-tuple-element.90), channel_id=1, source_target_pairs={{0,4},{4,0},{8,12},{12,8},{1,5},{5,1},{9,13},{13,9},{2,6},{6,2},{1... | collective-permute-start | bytes 24584 | tf_op jit(solution)/shard_map/ppermute | solution.py:794
  55.1 3.7 %collective-permute-start.19 = (bf16[16,256]{1,0:T(8,128)(2,1)S(1)}, bf16[16,256]{1,0:T(8,128)(2,1)S(1)}, u32[]{:S(2)}, u32[]{:S(2)}) collective-permute-start(bf16[16,256]{1,0:T(8,128)(2,1)S(1)} %get-tuple-element.91), channel_id=1, source_target_pairs={{0,8},{4,12},{8,0},{12,4},{1,9},{5,13},{9,1},{13,5},{2,10},{6,14},... | collective-permute-start | bytes 24584 | tf_op jit(solution)/shard_map/ppermute | solution.py:794
  56.3 3.1 %collective-permute-start.20 = (bf16[16,256]{1,0:T(8,128)(2,1)S(1)}, bf16[16,256]{1,0:T(8,128)(2,1)S(1)}, u32[]{:S(2)}, u32[]{:S(2)}) collective-permute-start(bf16[16,256]{1,0:T(8,128)(2,1)S(1)} %get-tuple-element.92), channel_id=1, source_target_pairs={{0,12},{4,8},{8,4},{12,0},{1,13},{5,9},{9,5},{13,1},{2,14},{6,10},... | collective-permute-start | bytes 24584 | tf_op jit(solution)/shard_map/ppermute | solution.py:794

commit v5 on v4

--- a/solution.py
+++ b/solution.py
@@ -400,16 +400,27 @@
 
 
 def ask_kernel(jobs, query, *rest):
-    for step, out in enumerate(rest[-4:]):
-        out[...] = query[job_from(jobs, step)[1]]
+    outs, marks = rest[-5:-1], rest[-1]
+    slots = query.shape[0]
+    replica = lax.axis_index("rep")
+    line = lax.broadcasted_iota(jnp.int32, marks.shape, 0)
+    found = jnp.zeros(marks.shape, jnp.int32)
+    for step, out in enumerate(outs):
+        hit, context, _ = job_from(jobs, step)
+        out[...] = query[context]
+        sent = jobs[0, replica * SENDS] == jnp.bitwise_xor(replica, step)
+        found = found + jnp.where(line == step * slots + context, hit.astype(jnp.int32), 0)
+        found = found + jnp.where(line == 4 * slots + step, sent.astype(jnp.int32), 0)
+    marks[...] = found.astype(F32)
 
 
 def ask(jobs, query, after):
     return pl.pallas_call(
         ask_kernel,
         in_specs=[whole(SMEM), whole()] + [whole(pl.ANY)] * len(after),
-        out_specs=[whole()] * 4,
-        out_shape=rep_shapes(*query.shape[1:]),
+        out_specs=[whole()] * 5,
+        out_shape=rep_shapes(*query.shape[1:])
+        + [jax.ShapeDtypeStruct((4 * query.shape[0] + 8, LANES), F32)],
         compiler_params=pltpu.CompilerParams(vmem_limit_bytes=LIMIT),
         cost_estimate=SMALL,
         name="ask",
@@ -522,7 +533,7 @@
 
 def finish_keys_kernel(jobs, own, near, first, third, frequency, *rest, stripe):
     asked, outs = rest[:4], rest[4:8]
-    scale, weights_out, share, level, finished = rest[8:]
+    scale, weights_out, share, tails, finished, level = rest[8:]
     replica = lax.axis_index("rep")
     shard = lax.axis_index("shard")
     rows, width = finished.shape
@@ -560,37 +571,44 @@
         weights_out[send] = weights.astype(BF16)
         share[send] = jnp.broadcast_to(1.0 / total, share.shape[1:])
         level[send] = jnp.broadcast_to(largest + jnp.log(total), level.shape[1:])
-
-
-def finish_values_kernel(jobs, own, near, first, third, scale, weights, share, level, *rest, shards, after):
+    here = level.shape[1] // tails.shape[0]
+    count = SENDS * here
+    for step in range(tails.shape[0]):
+        start = pl.multiple_of(jnp.bitwise_xor(shard, step) * here, here)
+        mine = level[:, pl.ds(start, here), :].reshape(count, LANES)
+        around = [jnp.zeros((rows_, LANES), F32) for rows_ in (step * count, LANES - (step + 1) * count)]
+        pieces = [piece for piece in (around[0], mine, around[1]) if piece.shape[0]]
+        tails[step] = split_lines(jnp.concatenate(pieces, axis=0).T[:16], 3)
+
+
+def finish_values_kernel(marks, own, near, first, third, scale, weights, share, tails, *rest, shards, after):
     kept_parts, outs = rest[:4], rest[4 + after : 8 + after]
     packed, finished, result = rest[8 + after : 12 + after], rest[12 + after], rest[13 + after]
     shard = lax.axis_index("shard")
+    page_len = own.shape[0] // SENDS
+    sent = [marks[marks.shape[0] - 8 + step : marks.shape[0] - 7 + step] > 0.0 for step in range(4)]
     for head in range(own.shape[1] // LANES):
         columns = slice(head * LANES, (head + 1) * LANES)
-        total = add_parts(own, near, first, third, slice(None), columns)
-        finished[:, columns] = (total * scale[...]).astype(BF16)
-    route(jobs, finished, outs)
-    page_len = own.shape[0] // SENDS
+        total = add_parts(own, near, first, third, slice(None), columns) * scale[...]
+        finished[:, columns] = total.astype(BF16)
+        for step, out in enumerate(outs):
+            out[:, columns] = jnp.where(sent[step], total[:page_len], total[page_len:]).astype(BF16)
     for send in range(SENDS):
         products = jnp.dot(
             weights[send], finished[send * page_len : (send + 1) * page_len], preferred_element_type=F32
         )
         result[send] = head_pick(products) * share[send]
-    here = level.shape[1] // shards
+    here = share.shape[1] // shards
     count = SENDS * here
     rows = kept_parts[0].shape[0] - 16
     for step in range(4):
         start = pl.multiple_of(jnp.bitwise_xor(shard, step) * here, here)
         packed[step][:rows] = kept_parts[step][:rows]
         packed[step][rows : rows + count] = result[:, pl.ds(start, here), :].reshape(count, LANES).astype(BF16)
-        mine = level[:, pl.ds(start, here), :].reshape(count, LANES)
-        lines = jnp.concatenate([mine] + [jnp.zeros((LANES - count, LANES), F32)], axis=0).T[:16]
-        tail = kept_parts[step][rows:].astype(F32) + split_lines(lines, 3)
-        packed[step][rows + count :] = tail.astype(BF16)
-
-
-def finish_keys(jobs, parts, frequency, asked, stripe):
+        packed[step][rows + count :] = (kept_parts[step][rows:].astype(F32) + tails[step]).astype(BF16)
+
+
+def finish_keys(jobs, parts, frequency, asked, stripe, shards):
     rows, width = parts[0].shape[0] - LINES, parts[0].shape[1]
     heads = asked[0].shape[0]
     page_len = rows // SENDS
@@ -603,30 +621,30 @@
             jax.ShapeDtypeStruct((rows, LANES), F32),
             jax.ShapeDtypeStruct((SENDS, heads, page_len), BF16),
             jax.ShapeDtypeStruct((SENDS, heads, LANES), F32),
-            jax.ShapeDtypeStruct((SENDS, heads, LANES), F32),
+            jax.ShapeDtypeStruct((shards, 16, LANES), F32),
         ],
-        scratch_shapes=[pltpu.VMEM((rows, width), BF16)],
+        scratch_shapes=[pltpu.VMEM((rows, width), BF16), pltpu.VMEM((SENDS, heads, LANES), F32)],
         compiler_params=pltpu.CompilerParams(vmem_limit_bytes=LIMIT),
         cost_estimate=SMALL,
         name="finish_keys",
     )(jobs, *parts, frequency, *asked)
 
 
-def finish_values(jobs, parts, scale, weights, share, level, kept_parts, after, shards):
+def finish_values(marks, parts, scale, weights, share, tails, kept_parts, after, shards):
     rows, width = parts[0].shape
-    heads = level.shape[1]
+    heads = share.shape[1]
     page_len = rows // SENDS
     packed = kept_parts[0].shape[0] + SENDS * heads // shards
     return pl.pallas_call(
         functools.partial(finish_values_kernel, shards=shards, after=len(after)),
-        in_specs=[whole(SMEM)] + [whole()] * 12 + [whole(pl.ANY)] * len(after),
+        in_specs=[whole()] * 13 + [whole(pl.ANY)] * len(after),
         out_specs=[whole()] * 8,
         out_shape=rep_shapes(page_len, width) + [jax.ShapeDtypeStruct((packed, LANES), BF16)] * 4,
         scratch_shapes=[pltpu.VMEM((rows, width), BF16), pltpu.VMEM((SENDS, heads, LANES), F32)],
         compiler_params=pltpu.CompilerParams(vmem_limit_bytes=LIMIT),
         cost_estimate=SMALL,
         name="finish_values",
-    )(jobs, *parts, scale, weights, share, level, *kept_parts, *after)
+    )(marks, *parts, scale, weights, share, tails, *kept_parts, *after)
 
 
 def job_from(jobs, step):
@@ -681,18 +699,19 @@
     return total / both, top + jnp.log(both)
 
 
-def gather_kernel(jobs, *refs, rows, count):
+def gather_kernel(marks, *refs, rows, count):
     parts, page, outs, page_out = refs[:4], refs[4], refs[5:9], refs[9]
     page_out[...] = page[...]
+    tail = functools.reduce(jnp.add, [ref[rows + count :].astype(F32) for ref in parts])
+    levels = join_lines(tail, 3, LANES)
     mixed, level = blend(
         [ref[rows : rows + count].astype(F32) for ref in parts],
-        [join_lines(ref[rows + count :], 3, count) for ref in parts],
+        [levels[step * count : (step + 1) * count] for step in (0, 3, 2, 1)],
     )
     here = count // SENDS
-    replica = lax.axis_index("rep")
     lane = lax.broadcasted_iota(jnp.int32, (here, LANES), 1)
     for step, out in enumerate(outs):
-        chosen = jobs[0, replica * SENDS] == jnp.bitwise_xor(replica, step)
+        chosen = marks[marks.shape[0] - 8 + step : marks.shape[0] - 7 + step] > 0.0
         total = jnp.where(chosen, level[:here], level[here:])
         high = total.astype(BF16).astype(F32)
         middle_part = (total - high).astype(BF16).astype(F32)
@@ -703,16 +722,16 @@
         ).astype(BF16)
 
 
-def gather_parts(jobs, parts, page, rows, count):
+def gather_parts(marks, parts, page, rows, count):
     return pl.pallas_call(
         functools.partial(gather_kernel, rows=rows, count=count),
-        in_specs=[whole(SMEM)] + [whole()] * 5,
+        in_specs=[whole()] * 6,
         out_specs=[whole()] * 5,
         out_shape=rep_shapes(count // SENDS, 2 * LANES) + [jax.ShapeDtypeStruct(page.shape, BF16)],
         compiler_params=pltpu.CompilerParams(vmem_limit_bytes=LIMIT),
         cost_estimate=SMALL,
         name="gather_parts",
-    )(jobs, *parts, page)
+    )(marks, *parts, page)
 
 
 def blend_kernel(*refs, rows, count):
@@ -736,37 +755,45 @@
     )(*parts, after)
 
 
-def combine_kernel(jobs, kept_out, kept_level, *refs):
+FRESH_ORDER = (0, 2, 3, 1)
+
+
+def combine_kernel(marks, kept_out, kept_level, *refs):
     parts, out, mixed = refs[:4], refs[5], refs[6]
     slots, here, size = mixed.shape
-    mixed[...] = kept_out[...].reshape(mixed.shape)
-    for step, ref in enumerate(parts):
-        hit, context, _ = job_from(jobs, step)
-
-        @pl.when(hit)
-        def _():
-            fresh_level = jnp.sum(ref[:, LANES:].astype(F32), axis=1, keepdims=True)
-            fresh_level = jnp.broadcast_to(fresh_level, (here, LANES))
-            old_level = kept_level[pl.ds(pl.multiple_of(context * here, here), here)]
-            blended, _ = blend([mixed[context], ref[:, :LANES].astype(F32)], [old_level, fresh_level])
-            mixed[context] = blended
-
+    spans = [slice(context * here, (context + 1) * here) for context in range(slots)]
+    blended = []
+    for step, ref in zip(FRESH_ORDER, parts):
+        hits = [marks[step * slots + context : step * slots + context + 1] > 0.0 for context in range(slots)]
+        old, old_level = jnp.zeros((here, size), F32), jnp.zeros((here, size), F32)
+        for hit, span in zip(hits, spans):
+            old = jnp.where(hit, kept_out[span], old)
+            old_level = jnp.where(hit, kept_level[span], old_level)
+        fresh_level = jnp.sum(ref[:, LANES:].astype(F32), axis=1, keepdims=True)
+        fresh_level = jnp.broadcast_to(fresh_level, (here, size))
+        result, _ = blend([old, ref[:, :LANES].astype(F32)], [old_level, fresh_level])
+        blended.append((hits, result))
+    for context, span in enumerate(spans):
+        total = kept_out[span]
+        for hits, result in blended:
+            total = jnp.where(hits[context], result, total)
+        mixed[context] = total
     for head in range(here):
         out[:, head * size : (head + 1) * size] = mixed[:, head, :].astype(BF16)
 
 
-def combine(jobs, kept_out, kept_level, parts, after, slots):
+def combine(marks, kept_out, kept_level, parts, after, slots):
     here = kept_out.shape[0] // slots
     return pl.pallas_call(
         combine_kernel,
-        in_specs=[whole(SMEM)] + [whole()] * 6 + [whole(pl.ANY)],
+        in_specs=[whole()] * 7 + [whole(pl.ANY)],
         out_specs=whole(),
         out_shape=jax.ShapeDtypeStruct((slots, here * LANES), BF16),
         scratch_shapes=[pltpu.VMEM((slots, here, LANES), F32)],
         compiler_params=pltpu.CompilerParams(vmem_limit_bytes=LIMIT),
         cost_estimate=SMALL,
         name="combine",
-    )(jobs, kept_out, kept_level, *parts, after)
+    )(marks, kept_out, kept_level, *parts, after)
 
 
 def on_device(
@@ -805,24 +832,25 @@
     key_near = along(key_1, NEAR)
     key_2 = carry(key_2, key_first, [])
     key_third = along(key_2, THIRD)
-    asked = between(ask(jobs, query, [key_2]))
+    *asked, marks = ask(jobs, query, [key_2])
+    asked = between(asked)
     value_0, value_1, value_2 = project_values(gained, tile, [asked[0], value_first])
     value_near = along(value_1, NEAR)
     *kept_parts, new_pool = kept(jobs, table, context_lengths, query, kv_pool, [value_1] + asked[1:], shards)
     value_third = along(carry(value_2, value_first, [kept_parts[0]]), THIRD)
     frequency = THETA ** (-(jnp.arange(HD // 2, dtype=F32) * 2.0 / HD))
     frequency = jnp.concatenate([frequency, frequency])[None, :]
-    *key_out, scale, weights, share, level = finish_keys(
-        jobs, (key_0, key_near, key_first, key_third), frequency, asked, stripe
+    *key_out, scale, weights, share, tails = finish_keys(
+        jobs, (key_0, key_near, key_first, key_third), frequency, asked, stripe, shards
     )
     key_pages = between(key_out)
     finished = finish_values(
-        jobs,
+        marks,
         (value_0, value_near, value_first, value_third),
         scale,
         weights,
         share,
-        level,
+        tails,
         kept_parts,
         key_pages[1:],
         shards,
@@ -833,12 +861,12 @@
         along(packed[step], [(i, i ^ step) for i in range(shards)]) for step in range(shards - 1, 0, -1)
     ]
     here = QH // shards
-    *gathered, near_page = gather_parts(jobs, parts, finished[1], slots * here, SENDS * here)
-    fresh = between(gathered)
+    *gathered, near_page = gather_parts(marks, parts, finished[1], slots * here, SENDS * here)
+    fresh = [gathered[0]] + [across(gathered[step], step) for step in FRESH_ORDER[1:]]
     value_pages[1] = across(near_page, 1)
     kept_out, kept_level = blend_kept(parts, gathered[0], slots * here, SENDS * here)
     new_pool, placed = place_pages(jobs, table, new_pool, key_pages, value_pages)
-    return (new_pool, combine(jobs, kept_out, kept_level, fresh, placed, slots))
+    return (new_pool, combine(marks, kept_out, kept_level, fresh, placed, slots))
 
 
 def solution(mesh):

time: 61.1 us -> 59 us (0.966)
  Pallas kernels: 22.2 us -> 20.4 us
    pallas_call x1, Pallas kernels: 1.56 us -> 0.8 us  [combine(): pl.pallas_call(combine_kernel, in_specs=[whole()] * 7 + [whole(pl.ANY)],...]
  transfers between devices with their start and end apart: 21 -> 21, of which waited for: 8 -> 7; matrix products, arithmetic and copies ran while one was open for 0% -> 0% of each run, Pallas kernels for 27% -> 27%
where the time goes in v5:
time: 59 us; the launch traced here: 58.9 us
  starting transfers between devices  27 us (46%)
  Pallas kernels  20.4 us (35%)
  waiting for transfers between devices  10.6 us (18%)
  between operations  0.82 us (1%)
    ppermute x9, starting transfers between devices, along(): return lax.ppermute(array, 'shard', pairs)  19.4 us
    ppermute x9, waiting for transfers between devices, along(): return lax.ppermute(array, 'shard', pairs)  9.52 us
    ppermute x12, starting transfers between devices, across(): return lax.ppermute(array, 'rep', [(i, i ^ step) for i in range(replicas)])  7.63 us
    pallas_call x1, Pallas kernels, kept(): pl.pallas_call(functools.partial(kept_kernel, shards=shards, after=len(af...  6 us
    pallas_call x1, Pallas kernels, project_keys(): pl.pallas_call(project_keys_kernel, in_specs=[whole(pl.ANY)] * 3 + [whole...  4.14 us
    pallas_call x1, Pallas kernels, project_first(): pl.pallas_call(first_kernel, in_specs=[whole(pl.ANY)] * 3, out_specs=[who...  2.95 us
    pallas_call x1, Pallas kernels, project_values(): pl.pallas_call(project_values_kernel, in_specs=[whole()] * 2 + [whole(pl....  1.78 us
    pallas_call x1, Pallas kernels, finish_keys(): pl.pallas_call(functools.partial(finish_keys_kernel, stripe=stripe), in_s...  1.63 us
  transfers between devices with their start and end apart: 21, of which 7 were waited for; matrix products, arithmetic and copies ran while one was open for 0% of the time, Pallas kernels for 27%

profile of v5, /device:TPU:0, one launch (start us, length us, event | category | flops | bytes accessed | tf_op | source)
XLA Modules:
  0.0 58.9 jit_solution(3662392736419493754)
XLA Ops:
  0.6 3.0 %project_first.1 = (bf16[136,1024]{1,0:T(8,128)(2,1)S(1)}, bf16[128,2048]{1,0:T(8,128)(2,1)S(1)}, bf16[2048,1024]{1,0:T(8,128)(2,1)S(1)}) custom-call(bf16[2,4,64,2048]{3,2,1,0:T(8,128)(2,1)} %bitcast.19, bf16[2048]{0:T(1024)(128)(2,1)} %gain.3, bf16[2048,2048]{1,0:T(8,128)(2,1)} %weight.3), custom_call_target="tpu_custom_call" | custom-call | flops 1 | bytes 1 | tf_op jit(solution)/shard_map/project_first/pallas_call | solution.py:236
  3.6 3.1 %collective-permute-start = (bf16[136,1024]{1,0:T(8,128)(2,1)S(1)}, bf16[136,1024]{1,0:T(8,128)(2,1)S(1)}, u32[]{:S(2)}, u32[]{:S(2)}) collective-permute-start(bf16[136,1024]{1,0:T(8,128)(2,1)S(1)} %get-tuple-element.54), channel_id=1, source_target_pairs={{0,1},{3,2},{1,3},{2,0},{4,5},{7,6},{5,7},{6,4},{8,9},{11,10},{9,1... | collective-permute-start | bytes 835592 | tf_op jit(solution)/shard_map/ppermute | solution.py:818
  6.6 0.0 copy-start.3
  6.6 0.0 copy-start
  6.6 4.1 %project_keys.1 = (bf16[136,1024]{1,0:T(8,128)(2,1)S(1)}, bf16[136,1024]{1,0:T(8,128)(2,1)S(1)}, bf16[136,1024]{1,0:T(8,128)(2,1)S(1)}, bf16[128,1024]{1,0:T(8,1...) custom-call(bf16[2,4,64,2048]{3,2,1,0:T(8,128)(2,1)} %bitcast.20, bf16[2048]{0:T(1024)(128)(2,1)} %gain.3, ...), custom_call_target="tpu_custom_call" | custom-call | flops 1 | bytes 1 | tf_op jit(solution)/shard_map/project_keys/pallas_call | solution.py:338
  10.8 0.0 copy-start.1
  10.8 0.0 copy-start.2
  10.8 2.6 %collective-permute-start.1 = (bf16[128,1024]{1,0:T(8,128)(2,1)S(1)}, bf16[128,1024]{1,0:T(8,128)(2,1)S(1)}, u32[]{:S(2)}, u32[]{:S(2)}) collective-permute-start(bf16[128,1024]{1,0:T(8,128)(2,1)S(1)} %get-tuple-element.56), channel_id=1, source_target_pairs={{0,1},{3,2},{1,3},{2,0},{4,5},{7,6},{5,7},{6,4},{8,9},{11,10},{9,1... | collective-permute-start | bytes 786440 | tf_op jit(solution)/shard_map/ppermute | solution.py:818
  13.5 0.4 collective-permute-start.5
  13.9 0.7 %collective-permute-done.first = bf16[136,1024]{1,0:T(8,128)(2,1)S(1)} collective-permute-done((bf16[136,1024]{1,0:T(8,128)(2,1)S(1)}, bf16[136,1024]{1,0:T(8,128)(2,1)S(1)}, u32[]{:S(2)}, u32[]{:S(2)}) %collective-permute-start) | collective-permute-done | bytes 278560 | tf_op jit(solution)/shard_map/ppermute | solution.py:818
  14.6 0.1 carry.2.rest_0_
  14.7 4.6 %collective-permute-start.6 = (bf16[136,1024]{1,0:T(8,128)(2,1)S(1)}, bf16[136,1024]{1,0:T(8,128)(2,1)S(1)}, u32[]{:S(2)}, u32[]{:S(2)}) collective-permute-start(bf16[136,1024]{1,0:T(8,128)(2,1)S(1)} %carry.2.rest_0_), channel_id=1, source_target_pairs={{0,3},{3,0},{1,2},{2,1},{4,7},{7,4},{5,6},{6,5},{8,11},{11,8},{9,1... | collective-permute-start | bytes 835592 | tf_op jit(solution)/shard_map/ppermute | solution.py:818
  19.4 0.0 copy-done.3
  19.4 0.0 copy-done
  19.4 0.6 %ask.1 = (bf16[64,128]{1,0:T(8,128)(2,1)S(1)}, bf16[64,128]{1,0:T(8,128)(2,1)S(1)}, bf16[64,128]{1,0:T(8,128)(2,1)S(1)}, bf16[64,128]{1,0:T(8,128)(2,1)S(1)}, f32[40,128]{1,0:T(8,128)S(1)}) custom-call(s32[3,8]{1,0:T(4,128)S(1)} %bitcast.13, bf16[8,64,128]{2,1,0:T(8,128)(2,1)S(1)} %bitcast.11, bf16[136,1024]{1,0:T(8,128)(2,1)S(1)} %carry.2.rest_0_), custom_call_target="tpu_custom_call" | custom-call | flops 1 | bytes 1 | tf_op jit(solution)/shard_map/ask/pallas_call | solution.py:418
  20.0 0.1 collective-permute-start.2
  20.1 1.5 %collective-permute-start.3 = (bf16[64,128]{1,0:T(8,128)(2,1)S(1)}, bf16[64,128]{1,0:T(8,128)(2,1)S(1)}, u32[]{:S(2)}, u32[]{:S(2)}) collective-permute-start(bf16[64,128]{1,0:T(8,128)(2,1)S(1)} %get-tuple-element.59), channel_id=1, source_target_pairs={{0,8},{4,12},{8,0},{12,4},{1,9},{5,13},{9,1},{13,5},{2,10},{6,14},... | collective-permute-start | bytes 49160 | tf_op jit(solution)/shard_map/ppermute | solution.py:821
  21.7 0.0 collective-permute-done.1.rest_1_.first
  21.7 0.3 collective-permute-start.4
  22.0 1.8 %project_values.1 = (bf16[128,1024]{1,0:T(8,128)(2,1)S(1)}, bf16[128,1024]{1,0:T(8,128)(2,1)S(1)}, bf16[128,1024]{1,0:T(8,128)(2,1)S(1)}) custom-call(bf16[384,2048]{1,0:T(8,128)(2,1)S(1)} %get-tuple-element.51.gained, bf16[2048,1024]{1,0:T(8,128)(2,1)S(1)} %get-tuple-element.52.tile, bf16[64,128]{1,0:T(8,128)(2,1)S(1)} %get-tuple-element.55.rest_0_, ...), custom_call_target="tpu_custom_call" | custom-call | flops 1 | bytes 1 | tf_op jit(solution)/shard_map/project_values/pallas_call | solution.py:369
  23.8 0.0 collective-permute-done.2.rest_1_
  23.8 0.8 %collective-permute-start.10 = (bf16[128,1024]{1,0:T(8,128)(2,1)S(1)}, bf16[128,1024]{1,0:T(8,128)(2,1)S(1)}, u32[]{:S(2)}, u32[]{:S(2)}) collective-permute-start(bf16[128,1024]{1,0:T(8,128)(2,1)S(1)} %get-tuple-element.57.rest_0_), channel_id=1, source_target_pairs={{0,1},{1,0},{2,3},{3,2},{4,5},{5,4},{6,7},{7,6},{8,9},{9,8},{10,11... | collective-permute-start | bytes 786440 | tf_op jit(solution)/shard_map/ppermute | solution.py:818
  24.6 0.0 collective-permute-done.3.rest_2_
  24.6 0.3 collective-permute-done.4.rest_3_
  24.8 0.0 copy-done.1
  24.8 0.0 copy-done.2
  24.8 6.0 %kept.1 = (bf16[144,128]{1,0:T(8,128)(2,1)S(1)}, bf16[144,128]{1,0:T(8,128)(2,1)S(1)}, bf16[144,128]{1,0:T(8,128)(2,1)S(1)}, bf16[144,128]{1,0:T(8,128)(2,1)S(1)}, bf16[16,64,2048]{2,1,0:T(8,128)(2,1)}) custom-call(s32[3,8]{1,0:T(4,128)S(1)} %bitcast.14, s32[2,8]{1,0:T(2,128)S(1)} %bitcast.17, s32[8]{0:T(128)S(1)} %copy-done.2, ...), custom_call_target="tpu_custom_call" | custom-call | flops 1 | bytes 1 | tf_op jit(solution)/shard_map/kept/pallas_call | solution.py:494
  30.8 0.1 carry.3
  30.9 3.3 %collective-permute-start.11 = (bf16[128,1024]{1,0:T(8,128)(2,1)S(1)}, bf16[128,1024]{1,0:T(8,128)(2,1)S(1)}, u32[]{:S(2)}, u32[]{:S(2)}) collective-permute-start(bf16[128,1024]{1,0:T(8,128)(2,1)S(1)} %carry.3), channel_id=1, source_target_pairs={{0,3},{3,0},{1,2},{2,1},{4,7},{7,4},{5,6},{6,5},{8,11},{11,8},{9,1... | collective-permute-start | bytes 786440 | tf_op jit(solution)/shard_map/ppermute | solution.py:818
  34.3 0.1 maximum_bitcast_fusion.frequency
  34.4 0.0 collective-permute-done.5.near
  34.4 0.0 collective-permute-done.6.third
  34.4 1.6 %finish_keys.1 = (bf16[64,1024]{1,0:T(8,128)(2,1)S(1)}, bf16[64,1024]{1,0:T(8,128)(2,1)S(1)}, bf16[64,1024]{1,0:T(8,128)(2,1)S(1)}, bf16[64,1024]{1,0:T(8,128)(2...) custom-call(s32[3,8]{1,0:T(4,128)S(1)} %bitcast.15, ...), custom_call_target="tpu_custom_call" | custom-call | flops 1 | bytes 1 | tf_op jit(solution)/shard_map/finish_keys/pallas_call | solution.py:615
  36.0 0.1 collective-permute-start.7
  36.1 1.4 %collective-permute-start.8 = (bf16[64,1024]{1,0:T(8,128)(2,1)S(1)}, bf16[64,1024]{1,0:T(8,128)(2,1)S(1)}, u32[]{:S(2)}, u32[]{:S(2)}) collective-permute-start(bf16[64,1024]{1,0:T(8,128)(2,1)S(1)} %get-tuple-element.66), channel_id=1, source_target_pairs={{0,8},{4,12},{8,0},{12,4},{1,9},{5,13},{9,1},{13,5},{2,10},{6,14},... | collective-permute-start | bytes 393224 | tf_op jit(solution)/shard_map/ppermute | solution.py:821
  37.5 0.5 collective-permute-start.9
  37.9 0.8 %collective-permute-done.10.near = bf16[128,1024]{1,0:T(8,128)(2,1)S(1)} collective-permute-done((bf16[128,1024]{1,0:T(8,128)(2,1)S(1)}, bf16[128,1024]{1,0:T(8,128)(2,1)S(1)}, u32[]{:S(2)}, u32[]{:S(2)}) %collective-permute-start.10) | collective-permute-done | bytes 262176 | tf_op jit(solution)/shard_map/ppermute | solution.py:818
  38.7 5.7 %collective-permute-done.11.third = bf16[128,1024]{1,0:T(8,128)(2,1)S(1)} collective-permute-done((bf16[128,1024]{1,0:T(8,128)(2,1)S(1)}, bf16[128,1024]{1,0:T(8,128)(2,1)S(1)}, u32[]{:S(2)}, u32[]{:S(2)}) %collective-permute-start.11) | collective-permute-done | bytes 262176 | tf_op jit(solution)/shard_map/ppermute | solution.py:818
  44.4 0.0 collective-permute-done.7.rest_4_.rest_1_
  44.4 0.0 collective-permute-done.8.rest_5_.rest_2_
  44.4 0.0 collective-permute-done.9.rest_6_.rest_3_
  44.4 0.5 finish_values.1
  44.9 2.5 %collective-permute-start.12 = (bf16[176,128]{1,0:T(8,128)(2,1)S(1)}, bf16[176,128]{1,0:T(8,128)(2,1)S(1)}, u32[]{:S(2)}, u32[]{:S(2)}) collective-permute-start(bf16[176,128]{1,0:T(8,128)(2,1)S(1)} %get-tuple-element.81), channel_id=1, source_target_pairs={{0,3},{1,2},{2,1},{3,0},{4,7},{5,6},{6,5},{7,4},{8,11},{9,10},{10,... | collective-permute-start | bytes 135176 | tf_op jit(solution)/shard_map/ppermute | solution.py:818
  47.3 1.3 %collective-permute-start.13 = (bf16[176,128]{1,0:T(8,128)(2,1)S(1)}, bf16[176,128]{1,0:T(8,128)(2,1)S(1)}, u32[]{:S(2)}, u32[]{:S(2)}) collective-permute-start(bf16[176,128]{1,0:T(8,128)(2,1)S(1)} %get-tuple-element.82), channel_id=1, source_target_pairs={{0,2},{1,3},{2,0},{3,1},{4,6},{5,7},{6,4},{7,5},{8,10},{9,11},{10,... | collective-permute-start | bytes 135176 | tf_op jit(solution)/shard_map/ppermute | solution.py:818
  48.7 0.7 %collective-permute-start.14 = (bf16[176,128]{1,0:T(8,128)(2,1)S(1)}, bf16[176,128]{1,0:T(8,128)(2,1)S(1)}, u32[]{:S(2)}, u32[]{:S(2)}) collective-permute-start(bf16[176,128]{1,0:T(8,128)(2,1)S(1)} %get-tuple-element.83), channel_id=1, source_target_pairs={{0,1},{1,0},{2,3},{3,2},{4,5},{5,4},{6,7},{7,6},{8,9},{9,8},{10,11... | collective-permute-start | bytes 135176 | tf_op jit(solution)/shard_map/ppermute | solution.py:818
  49.3 1.5 %collective-permute-start.16 = (bf16[64,1024]{1,0:T(8,128)(2,1)S(1)}, bf16[64,1024]{1,0:T(8,128)(2,1)S(1)}, u32[]{:S(2)}, u32[]{:S(2)}) collective-permute-start(bf16[64,1024]{1,0:T(8,128)(2,1)S(1)} %get-tuple-element.86), channel_id=1, source_target_pairs={{0,8},{4,12},{8,0},{12,4},{1,9},{5,13},{9,1},{13,5},{2,10},{6,14},... | collective-permute-start | bytes 393224 | tf_op jit(solution)/shard_map/ppermute | solution.py:821
  50.8 0.0 collective-permute-start.17
  50.8 0.0 collective-permute-done.12.refs_1_
  50.9 2.0 %collective-permute-done.13.refs_2_ = bf16[176,128]{1,0:T(8,128)(2,1)S(1)} collective-permute-done((bf16[176,128]{1,0:T(8,128)(2,1)S(1)}, bf16[176,128]{1,0:T(8,128)(2,1)S(1)}, u32[]{:S(2)}, u32[]{:S(2)}) %collective-permute-start.13) | collective-permute-done | bytes 45088 | tf_op jit(solution)/shard_map/ppermute | solution.py:818
  52.9 0.3 collective-permute-done.14.refs_3_
  53.2 0.2 gather_parts.1
  53.3 0.1 collective-permute-start.15
  53.4 1.3 %collective-permute-start.18 = (bf16[16,256]{1,0:T(8,128)(2,1)S(1)}, bf16[16,256]{1,0:T(8,128)(2,1)S(1)}, u32[]{:S(2)}, u32[]{:S(2)}) collective-permute-start(bf16[16,256]{1,0:T(8,128)(2,1)S(1)} %get-tuple-element.92), channel_id=1, source_target_pairs={{0,8},{4,12},{8,0},{12,4},{1,9},{5,13},{9,1},{13,5},{2,10},{6,14},... | collective-permute-start | bytes 24584 | tf_op jit(solution)/shard_map/ppermute | solution.py:821
  54.7 0.6 collective-permute-start.19
  55.3 0.0 collective-permute-done.16.rest_6_
  55.3 0.3 collective-permute-start.20
  55.6 0.2 blend_kept.1
  55.8 0.8 %collective-permute-done.17.rest_7_ = bf16[64,1024]{1,0:T(8,128)(2,1)S(1)} collective-permute-done((bf16[64,1024]{1,0:T(8,128)(2,1)S(1)}, bf16[64,1024]{1,0:T(8,128)(2,1)S(1)}, u32[]{:S(2)}, u32[]{:S(2)}) %collective-permute-start.17) | collective-permute-done | bytes 131104 | tf_op jit(solution)/shard_map/ppermute | solution.py:821
  56.6 0.0 collective-permute-done.15.rest_5_
  56.6 1.4 %place_pages.1 = (bf16[16,64,2048]{2,1,0:T(8,128)(2,1)}, bf16[16,128]{1,0:T(8,128)(2,1)S(1)}) custom-call(s32[3,8]{1,0:T(4,128)S(1)} %bitcast.16, s32[2,8]{1,0:T(2,128)S(1)} %bitcast.18, bf16[16,64,2048]{2,1,0:T(8,128)(2,1)} %get-tuple-element.61.pool, bf16[64,1024]{1,0:T(8,128)(2,1)S(1)} %get-tuple-element.64.rest_0_, ...), custom_call_target="tpu_custom_call", output_to_operand_aliasing={{0}: (2, {})} | custom-call | flops 1 | bytes 1 | tf_op jit(solution)/shard_map/place_pages/pallas_call | solution.py:681
  58.1 0.0 collective-permute-done.18.refs_1_
  58.1 0.0 collective-permute-done.19.refs_2_
  58.1 0.0 collective-permute-done.20.refs_3_
  58.1 0.8 %combine.1 = bf16[8,2048]{1,0:T(8,128)(2,1)} custom-call(f32[40,128]{1,0:T(8,128)S(1)} %get-tuple-element.68.marks, f32[128,128]{1,0:T(8,128)S(1)} %get-tuple-element.90.kept_out, f32[128,128]{1,0:T(8,128)S(1)} %get-tuple-element.91.kept_level, bf16[16,256]{1,0:T(8,128)(2,1)S(1)} %get-tuple-element.89.refs_4_.refs_0_, ...), custom_call_target="tpu_custom_call" | custom-call | flops 1 | bytes 1 | tf_op jit(solution)/shard_map/combine/pallas_call | solution.py:787
  (2 shorter events, 0.0 us)
Async XLA Ops:
  3.6 11.1 %collective-permute-start = (bf16[136,1024]{1,0:T(8,128)(2,1)S(1)}, bf16[136,1024]{1,0:T(8,128)(2,1)S(1)}, u32[]{:S(2)}, u32[]{:S(2)}) collective-permute-start(bf16[136,1024]{1,0:T(8,128)(2,1)S(1)} %get-tuple-element.54), channel_id=1, source_target_pairs={{0,1},{3,2},{1,3},{2,0},{4,5},{7,6},{5,7},{6,4},{8,9},{11,10},{9,1... | collective-permute-start | bytes 835592 | tf_op jit(solution)/shard_map/ppermute | solution.py:818
  6.6 12.7 %copy-start.3 = (bf16[8,8192]{1,0:T(8,128)(2,1)S(1)}, bf16[8,8192]{1,0:T(8,128)(2,1)}, u32[]{:S(2)}) copy-start(bf16[8,8192]{1,0:T(8,128)(2,1)} %param.14) | copy-start | bytes 393220
  6.6 12.8 %copy-start = (s32[8,3]{0,1:T(4,128)S(1)}, s32[8,3]{0,1:T(4,128)}, u32[]{:S(2)}) copy-start(s32[8,3]{0,1:T(4,128)} %param.11) | copy-start | bytes 292
  10.8 14.0 %copy-start.1 = (s32[8,2,1]{0,2,1:T(1,128)S(1)}, s32[8,2,1]{0,2,1:T(1,128)}, u32[]{:S(2)}) copy-start(s32[8,2,1]{0,2,1:T(1,128)} %param.12) | copy-start | bytes 196
  10.8 14.0 %copy-start.2 = (s32[8]{0:T(128)S(1)}, s32[8]{0:T(128)}, u32[]{:S(2)}) copy-start(s32[8]{0:T(128)} %lengths.1) | copy-start | bytes 100
  10.8 10.9 %collective-permute-start.1 = (bf16[128,1024]{1,0:T(8,128)(2,1)S(1)}, bf16[128,1024]{1,0:T(8,128)(2,1)S(1)}, u32[]{:S(2)}, u32[]{:S(2)}) collective-permute-start(bf16[128,1024]{1,0:T(8,128)(2,1)S(1)} %get-tuple-element.56), channel_id=1, source_target_pairs={{0,1},{3,2},{1,3},{2,0},{4,5},{7,6},{5,7},{6,4},{8,9},{11,10},{9,1... | collective-permute-start | bytes 786440 | tf_op jit(solution)/shard_map/ppermute | solution.py:818
  13.5 20.9 %collective-permute-start.5 = (bf16[136,1024]{1,0:T(8,128)(2,1)S(1)}, bf16[136,1024]{1,0:T(8,128)(2,1)S(1)}, u32[]{:S(2)}, u32[]{:S(2)}) collective-permute-start(bf16[136,1024]{1,0:T(8,128)(2,1)S(1)} %get-tuple-element.63), channel_id=1, source_target_pairs={{0,1},{1,0},{2,3},{3,2},{4,5},{5,4},{6,7},{7,6},{8,9},{9,8},{10,11... | collective-permute-start | bytes 835592 | tf_op jit(solution)/shard_map/ppermute | solution.py:818
  14.7 19.6 %collective-permute-start.6 = (bf16[136,1024]{1,0:T(8,128)(2,1)S(1)}, bf16[136,1024]{1,0:T(8,128)(2,1)S(1)}, u32[]{:S(2)}, u32[]{:S(2)}) collective-permute-start(bf16[136,1024]{1,0:T(8,128)(2,1)S(1)} %carry.2.rest_0_), channel_id=1, source_target_pairs={{0,3},{3,0},{1,2},{2,1},{4,7},{7,4},{5,6},{6,5},{8,11},{11,8},{9,1... | collective-permute-start | bytes 835592 | tf_op jit(solution)/shard_map/ppermute | solution.py:818
  20.0 3.7 %collective-permute-start.2 = (bf16[64,128]{1,0:T(8,128)(2,1)S(1)}, bf16[64,128]{1,0:T(8,128)(2,1)S(1)}, u32[]{:S(2)}, u32[]{:S(2)}) collective-permute-start(bf16[64,128]{1,0:T(8,128)(2,1)S(1)} %get-tuple-element.58), channel_id=1, source_target_pairs={{0,4},{4,0},{8,12},{12,8},{1,5},{5,1},{9,13},{13,9},{2,6},{6,2},{1... | collective-permute-start | bytes 49160 | tf_op jit(solution)/shard_map/ppermute | solution.py:821
  20.1 4.5 %collective-permute-start.3 = (bf16[64,128]{1,0:T(8,128)(2,1)S(1)}, bf16[64,128]{1,0:T(8,128)(2,1)S(1)}, u32[]{:S(2)}, u32[]{:S(2)}) collective-permute-start(bf16[64,128]{1,0:T(8,128)(2,1)S(1)} %get-tuple-element.59), channel_id=1, source_target_pairs={{0,8},{4,12},{8,0},{12,4},{1,9},{5,13},{9,1},{13,5},{2,10},{6,14},... | collective-permute-start | bytes 49160 | tf_op jit(solution)/shard_map/ppermute | solution.py:821
  21.7 3.2 %collective-permute-start.4 = (bf16[64,128]{1,0:T(8,128)(2,1)S(1)}, bf16[64,128]{1,0:T(8,128)(2,1)S(1)}, u32[]{:S(2)}, u32[]{:S(2)}) collective-permute-start(bf16[64,128]{1,0:T(8,128)(2,1)S(1)} %get-tuple-element.60), channel_id=1, source_target_pairs={{0,12},{4,8},{8,4},{12,0},{1,13},{5,9},{9,5},{13,1},{2,14},{6,10},... | collective-permute-start | bytes 49160 | tf_op jit(solution)/shard_map/ppermute | solution.py:821
  23.8 14.9 %collective-permute-start.10 = (bf16[128,1024]{1,0:T(8,128)(2,1)S(1)}, bf16[128,1024]{1,0:T(8,128)(2,1)S(1)}, u32[]{:S(2)}, u32[]{:S(2)}) collective-permute-start(bf16[128,1024]{1,0:T(8,128)(2,1)S(1)} %get-tuple-element.57.rest_0_), channel_id=1, source_target_pairs={{0,1},{1,0},{2,3},{3,2},{4,5},{5,4},{6,7},{7,6},{8,9},{9,8},{10,11... | collective-permute-start | bytes 786440 | tf_op jit(solution)/shard_map/ppermute | solution.py:818
  30.9 13.5 %collective-permute-start.11 = (bf16[128,1024]{1,0:T(8,128)(2,1)S(1)}, bf16[128,1024]{1,0:T(8,128)(2,1)S(1)}, u32[]{:S(2)}, u32[]{:S(2)}) collective-permute-start(bf16[128,1024]{1,0:T(8,128)(2,1)S(1)} %carry.3), channel_id=1, source_target_pairs={{0,3},{3,0},{1,2},{2,1},{4,7},{7,4},{5,6},{6,5},{8,11},{11,8},{9,1... | collective-permute-start | bytes 786440 | tf_op jit(solution)/shard_map/ppermute | solution.py:818
  36.0 8.4 %collective-permute-start.7 = (bf16[64,1024]{1,0:T(8,128)(2,1)S(1)}, bf16[64,1024]{1,0:T(8,128)(2,1)S(1)}, u32[]{:S(2)}, u32[]{:S(2)}) collective-permute-start(bf16[64,1024]{1,0:T(8,128)(2,1)S(1)} %get-tuple-element.65), channel_id=1, source_target_pairs={{0,4},{4,0},{8,12},{12,8},{1,5},{5,1},{9,13},{13,9},{2,6},{6,2},{1... | collective-permute-start | bytes 393224 | tf_op jit(solution)/shard_map/ppermute | solution.py:821
  36.1 8.3 %collective-permute-start.8 = (bf16[64,1024]{1,0:T(8,128)(2,1)S(1)}, bf16[64,1024]{1,0:T(8,128)(2,1)S(1)}, u32[]{:S(2)}, u32[]{:S(2)}) collective-permute-start(bf16[64,1024]{1,0:T(8,128)(2,1)S(1)} %get-tuple-element.66), channel_id=1, source_target_pairs={{0,8},{4,12},{8,0},{12,4},{1,9},{5,13},{9,1},{13,5},{2,10},{6,14},... | collective-permute-start | bytes 393224 | tf_op jit(solution)/shard_map/ppermute | solution.py:821
  37.5 6.9 %collective-permute-start.9 = (bf16[64,1024]{1,0:T(8,128)(2,1)S(1)}, bf16[64,1024]{1,0:T(8,128)(2,1)S(1)}, u32[]{:S(2)}, u32[]{:S(2)}) collective-permute-start(bf16[64,1024]{1,0:T(8,128)(2,1)S(1)} %get-tuple-element.67), channel_id=1, source_target_pairs={{0,12},{4,8},{8,4},{12,0},{1,13},{5,9},{9,5},{13,1},{2,14},{6,10},... | collective-permute-start | bytes 393224 | tf_op jit(solution)/shard_map/ppermute | solution.py:821
  44.9 6.0 %collective-permute-start.12 = (bf16[176,128]{1,0:T(8,128)(2,1)S(1)}, bf16[176,128]{1,0:T(8,128)(2,1)S(1)}, u32[]{:S(2)}, u32[]{:S(2)}) collective-permute-start(bf16[176,128]{1,0:T(8,128)(2,1)S(1)} %get-tuple-element.81), channel_id=1, source_target_pairs={{0,3},{1,2},{2,1},{3,0},{4,7},{5,6},{6,5},{7,4},{8,11},{9,10},{10,... | collective-permute-start | bytes 135176 | tf_op jit(solution)/shard_map/ppermute | solution.py:818
  47.3 5.5 %collective-permute-start.13 = (bf16[176,128]{1,0:T(8,128)(2,1)S(1)}, bf16[176,128]{1,0:T(8,128)(2,1)S(1)}, u32[]{:S(2)}, u32[]{:S(2)}) collective-permute-start(bf16[176,128]{1,0:T(8,128)(2,1)S(1)} %get-tuple-element.82), channel_id=1, source_target_pairs={{0,2},{1,3},{2,0},{3,1},{4,6},{5,7},{6,4},{7,5},{8,10},{9,11},{10,... | collective-permute-start | bytes 135176 | tf_op jit(solution)/shard_map/ppermute | solution.py:818
  48.7 4.5 %collective-permute-start.14 = (bf16[176,128]{1,0:T(8,128)(2,1)S(1)}, bf16[176,128]{1,0:T(8,128)(2,1)S(1)}, u32[]{:S(2)}, u32[]{:S(2)}) collective-permute-start(bf16[176,128]{1,0:T(8,128)(2,1)S(1)} %get-tuple-element.83), channel_id=1, source_target_pairs={{0,1},{1,0},{2,3},{3,2},{4,5},{5,4},{6,7},{7,6},{8,9},{9,8},{10,11... | collective-permute-start | bytes 135176 | tf_op jit(solution)/shard_map/ppermute | solution.py:818
  49.3 5.9 %collective-permute-start.16 = (bf16[64,1024]{1,0:T(8,128)(2,1)S(1)}, bf16[64,1024]{1,0:T(8,128)(2,1)S(1)}, u32[]{:S(2)}, u32[]{:S(2)}) collective-permute-start(bf16[64,1024]{1,0:T(8,128)(2,1)S(1)} %get-tuple-element.86), channel_id=1, source_target_pairs={{0,8},{4,12},{8,0},{12,4},{1,9},{5,13},{9,1},{13,5},{2,10},{6,14},... | collective-permute-start | bytes 393224 | tf_op jit(solution)/shard_map/ppermute | solution.py:821
  50.8 5.8 %collective-permute-start.17 = (bf16[64,1024]{1,0:T(8,128)(2,1)S(1)}, bf16[64,1024]{1,0:T(8,128)(2,1)S(1)}, u32[]{:S(2)}, u32[]{:S(2)}) collective-permute-start(bf16[64,1024]{1,0:T(8,128)(2,1)S(1)} %get-tuple-element.87), channel_id=1, source_target_pairs={{0,12},{4,8},{8,4},{12,0},{1,13},{5,9},{9,5},{13,1},{2,14},{6,10},... | collective-permute-start | bytes 393224 | tf_op jit(solution)/shard_map/ppermute | solution.py:821
  53.3 3.3 %collective-permute-start.15 = (bf16[64,1024]{1,0:T(8,128)(2,1)S(1)}, bf16[64,1024]{1,0:T(8,128)(2,1)S(1)}, u32[]{:S(2)}, u32[]{:S(2)}) collective-permute-start(bf16[64,1024]{1,0:T(8,128)(2,1)S(1)} %get-tuple-element.85), channel_id=1, source_target_pairs={{0,4},{4,0},{8,12},{12,8},{1,5},{5,1},{9,13},{13,9},{2,6},{6,2},{1... | collective-permute-start | bytes 393224 | tf_op jit(solution)/shard_map/ppermute | solution.py:821
  53.4 4.7 %collective-permute-start.18 = (bf16[16,256]{1,0:T(8,128)(2,1)S(1)}, bf16[16,256]{1,0:T(8,128)(2,1)S(1)}, u32[]{:S(2)}, u32[]{:S(2)}) collective-permute-start(bf16[16,256]{1,0:T(8,128)(2,1)S(1)} %get-tuple-element.92), channel_id=1, source_target_pairs={{0,8},{4,12},{8,0},{12,4},{1,9},{5,13},{9,1},{13,5},{2,10},{6,14},... | collective-permute-start | bytes 24584 | tf_op jit(solution)/shard_map/ppermute | solution.py:821
  54.7 3.4 %collective-permute-start.19 = (bf16[16,256]{1,0:T(8,128)(2,1)S(1)}, bf16[16,256]{1,0:T(8,128)(2,1)S(1)}, u32[]{:S(2)}, u32[]{:S(2)}) collective-permute-start(bf16[16,256]{1,0:T(8,128)(2,1)S(1)} %get-tuple-element.93), channel_id=1, source_target_pairs={{0,12},{4,8},{8,4},{12,0},{1,13},{5,9},{9,5},{13,1},{2,14},{6,10},... | collective-permute-start | bytes 24584 | tf_op jit(solution)/shard_map/ppermute | solution.py:821
  55.3 2.8 %collective-permute-start.20 = (bf16[16,256]{1,0:T(8,128)(2,1)S(1)}, bf16[16,256]{1,0:T(8,128)(2,1)S(1)}, u32[]{:S(2)}, u32[]{:S(2)}) collective-permute-start(bf16[16,256]{1,0:T(8,128)(2,1)S(1)} %get-tuple-element.94), channel_id=1, source_target_pairs={{0,4},{4,0},{8,12},{12,8},{1,5},{5,1},{9,13},{13,9},{2,6},{6,2},{1... | collective-permute-start | bytes 24584 | tf_op jit(solution)/shard_map/ppermute | solution.py:821

commit v6 on v5

--- a/solution.py
+++ b/solution.py
@@ -399,32 +399,39 @@
     return [jax.ShapeDtypeStruct((rows, width), BF16)] * 4
 
 
-def ask_kernel(jobs, query, *rest):
-    outs, marks = rest[-5:-1], rest[-1]
+def ask_kernel(jobs, table, query, *rest):
+    outs, marks, places = rest[-6:-2], rest[-2], rest[-1]
     slots = query.shape[0]
     replica = lax.axis_index("rep")
     line = lax.broadcasted_iota(jnp.int32, marks.shape, 0)
     found = jnp.zeros(marks.shape, jnp.int32)
+    place_line = lax.broadcasted_iota(jnp.int32, places.shape, 0)
+    spots = jnp.full(places.shape, -1, jnp.int32)
     for step, out in enumerate(outs):
-        hit, context, _ = job_from(jobs, step)
+        hit, context, page = job_from(jobs, step)
         out[...] = query[context]
         sent = jobs[0, replica * SENDS] == jnp.bitwise_xor(replica, step)
         found = found + jnp.where(line == step * slots + context, hit.astype(jnp.int32), 0)
         found = found + jnp.where(line == 4 * slots + step, sent.astype(jnp.int32), 0)
+        spots = jnp.where(place_line == step, jnp.where(hit, table[page, context], -1), spots)
     marks[...] = found.astype(F32)
-
-
-def ask(jobs, query, after):
+    places[...] = spots
+
+
+def ask(jobs, table, query, after):
     return pl.pallas_call(
         ask_kernel,
-        in_specs=[whole(SMEM), whole()] + [whole(pl.ANY)] * len(after),
-        out_specs=[whole()] * 5,
+        in_specs=[whole(SMEM)] * 2 + [whole()] + [whole(pl.ANY)] * len(after),
+        out_specs=[whole()] * 6,
         out_shape=rep_shapes(*query.shape[1:])
-        + [jax.ShapeDtypeStruct((4 * query.shape[0] + 8, LANES), F32)],
+        + [
+            jax.ShapeDtypeStruct((4 * query.shape[0] + 8, LANES), F32),
+            jax.ShapeDtypeStruct((8, LANES), jnp.int32),
+        ],
         compiler_params=pltpu.CompilerParams(vmem_limit_bytes=LIMIT),
         cost_estimate=SMALL,
         name="ask",
-    )(jobs, query, *after)
+    )(jobs, table, query, *after)
 
 
 def kept_kernel(jobs, table, lengths, query, pool, *rest, shards, after):
@@ -656,19 +663,18 @@
     return hit, jobs[1, row], jobs[2, row]
 
 
-def place_kernel(jobs, table, pool, *rest):
+def place_kernel(places, pool, *rest):
     key_pages, value_pages = rest[:4], rest[4:8]
     out, done, pages, sem = rest[8:]
-    half = rest[0].shape[1]
+    half = key_pages[0].shape[1]
+    spots = [jnp.max(places[step : step + 1]) for step in range(4)]
     done[...] = jnp.zeros_like(done)
     for wait in (False, True):
-        for step in range(4):
-            hit, context, page = job_from(jobs, step)
-
-            @pl.when(hit)
+        for step, spot in enumerate(spots):
+
+            @pl.when(spot >= 0)
             def _():
-                slot = table[page, context]
-                copy = pltpu.make_async_copy(pages.at[step], out.at[slot], sem.at[step])
+                copy = pltpu.make_async_copy(pages.at[step], out.at[spot], sem.at[step])
                 if wait:
                     copy.wait()
                 else:
@@ -677,18 +683,18 @@
                     copy.start()
 
 
-def place_pages(jobs, table, pool, key_pages, value_pages):
+def place_pages(places, pool, key_pages, value_pages):
     return pl.pallas_call(
         place_kernel,
-        in_specs=[whole(SMEM)] * 2 + [whole(pl.ANY)] + [whole()] * 8,
+        in_specs=[whole(), whole(pl.ANY)] + [whole()] * 8,
         out_specs=[whole(pl.ANY), whole()],
         out_shape=[jax.ShapeDtypeStruct(pool.shape, pool.dtype), jax.ShapeDtypeStruct((16, LANES), BF16)],
         scratch_shapes=[pltpu.VMEM((4,) + pool.shape[1:], pool.dtype), pltpu.SemaphoreType.DMA((4,))],
-        input_output_aliases={2: 0},
+        input_output_aliases={1: 0},
         compiler_params=pltpu.CompilerParams(vmem_limit_bytes=LIMIT),
         cost_estimate=SMALL,
         name="place_pages",
-    )(jobs, table, pool, *key_pages, *value_pages)
+    )(places, pool, *key_pages, *value_pages)
 
 
 def blend(parts, levels):
@@ -706,7 +712,7 @@
     levels = join_lines(tail, 3, LANES)
     mixed, level = blend(
         [ref[rows : rows + count].astype(F32) for ref in parts],
-        [levels[step * count : (step + 1) * count] for step in (0, 3, 2, 1)],
+        [levels[step * count : (step + 1) * count] for step in (0, 2, 3, 1)],
     )
     here = count // SENDS
     lane = lax.broadcasted_iota(jnp.int32, (here, LANES), 1)
@@ -832,12 +838,13 @@
     key_near = along(key_1, NEAR)
     key_2 = carry(key_2, key_first, [])
     key_third = along(key_2, THIRD)
-    *asked, marks = ask(jobs, query, [key_2])
+    *asked, marks, places = ask(jobs, table, query, [key_2])
     asked = between(asked)
     value_0, value_1, value_2 = project_values(gained, tile, [asked[0], value_first])
     value_near = along(value_1, NEAR)
-    *kept_parts, new_pool = kept(jobs, table, context_lengths, query, kv_pool, [value_1] + asked[1:], shards)
-    value_third = along(carry(value_2, value_first, [kept_parts[0]]), THIRD)
+    value_2 = carry(value_2, value_first, asked[1:])
+    value_third = along(value_2, THIRD)
+    *kept_parts, new_pool = kept(jobs, table, context_lengths, query, kv_pool, [value_2], shards)
     frequency = THETA ** (-(jnp.arange(HD // 2, dtype=F32) * 2.0 / HD))
     frequency = jnp.concatenate([frequency, frequency])[None, :]
     *key_out, scale, weights, share, tails = finish_keys(
@@ -858,14 +865,14 @@
     value_pages = [finished[0], None, across(finished[2], 2), across(finished[3], 3)]
     packed = finished[4:]
     parts = [packed[0]] + [
-        along(packed[step], [(i, i ^ step) for i in range(shards)]) for step in range(shards - 1, 0, -1)
+        along(packed[step], [(i, i ^ step) for i in range(shards)]) for step in (2, 3, 1)
     ]
     here = QH // shards
     *gathered, near_page = gather_parts(marks, parts, finished[1], slots * here, SENDS * here)
     fresh = [gathered[0]] + [across(gathered[step], step) for step in FRESH_ORDER[1:]]
     value_pages[1] = across(near_page, 1)
     kept_out, kept_level = blend_kept(parts, gathered[0], slots * here, SENDS * here)
-    new_pool, placed = place_pages(jobs, table, new_pool, key_pages, value_pages)
+    new_pool, placed = place_pages(places, new_pool, key_pages, value_pages)
     return (new_pool, combine(marks, kept_out, kept_level, fresh, placed, slots))
 
 

time: 59 us -> 58.1 us (0.985)
  starting transfers between devices: 27 us -> 25.9 us
    ppermute x9, starting transfers between devices: 19.4 us -> 18.3 us  [along(): return lax.ppermute(array, 'shard', pairs)]
  transfers between devices with their start and end apart: 21 -> 21, of which waited for: 7 -> 8; matrix products, arithmetic and copies ran while one was open for 0% -> 0% of each run, Pallas kernels for 27% -> 27%
where the time goes in v6:
time: 58.1 us; the launch traced here: 58 us
  starting transfers between devices  25.9 us (45%)
  Pallas kernels  20.1 us (35%)
  waiting for transfers between devices  11.1 us (19%)
  between operations  0.81 us (1%)
    ppermute x9, starting transfers between devices, along(): return lax.ppermute(array, 'shard', pairs)  18.3 us
    ppermute x9, waiting for transfers between devices, along(): return lax.ppermute(array, 'shard', pairs)  9.64 us
    ppermute x12, starting transfers between devices, across(): return lax.ppermute(array, 'rep', [(i, i ^ step) for i in range(replicas)])  7.63 us
    pallas_call x1, Pallas kernels, kept(): pl.pallas_call(functools.partial(kept_kernel, shards=shards, after=len(af...  6 us
    pallas_call x1, Pallas kernels, project_keys(): pl.pallas_call(project_keys_kernel, in_specs=[whole(pl.ANY)] * 3 + [whole...  4.14 us
    pallas_call x1, Pallas kernels, project_first(): pl.pallas_call(first_kernel, in_specs=[whole(pl.ANY)] * 3, out_specs=[who...  2.95 us
    pallas_call x1, Pallas kernels, project_values(): pl.pallas_call(project_values_kernel, in_specs=[whole()] * 2 + [whole(pl....  1.78 us
    pallas_call x1, Pallas kernels, finish_keys(): pl.pallas_call(functools.partial(finish_keys_kernel, stripe=stripe), in_s...  1.62 us
  transfers between devices with their start and end apart: 21, of which 8 were waited for; matrix products, arithmetic and copies ran while one was open for 0% of the time, Pallas kernels for 27%

profile of v6, /device:TPU:0, one launch (start us, length us, event | category | flops | bytes accessed | tf_op | source)
XLA Modules:
  0.0 58.0 jit_solution(17011114848588127921)
XLA Ops:
  0.6 3.0 %project_first.1 = (bf16[136,1024]{1,0:T(8,128)(2,1)S(1)}, bf16[128,2048]{1,0:T(8,128)(2,1)S(1)}, bf16[2048,1024]{1,0:T(8,128)(2,1)S(1)}) custom-call(bf16[2,4,64,2048]{3,2,1,0:T(8,128)(2,1)} %bitcast.18, bf16[2048]{0:T(1024)(128)(2,1)} %gain.3, bf16[2048,2048]{1,0:T(8,128)(2,1)} %weight.3), custom_call_target="tpu_custom_call" | custom-call | flops 1 | bytes 1 | tf_op jit(solution)/shard_map/project_first/pallas_call | solution.py:236
  3.6 3.1 %collective-permute-start = (bf16[136,1024]{1,0:T(8,128)(2,1)S(1)}, bf16[136,1024]{1,0:T(8,128)(2,1)S(1)}, u32[]{:S(2)}, u32[]{:S(2)}) collective-permute-start(bf16[136,1024]{1,0:T(8,128)(2,1)S(1)} %get-tuple-element.53), channel_id=1, source_target_pairs={{0,1},{3,2},{1,3},{2,0},{4,5},{7,6},{5,7},{6,4},{8,9},{11,10},{9,1... | collective-permute-start | bytes 835592 | tf_op jit(solution)/shard_map/ppermute | solution.py:824
  6.6 0.0 copy-start.3
  6.6 0.0 copy-start
  6.6 0.0 copy-start.1
  6.6 4.1 %project_keys.1 = (bf16[136,1024]{1,0:T(8,128)(2,1)S(1)}, bf16[136,1024]{1,0:T(8,128)(2,1)S(1)}, bf16[136,1024]{1,0:T(8,128)(2,1)S(1)}, bf16[128,1024]{1,0:T(8,1...) custom-call(bf16[2,4,64,2048]{3,2,1,0:T(8,128)(2,1)} %bitcast.19, bf16[2048]{0:T(1024)(128)(2,1)} %gain.3, ...), custom_call_target="tpu_custom_call" | custom-call | flops 1 | bytes 1 | tf_op jit(solution)/shard_map/project_keys/pallas_call | solution.py:338
  10.8 2.6 %collective-permute-start.1 = (bf16[128,1024]{1,0:T(8,128)(2,1)S(1)}, bf16[128,1024]{1,0:T(8,128)(2,1)S(1)}, u32[]{:S(2)}, u32[]{:S(2)}) collective-permute-start(bf16[128,1024]{1,0:T(8,128)(2,1)S(1)} %get-tuple-element.58), channel_id=1, source_target_pairs={{0,1},{3,2},{1,3},{2,0},{4,5},{7,6},{5,7},{6,4},{8,9},{11,10},{9,1... | collective-permute-start | bytes 786440 | tf_op jit(solution)/shard_map/ppermute | solution.py:824
  13.4 0.4 collective-permute-start.5
  13.9 0.8 %collective-permute-done.first = bf16[136,1024]{1,0:T(8,128)(2,1)S(1)} collective-permute-done((bf16[136,1024]{1,0:T(8,128)(2,1)S(1)}, bf16[136,1024]{1,0:T(8,128)(2,1)S(1)}, u32[]{:S(2)}, u32[]{:S(2)}) %collective-permute-start) | collective-permute-done | bytes 278560 | tf_op jit(solution)/shard_map/ppermute | solution.py:824
  14.7 0.1 carry.2.rest_0_
  14.8 4.6 %collective-permute-start.6 = (bf16[136,1024]{1,0:T(8,128)(2,1)S(1)}, bf16[136,1024]{1,0:T(8,128)(2,1)S(1)}, u32[]{:S(2)}, u32[]{:S(2)}) collective-permute-start(bf16[136,1024]{1,0:T(8,128)(2,1)S(1)} %carry.2.rest_0_), channel_id=1, source_target_pairs={{0,3},{3,0},{1,2},{2,1},{4,7},{7,4},{5,6},{6,5},{8,11},{11,8},{9,1... | collective-permute-start | bytes 835592 | tf_op jit(solution)/shard_map/ppermute | solution.py:824
  19.4 0.0 copy-done.3
  19.4 0.0 copy-done
  19.4 0.0 copy-done.1
  19.4 0.0 copy-start.2
  19.4 0.6 %ask.1 = (bf16[64,128]{1,0:T(8,128)(2,1)S(1)}, bf16[64,128]{1,0:T(8,128)(2,1)S(1)}, bf16[64,128]{1,0:T(8,128)(2,1)S(1)}, bf16[64,128]{1,0:T(8,128)(2,1)S(1)}, f3...) custom-call(s32[3,8]{1,0:T(4,128)S(1)} %bitcast.13, s32[2,8]{1,0:T(2,128)S(1)} %bitcast.16, bf16[8,64,128]{2,1,0:T(8,128)(2,1)S(1)} %bitcast.11, ...), custom_call_target="tpu_custom_call" | custom-call | flops 1 | bytes 1 | tf_op jit(solution)/shard_map/ask/pallas_call | solution.py:422
  20.1 0.1 collective-permute-start.2
  20.2 1.5 %collective-permute-start.3 = (bf16[64,128]{1,0:T(8,128)(2,1)S(1)}, bf16[64,128]{1,0:T(8,128)(2,1)S(1)}, u32[]{:S(2)}, u32[]{:S(2)}) collective-permute-start(bf16[64,128]{1,0:T(8,128)(2,1)S(1)} %get-tuple-element.61), channel_id=1, source_target_pairs={{0,8},{4,12},{8,0},{12,4},{1,9},{5,13},{9,1},{13,5},{2,10},{6,14},... | collective-permute-start | bytes 49160 | tf_op jit(solution)/shard_map/ppermute | solution.py:827
  21.7 0.0 collective-permute-done.1.rest_1_.first
  21.7 0.3 collective-permute-start.4
  22.0 1.8 %project_values.1 = (bf16[128,1024]{1,0:T(8,128)(2,1)S(1)}, bf16[128,1024]{1,0:T(8,128)(2,1)S(1)}, bf16[128,1024]{1,0:T(8,128)(2,1)S(1)}) custom-call(bf16[384,2048]{1,0:T(8,128)(2,1)S(1)} %get-tuple-element.55.gained, bf16[2048,1024]{1,0:T(8,128)(2,1)S(1)} %get-tuple-element.56.tile, bf16[64,128]{1,0:T(8,128)(2,1)S(1)} %get-tuple-element.57.rest_0_, ...), custom_call_target="tpu_custom_call" | custom-call | flops 1 | bytes 1 | tf_op jit(solution)/shard_map/project_values/pallas_call | solution.py:369
  23.8 0.0 collective-permute-done.2.rest_0_.rest_1_
  23.8 0.7 %collective-permute-start.10 = (bf16[128,1024]{1,0:T(8,128)(2,1)S(1)}, bf16[128,1024]{1,0:T(8,128)(2,1)S(1)}, u32[]{:S(2)}, u32[]{:S(2)}) collective-permute-start(bf16[128,1024]{1,0:T(8,128)(2,1)S(1)} %get-tuple-element.72), channel_id=1, source_target_pairs={{0,1},{1,0},{2,3},{3,2},{4,5},{5,4},{6,7},{7,6},{8,9},{9,8},{10,11... | collective-permute-start | bytes 786440 | tf_op jit(solution)/shard_map/ppermute | solution.py:824
  24.5 0.0 collective-permute-done.3.rest_1_.rest_2_
  24.5 0.3 collective-permute-done.4.rest_2_.rest_3_
  24.9 0.1 carry.3.rest_0_
  25.0 3.3 %collective-permute-start.11 = (bf16[128,1024]{1,0:T(8,128)(2,1)S(1)}, bf16[128,1024]{1,0:T(8,128)(2,1)S(1)}, u32[]{:S(2)}, u32[]{:S(2)}) collective-permute-start(bf16[128,1024]{1,0:T(8,128)(2,1)S(1)} %carry.3.rest_0_), channel_id=1, source_target_pairs={{0,3},{3,0},{1,2},{2,1},{4,7},{7,4},{5,6},{6,5},{8,11},{11,8},{9,1... | collective-permute-start | bytes 786440 | tf_op jit(solution)/shard_map/ppermute | solution.py:824
  28.3 0.1 maximum_bitcast_fusion.frequency
  28.3 0.0 collective-permute-done.5.near
  28.3 5.9 %collective-permute-done.6.third = bf16[136,1024]{1,0:T(8,128)(2,1)S(1)} collective-permute-done((bf16[136,1024]{1,0:T(8,128)(2,1)S(1)}, bf16[136,1024]{1,0:T(8,128)(2,1)S(1)}, u32[]{:S(2)}, u32[]{:S(2)}) %collective-permute-start.6) | collective-permute-done | bytes 278560 | tf_op jit(solution)/shard_map/ppermute | solution.py:824
  34.2 1.6 %finish_keys.1 = (bf16[64,1024]{1,0:T(8,128)(2,1)S(1)}, bf16[64,1024]{1,0:T(8,128)(2,1)S(1)}, bf16[64,1024]{1,0:T(8,128)(2,1)S(1)}, bf16[64,1024]{1,0:T(8,128)(2...) custom-call(s32[3,8]{1,0:T(4,128)S(1)} %bitcast.14, ...), custom_call_target="tpu_custom_call" | custom-call | flops 1 | bytes 1 | tf_op jit(solution)/shard_map/finish_keys/pallas_call | solution.py:622
  35.9 0.1 collective-permute-start.7
  35.9 1.6 %collective-permute-start.8 = (bf16[64,1024]{1,0:T(8,128)(2,1)S(1)}, bf16[64,1024]{1,0:T(8,128)(2,1)S(1)}, u32[]{:S(2)}, u32[]{:S(2)}) collective-permute-start(bf16[64,1024]{1,0:T(8,128)(2,1)S(1)} %get-tuple-element.68), channel_id=1, source_target_pairs={{0,8},{4,12},{8,0},{12,4},{1,9},{5,13},{9,1},{13,5},{2,10},{6,14},... | collective-permute-start | bytes 393224 | tf_op jit(solution)/shard_map/ppermute | solution.py:827
  37.5 0.3 collective-permute-start.9
  37.8 0.0 copy-done.2
  37.8 6.0 %kept.1 = (bf16[144,128]{1,0:T(8,128)(2,1)S(1)}, bf16[144,128]{1,0:T(8,128)(2,1)S(1)}, bf16[144,128]{1,0:T(8,128)(2,1)S(1)}, bf16[144,128]{1,0:T(8,128)(2,1)S(1)}, bf16[16,64,2048]{2,1,0:T(8,128)(2,1)}) custom-call(s32[3,8]{1,0:T(4,128)S(1)} %bitcast.15, s32[2,8]{1,0:T(2,128)S(1)} %bitcast.17, s32[8]{0:T(128)S(1)} %copy-done.2, ...), custom_call_target="tpu_custom_call" | custom-call | flops 1 | bytes 1 | tf_op jit(solution)/shard_map/kept/pallas_call | solution.py:501
  43.8 0.0 collective-permute-done.10.near
  43.8 0.5 collective-permute-done.11.third
  44.3 0.0 collective-permute-done.7.rest_4_.rest_1_
  44.3 0.0 collective-permute-done.8.rest_5_.rest_2_
  44.3 0.0 collective-permute-done.9.rest_6_.rest_3_
  44.3 0.5 finish_values.1
  44.8 1.7 %collective-permute-start.12 = (bf16[176,128]{1,0:T(8,128)(2,1)S(1)}, bf16[176,128]{1,0:T(8,128)(2,1)S(1)}, u32[]{:S(2)}, u32[]{:S(2)}) collective-permute-start(bf16[176,128]{1,0:T(8,128)(2,1)S(1)} %get-tuple-element.83), channel_id=1, source_target_pairs={{0,2},{1,3},{2,0},{3,1},{4,6},{5,7},{6,4},{7,5},{8,10},{9,11},{10,... | collective-permute-start | bytes 135176 | tf_op jit(solution)/shard_map/ppermute | solution.py:824
  46.5 0.9 %collective-permute-start.13 = (bf16[176,128]{1,0:T(8,128)(2,1)S(1)}, bf16[176,128]{1,0:T(8,128)(2,1)S(1)}, u32[]{:S(2)}, u32[]{:S(2)}) collective-permute-start(bf16[176,128]{1,0:T(8,128)(2,1)S(1)} %get-tuple-element.84), channel_id=1, source_target_pairs={{0,3},{1,2},{2,1},{3,0},{4,7},{5,6},{6,5},{7,4},{8,11},{9,10},{10,... | collective-permute-start | bytes 135176 | tf_op jit(solution)/shard_map/ppermute | solution.py:824
  47.4 1.0 %collective-permute-start.14 = (bf16[176,128]{1,0:T(8,128)(2,1)S(1)}, bf16[176,128]{1,0:T(8,128)(2,1)S(1)}, u32[]{:S(2)}, u32[]{:S(2)}) collective-permute-start(bf16[176,128]{1,0:T(8,128)(2,1)S(1)} %get-tuple-element.85), channel_id=1, source_target_pairs={{0,1},{1,0},{2,3},{3,2},{4,5},{5,4},{6,7},{7,6},{8,9},{9,8},{10,11... | collective-permute-start | bytes 135176 | tf_op jit(solution)/shard_map/ppermute | solution.py:824
  48.4 1.5 %collective-permute-start.16 = (bf16[64,1024]{1,0:T(8,128)(2,1)S(1)}, bf16[64,1024]{1,0:T(8,128)(2,1)S(1)}, u32[]{:S(2)}, u32[]{:S(2)}) collective-permute-start(bf16[64,1024]{1,0:T(8,128)(2,1)S(1)} %get-tuple-element.88), channel_id=1, source_target_pairs={{0,8},{4,12},{8,0},{12,4},{1,9},{5,13},{9,1},{13,5},{2,10},{6,14},... | collective-permute-start | bytes 393224 | tf_op jit(solution)/shard_map/ppermute | solution.py:827
  49.9 0.0 collective-permute-start.17
  49.9 0.5 collective-permute-done.12.refs_1_
  50.3 2.0 %collective-permute-done.13.refs_2_ = bf16[176,128]{1,0:T(8,128)(2,1)S(1)} collective-permute-done((bf16[176,128]{1,0:T(8,128)(2,1)S(1)}, bf16[176,128]{1,0:T(8,128)(2,1)S(1)}, u32[]{:S(2)}, u32[]{:S(2)}) %collective-permute-start.13) | collective-permute-done | bytes 45088 | tf_op jit(solution)/shard_map/ppermute | solution.py:824
  52.3 0.0 collective-permute-done.14.refs_3_
  52.3 0.2 gather_parts.1
  52.5 0.1 collective-permute-start.15
  52.6 1.5 %collective-permute-start.18 = (bf16[16,256]{1,0:T(8,128)(2,1)S(1)}, bf16[16,256]{1,0:T(8,128)(2,1)S(1)}, u32[]{:S(2)}, u32[]{:S(2)}) collective-permute-start(bf16[16,256]{1,0:T(8,128)(2,1)S(1)} %get-tuple-element.94), channel_id=1, source_target_pairs={{0,8},{4,12},{8,0},{12,4},{1,9},{5,13},{9,1},{13,5},{2,10},{6,14},... | collective-permute-start | bytes 24584 | tf_op jit(solution)/shard_map/ppermute | solution.py:827
  54.1 0.3 collective-permute-start.19
  54.4 0.0 collective-permute-done.16.rest_6_
  54.4 0.3 collective-permute-start.20
  54.8 0.2 blend_kept.1
  55.0 0.7 %collective-permute-done.17.rest_7_ = bf16[64,1024]{1,0:T(8,128)(2,1)S(1)} collective-permute-done((bf16[64,1024]{1,0:T(8,128)(2,1)S(1)}, bf16[64,1024]{1,0:T(8,128)(2,1)S(1)}, u32[]{:S(2)}, u32[]{:S(2)}) %collective-permute-start.17) | collective-permute-done | bytes 131104 | tf_op jit(solution)/shard_map/ppermute | solution.py:827
  55.6 0.0 collective-permute-done.15.rest_5_
  55.6 1.1 %place_pages.1 = (bf16[16,64,2048]{2,1,0:T(8,128)(2,1)}, bf16[16,128]{1,0:T(8,128)(2,1)S(1)}) custom-call(s32[8,128]{1,0:T(8,128)S(1)} %get-tuple-element.54.places, bf16[16,64,2048]{2,1,0:T(8,128)(2,1)} %get-tuple-element.63.pool, bf16[64,1024]{1,0:T(8,128)(2,1)S(1)} %get-tuple-element.66.rest_0_, ...), custom_call_target="tpu_custom_call", output_to_operand_aliasing={{0}: (1, {})} | custom-call | flops 1 | bytes 1 | tf_op jit(solution)/shard_map/place_pages/pallas_call | solution.py:687
  56.8 0.0 collective-permute-done.18.refs_1_
  56.8 0.4 collective-permute-done.19.refs_2_
  57.2 0.0 collective-permute-done.20.refs_3_
  57.2 0.8 %combine.1 = bf16[8,2048]{1,0:T(8,128)(2,1)} custom-call(f32[40,128]{1,0:T(8,128)S(1)} %get-tuple-element.70.marks, f32[128,128]{1,0:T(8,128)S(1)} %get-tuple-element.92.kept_out, f32[128,128]{1,0:T(8,128)S(1)} %get-tuple-element.93.kept_level, bf16[16,256]{1,0:T(8,128)(2,1)S(1)} %get-tuple-element.91.refs_4_.refs_0_, ...), custom_call_target="tpu_custom_call" | custom-call | flops 1 | bytes 1 | tf_op jit(solution)/shard_map/combine/pallas_call | solution.py:793
  (2 shorter events, 0.0 us)
Async XLA Ops:
  3.6 11.1 %collective-permute-start = (bf16[136,1024]{1,0:T(8,128)(2,1)S(1)}, bf16[136,1024]{1,0:T(8,128)(2,1)S(1)}, u32[]{:S(2)}, u32[]{:S(2)}) collective-permute-start(bf16[136,1024]{1,0:T(8,128)(2,1)S(1)} %get-tuple-element.53), channel_id=1, source_target_pairs={{0,1},{3,2},{1,3},{2,0},{4,5},{7,6},{5,7},{6,4},{8,9},{11,10},{9,1... | collective-permute-start | bytes 835592 | tf_op jit(solution)/shard_map/ppermute | solution.py:824
  6.6 12.7 %copy-start.3 = (bf16[8,8192]{1,0:T(8,128)(2,1)S(1)}, bf16[8,8192]{1,0:T(8,128)(2,1)}, u32[]{:S(2)}) copy-start(bf16[8,8192]{1,0:T(8,128)(2,1)} %param.14) | copy-start | bytes 393220
  6.6 12.8 %copy-start = (s32[8,3]{0,1:T(4,128)S(1)}, s32[8,3]{0,1:T(4,128)}, u32[]{:S(2)}) copy-start(s32[8,3]{0,1:T(4,128)} %param.11) | copy-start | bytes 292
  6.6 12.8 %copy-start.1 = (s32[8,2,1]{0,2,1:T(1,128)S(1)}, s32[8,2,1]{0,2,1:T(1,128)}, u32[]{:S(2)}) copy-start(s32[8,2,1]{0,2,1:T(1,128)} %param.12) | copy-start | bytes 196
  10.8 10.9 %collective-permute-start.1 = (bf16[128,1024]{1,0:T(8,128)(2,1)S(1)}, bf16[128,1024]{1,0:T(8,128)(2,1)S(1)}, u32[]{:S(2)}, u32[]{:S(2)}) collective-permute-start(bf16[128,1024]{1,0:T(8,128)(2,1)S(1)} %get-tuple-element.58), channel_id=1, source_target_pairs={{0,1},{3,2},{1,3},{2,0},{4,5},{7,6},{5,7},{6,4},{8,9},{11,10},{9,1... | collective-permute-start | bytes 786440 | tf_op jit(solution)/shard_map/ppermute | solution.py:824
  13.4 14.9 %collective-permute-start.5 = (bf16[136,1024]{1,0:T(8,128)(2,1)S(1)}, bf16[136,1024]{1,0:T(8,128)(2,1)S(1)}, u32[]{:S(2)}, u32[]{:S(2)}) collective-permute-start(bf16[136,1024]{1,0:T(8,128)(2,1)S(1)} %get-tuple-element.65), channel_id=1, source_target_pairs={{0,1},{1,0},{2,3},{3,2},{4,5},{5,4},{6,7},{7,6},{8,9},{9,8},{10,11... | collective-permute-start | bytes 835592 | tf_op jit(solution)/shard_map/ppermute | solution.py:824
  14.8 19.5 %collective-permute-start.6 = (bf16[136,1024]{1,0:T(8,128)(2,1)S(1)}, bf16[136,1024]{1,0:T(8,128)(2,1)S(1)}, u32[]{:S(2)}, u32[]{:S(2)}) collective-permute-start(bf16[136,1024]{1,0:T(8,128)(2,1)S(1)} %carry.2.rest_0_), channel_id=1, source_target_pairs={{0,3},{3,0},{1,2},{2,1},{4,7},{7,4},{5,6},{6,5},{8,11},{11,8},{9,1... | collective-permute-start | bytes 835592 | tf_op jit(solution)/shard_map/ppermute | solution.py:824
  19.4 18.4 %copy-start.2 = (s32[8]{0:T(128)S(1)}, s32[8]{0:T(128)}, u32[]{:S(2)}) copy-start(s32[8]{0:T(128)} %lengths.1) | copy-start | bytes 100
  20.1 3.7 %collective-permute-start.2 = (bf16[64,128]{1,0:T(8,128)(2,1)S(1)}, bf16[64,128]{1,0:T(8,128)(2,1)S(1)}, u32[]{:S(2)}, u32[]{:S(2)}) collective-permute-start(bf16[64,128]{1,0:T(8,128)(2,1)S(1)} %get-tuple-element.60), channel_id=1, source_target_pairs={{0,4},{4,0},{8,12},{12,8},{1,5},{5,1},{9,13},{13,9},{2,6},{6,2},{1... | collective-permute-start | bytes 49160 | tf_op jit(solution)/shard_map/ppermute | solution.py:827
  20.2 4.4 %collective-permute-start.3 = (bf16[64,128]{1,0:T(8,128)(2,1)S(1)}, bf16[64,128]{1,0:T(8,128)(2,1)S(1)}, u32[]{:S(2)}, u32[]{:S(2)}) collective-permute-start(bf16[64,128]{1,0:T(8,128)(2,1)S(1)} %get-tuple-element.61), channel_id=1, source_target_pairs={{0,8},{4,12},{8,0},{12,4},{1,9},{5,13},{9,1},{13,5},{2,10},{6,14},... | collective-permute-start | bytes 49160 | tf_op jit(solution)/shard_map/ppermute | solution.py:827
  21.7 3.2 %collective-permute-start.4 = (bf16[64,128]{1,0:T(8,128)(2,1)S(1)}, bf16[64,128]{1,0:T(8,128)(2,1)S(1)}, u32[]{:S(2)}, u32[]{:S(2)}) collective-permute-start(bf16[64,128]{1,0:T(8,128)(2,1)S(1)} %get-tuple-element.62), channel_id=1, source_target_pairs={{0,12},{4,8},{8,4},{12,0},{1,13},{5,9},{9,5},{13,1},{2,14},{6,10},... | collective-permute-start | bytes 49160 | tf_op jit(solution)/shard_map/ppermute | solution.py:827
  23.8 20.0 %collective-permute-start.10 = (bf16[128,1024]{1,0:T(8,128)(2,1)S(1)}, bf16[128,1024]{1,0:T(8,128)(2,1)S(1)}, u32[]{:S(2)}, u32[]{:S(2)}) collective-permute-start(bf16[128,1024]{1,0:T(8,128)(2,1)S(1)} %get-tuple-element.72), channel_id=1, source_target_pairs={{0,1},{1,0},{2,3},{3,2},{4,5},{5,4},{6,7},{7,6},{8,9},{9,8},{10,11... | collective-permute-start | bytes 786440 | tf_op jit(solution)/shard_map/ppermute | solution.py:824
  25.0 19.4 %collective-permute-start.11 = (bf16[128,1024]{1,0:T(8,128)(2,1)S(1)}, bf16[128,1024]{1,0:T(8,128)(2,1)S(1)}, u32[]{:S(2)}, u32[]{:S(2)}) collective-permute-start(bf16[128,1024]{1,0:T(8,128)(2,1)S(1)} %carry.3.rest_0_), channel_id=1, source_target_pairs={{0,3},{3,0},{1,2},{2,1},{4,7},{7,4},{5,6},{6,5},{8,11},{11,8},{9,1... | collective-permute-start | bytes 786440 | tf_op jit(solution)/shard_map/ppermute | solution.py:824
  35.9 8.5 %collective-permute-start.7 = (bf16[64,1024]{1,0:T(8,128)(2,1)S(1)}, bf16[64,1024]{1,0:T(8,128)(2,1)S(1)}, u32[]{:S(2)}, u32[]{:S(2)}) collective-permute-start(bf16[64,1024]{1,0:T(8,128)(2,1)S(1)} %get-tuple-element.67), channel_id=1, source_target_pairs={{0,4},{4,0},{8,12},{12,8},{1,5},{5,1},{9,13},{13,9},{2,6},{6,2},{1... | collective-permute-start | bytes 393224 | tf_op jit(solution)/shard_map/ppermute | solution.py:827
  35.9 8.4 %collective-permute-start.8 = (bf16[64,1024]{1,0:T(8,128)(2,1)S(1)}, bf16[64,1024]{1,0:T(8,128)(2,1)S(1)}, u32[]{:S(2)}, u32[]{:S(2)}) collective-permute-start(bf16[64,1024]{1,0:T(8,128)(2,1)S(1)} %get-tuple-element.68), channel_id=1, source_target_pairs={{0,8},{4,12},{8,0},{12,4},{1,9},{5,13},{9,1},{13,5},{2,10},{6,14},... | collective-permute-start | bytes 393224 | tf_op jit(solution)/shard_map/ppermute | solution.py:827
  37.5 6.8 %collective-permute-start.9 = (bf16[64,1024]{1,0:T(8,128)(2,1)S(1)}, bf16[64,1024]{1,0:T(8,128)(2,1)S(1)}, u32[]{:S(2)}, u32[]{:S(2)}) collective-permute-start(bf16[64,1024]{1,0:T(8,128)(2,1)S(1)} %get-tuple-element.69), channel_id=1, source_target_pairs={{0,12},{4,8},{8,4},{12,0},{1,13},{5,9},{9,5},{13,1},{2,14},{6,10},... | collective-permute-start | bytes 393224 | tf_op jit(solution)/shard_map/ppermute | solution.py:827
  44.8 5.5 %collective-permute-start.12 = (bf16[176,128]{1,0:T(8,128)(2,1)S(1)}, bf16[176,128]{1,0:T(8,128)(2,1)S(1)}, u32[]{:S(2)}, u32[]{:S(2)}) collective-permute-start(bf16[176,128]{1,0:T(8,128)(2,1)S(1)} %get-tuple-element.83), channel_id=1, source_target_pairs={{0,2},{1,3},{2,0},{3,1},{4,6},{5,7},{6,4},{7,5},{8,10},{9,11},{10,... | collective-permute-start | bytes 135176 | tf_op jit(solution)/shard_map/ppermute | solution.py:824
  46.5 5.8 %collective-permute-start.13 = (bf16[176,128]{1,0:T(8,128)(2,1)S(1)}, bf16[176,128]{1,0:T(8,128)(2,1)S(1)}, u32[]{:S(2)}, u32[]{:S(2)}) collective-permute-start(bf16[176,128]{1,0:T(8,128)(2,1)S(1)} %get-tuple-element.84), channel_id=1, source_target_pairs={{0,3},{1,2},{2,1},{3,0},{4,7},{5,6},{6,5},{7,4},{8,11},{9,10},{10,... | collective-permute-start | bytes 135176 | tf_op jit(solution)/shard_map/ppermute | solution.py:824
  47.4 4.9 %collective-permute-start.14 = (bf16[176,128]{1,0:T(8,128)(2,1)S(1)}, bf16[176,128]{1,0:T(8,128)(2,1)S(1)}, u32[]{:S(2)}, u32[]{:S(2)}) collective-permute-start(bf16[176,128]{1,0:T(8,128)(2,1)S(1)} %get-tuple-element.85), channel_id=1, source_target_pairs={{0,1},{1,0},{2,3},{3,2},{4,5},{5,4},{6,7},{7,6},{8,9},{9,8},{10,11... | collective-permute-start | bytes 135176 | tf_op jit(solution)/shard_map/ppermute | solution.py:824
  48.4 6.1 %collective-permute-start.16 = (bf16[64,1024]{1,0:T(8,128)(2,1)S(1)}, bf16[64,1024]{1,0:T(8,128)(2,1)S(1)}, u32[]{:S(2)}, u32[]{:S(2)}) collective-permute-start(bf16[64,1024]{1,0:T(8,128)(2,1)S(1)} %get-tuple-element.88), channel_id=1, source_target_pairs={{0,8},{4,12},{8,0},{12,4},{1,9},{5,13},{9,1},{13,5},{2,10},{6,14},... | collective-permute-start | bytes 393224 | tf_op jit(solution)/shard_map/ppermute | solution.py:827
  49.9 5.8 %collective-permute-start.17 = (bf16[64,1024]{1,0:T(8,128)(2,1)S(1)}, bf16[64,1024]{1,0:T(8,128)(2,1)S(1)}, u32[]{:S(2)}, u32[]{:S(2)}) collective-permute-start(bf16[64,1024]{1,0:T(8,128)(2,1)S(1)} %get-tuple-element.89), channel_id=1, source_target_pairs={{0,12},{4,8},{8,4},{12,0},{1,13},{5,9},{9,5},{13,1},{2,14},{6,10},... | collective-permute-start | bytes 393224 | tf_op jit(solution)/shard_map/ppermute | solution.py:827
  52.5 3.2 %collective-permute-start.15 = (bf16[64,1024]{1,0:T(8,128)(2,1)S(1)}, bf16[64,1024]{1,0:T(8,128)(2,1)S(1)}, u32[]{:S(2)}, u32[]{:S(2)}) collective-permute-start(bf16[64,1024]{1,0:T(8,128)(2,1)S(1)} %get-tuple-element.87), channel_id=1, source_target_pairs={{0,4},{4,0},{8,12},{12,8},{1,5},{5,1},{9,13},{13,9},{2,6},{6,2},{1... | collective-permute-start | bytes 393224 | tf_op jit(solution)/shard_map/ppermute | solution.py:827
  52.6 4.2 %collective-permute-start.18 = (bf16[16,256]{1,0:T(8,128)(2,1)S(1)}, bf16[16,256]{1,0:T(8,128)(2,1)S(1)}, u32[]{:S(2)}, u32[]{:S(2)}) collective-permute-start(bf16[16,256]{1,0:T(8,128)(2,1)S(1)} %get-tuple-element.94), channel_id=1, source_target_pairs={{0,8},{4,12},{8,0},{12,4},{1,9},{5,13},{9,1},{13,5},{2,10},{6,14},... | collective-permute-start | bytes 24584 | tf_op jit(solution)/shard_map/ppermute | solution.py:827
  54.1 3.1 %collective-permute-start.19 = (bf16[16,256]{1,0:T(8,128)(2,1)S(1)}, bf16[16,256]{1,0:T(8,128)(2,1)S(1)}, u32[]{:S(2)}, u32[]{:S(2)}) collective-permute-start(bf16[16,256]{1,0:T(8,128)(2,1)S(1)} %get-tuple-element.95), channel_id=1, source_target_pairs={{0,12},{4,8},{8,4},{12,0},{1,13},{5,9},{9,5},{13,1},{2,14},{6,10},... | collective-permute-start | bytes 24584 | tf_op jit(solution)/shard_map/ppermute | solution.py:827
  54.4 2.8 %collective-permute-start.20 = (bf16[16,256]{1,0:T(8,128)(2,1)S(1)}, bf16[16,256]{1,0:T(8,128)(2,1)S(1)}, u32[]{:S(2)}, u32[]{:S(2)}) collective-permute-start(bf16[16,256]{1,0:T(8,128)(2,1)S(1)} %get-tuple-element.96), channel_id=1, source_target_pairs={{0,4},{4,0},{8,12},{12,8},{1,5},{5,1},{9,13},{13,9},{2,6},{6,2},{1... | collective-permute-start | bytes 24584 | tf_op jit(solution)/shard_map/ppermute | solution.py:827

commit v7 on v6

--- a/solution.py
+++ b/solution.py
@@ -321,12 +321,12 @@
     for copy in rows_here:
         copy.wait()
     scale_rows(rows_in, gained, gain_in, slice(None))
+    product = jnp.dot(gained[...], key_tile[...], preferred_element_type=F32).astype(BF16)
+    for place, ref in enumerate((own, near, third)):
+        ref[:rows] = product[place * rows : (place + 1) * rows]
     for place, ref in enumerate((own, near, third)):
         span = slice(place * rows, (place + 1) * rows)
         put_squares(rows_in, span, ref, 2 if place == 2 else 0)
-    product = jnp.dot(gained[...], key_tile[...], preferred_element_type=F32).astype(BF16)
-    for place, ref in enumerate((own, near, third)):
-        ref[:rows] = product[place * rows : (place + 1) * rows]
     tile_copy.wait()
     values[...] = jnp.dot(sent[...], value_tile[...], preferred_element_type=F32).astype(BF16)
 

time: 58.1 us -> 58.1 us (level)
  no operation moved by 1% of the time
where the time goes in v7:
time: 58.1 us; the launch traced here: 58 us
  starting transfers between devices  25.9 us (45%)
  Pallas kernels  20 us (34%)
  waiting for transfers between devices  11.2 us (19%)
  between operations  0.81 us (1%)
    ppermute x9, starting transfers between devices, along(): return lax.ppermute(array, 'shard', pairs)  18.3 us
    ppermute x9, waiting for transfers between devices, along(): return lax.ppermute(array, 'shard', pairs)  9.64 us
    ppermute x12, starting transfers between devices, across(): return lax.ppermute(array, 'rep', [(i, i ^ step) for i in range(replicas)])  7.63 us
    pallas_call x1, Pallas kernels, kept(): pl.pallas_call(functools.partial(kept_kernel, shards=shards, after=len(af...  6 us
    pallas_call x1, Pallas kernels, project_keys(): pl.pallas_call(project_keys_kernel, in_specs=[whole(pl.ANY)] * 3 + [whole...  4.14 us
    pallas_call x1, Pallas kernels, project_first(): pl.pallas_call(first_kernel, in_specs=[whole(pl.ANY)] * 3, out_specs=[who...  2.95 us
    pallas_call x1, Pallas kernels, project_values(): pl.pallas_call(project_values_kernel, in_specs=[whole()] * 2 + [whole(pl....  1.78 us
    pallas_call x1, Pallas kernels, finish_keys(): pl.pallas_call(functools.partial(finish_keys_kernel, stripe=stripe), in_s...  1.62 us
  transfers between devices with their start and end apart: 21, of which 8 were waited for; matrix products, arithmetic and copies ran while one was open for 0% of the time, Pallas kernels for 27%

profile of v7, /device:TPU:0, one launch (start us, length us, event | category | flops | bytes accessed | tf_op | source)
XLA Modules:
  0.0 58.0 jit_solution(17011114848588127921)
XLA Ops:
  0.6 3.0 %project_first.1 = (bf16[136,1024]{1,0:T(8,128)(2,1)S(1)}, bf16[128,2048]{1,0:T(8,128)(2,1)S(1)}, bf16[2048,1024]{1,0:T(8,128)(2,1)S(1)}) custom-call(bf16[2,4,64,2048]{3,2,1,0:T(8,128)(2,1)} %bitcast.18, bf16[2048]{0:T(1024)(128)(2,1)} %gain.3, bf16[2048,2048]{1,0:T(8,128)(2,1)} %weight.3), custom_call_target="tpu_custom_call" | custom-call | flops 1 | bytes 1 | tf_op jit(solution)/shard_map/project_first/pallas_call | solution.py:236
  3.6 3.1 %collective-permute-start = (bf16[136,1024]{1,0:T(8,128)(2,1)S(1)}, bf16[136,1024]{1,0:T(8,128)(2,1)S(1)}, u32[]{:S(2)}, u32[]{:S(2)}) collective-permute-start(bf16[136,1024]{1,0:T(8,128)(2,1)S(1)} %get-tuple-element.53), channel_id=1, source_target_pairs={{0,1},{3,2},{1,3},{2,0},{4,5},{7,6},{5,7},{6,4},{8,9},{11,10},{9,1... | collective-permute-start | bytes 835592 | tf_op jit(solution)/shard_map/ppermute | solution.py:824
  6.6 0.0 copy-start.3
  6.6 0.0 copy-start
  6.6 0.0 copy-start.1
  6.6 4.1 %project_keys.1 = (bf16[136,1024]{1,0:T(8,128)(2,1)S(1)}, bf16[136,1024]{1,0:T(8,128)(2,1)S(1)}, bf16[136,1024]{1,0:T(8,128)(2,1)S(1)}, bf16[128,1024]{1,0:T(8,1...) custom-call(bf16[2,4,64,2048]{3,2,1,0:T(8,128)(2,1)} %bitcast.19, bf16[2048]{0:T(1024)(128)(2,1)} %gain.3, ...), custom_call_target="tpu_custom_call" | custom-call | flops 1 | bytes 1 | tf_op jit(solution)/shard_map/project_keys/pallas_call | solution.py:338
  10.8 2.6 %collective-permute-start.1 = (bf16[128,1024]{1,0:T(8,128)(2,1)S(1)}, bf16[128,1024]{1,0:T(8,128)(2,1)S(1)}, u32[]{:S(2)}, u32[]{:S(2)}) collective-permute-start(bf16[128,1024]{1,0:T(8,128)(2,1)S(1)} %get-tuple-element.58), channel_id=1, source_target_pairs={{0,1},{3,2},{1,3},{2,0},{4,5},{7,6},{5,7},{6,4},{8,9},{11,10},{9,1... | collective-permute-start | bytes 786440 | tf_op jit(solution)/shard_map/ppermute | solution.py:824
  13.4 0.4 collective-permute-start.5
  13.9 0.8 %collective-permute-done.first = bf16[136,1024]{1,0:T(8,128)(2,1)S(1)} collective-permute-done((bf16[136,1024]{1,0:T(8,128)(2,1)S(1)}, bf16[136,1024]{1,0:T(8,128)(2,1)S(1)}, u32[]{:S(2)}, u32[]{:S(2)}) %collective-permute-start) | collective-permute-done | bytes 278560 | tf_op jit(solution)/shard_map/ppermute | solution.py:824
  14.7 0.1 carry.2.rest_0_
  14.8 4.6 %collective-permute-start.6 = (bf16[136,1024]{1,0:T(8,128)(2,1)S(1)}, bf16[136,1024]{1,0:T(8,128)(2,1)S(1)}, u32[]{:S(2)}, u32[]{:S(2)}) collective-permute-start(bf16[136,1024]{1,0:T(8,128)(2,1)S(1)} %carry.2.rest_0_), channel_id=1, source_target_pairs={{0,3},{3,0},{1,2},{2,1},{4,7},{7,4},{5,6},{6,5},{8,11},{11,8},{9,1... | collective-permute-start | bytes 835592 | tf_op jit(solution)/shard_map/ppermute | solution.py:824
  19.4 0.0 copy-done.3
  19.4 0.0 copy-done
  19.4 0.0 copy-done.1
  19.4 0.0 copy-start.2
  19.4 0.6 %ask.1 = (bf16[64,128]{1,0:T(8,128)(2,1)S(1)}, bf16[64,128]{1,0:T(8,128)(2,1)S(1)}, bf16[64,128]{1,0:T(8,128)(2,1)S(1)}, bf16[64,128]{1,0:T(8,128)(2,1)S(1)}, f3...) custom-call(s32[3,8]{1,0:T(4,128)S(1)} %bitcast.13, s32[2,8]{1,0:T(2,128)S(1)} %bitcast.16, bf16[8,64,128]{2,1,0:T(8,128)(2,1)S(1)} %bitcast.11, ...), custom_call_target="tpu_custom_call" | custom-call | flops 1 | bytes 1 | tf_op jit(solution)/shard_map/ask/pallas_call | solution.py:422
  20.1 0.1 collective-permute-start.2
  20.2 1.5 %collective-permute-start.3 = (bf16[64,128]{1,0:T(8,128)(2,1)S(1)}, bf16[64,128]{1,0:T(8,128)(2,1)S(1)}, u32[]{:S(2)}, u32[]{:S(2)}) collective-permute-start(bf16[64,128]{1,0:T(8,128)(2,1)S(1)} %get-tuple-element.61), channel_id=1, source_target_pairs={{0,8},{4,12},{8,0},{12,4},{1,9},{5,13},{9,1},{13,5},{2,10},{6,14},... | collective-permute-start | bytes 49160 | tf_op jit(solution)/shard_map/ppermute | solution.py:827
  21.7 0.0 collective-permute-done.1.rest_1_.first
  21.7 0.3 collective-permute-start.4
  22.0 1.8 %project_values.1 = (bf16[128,1024]{1,0:T(8,128)(2,1)S(1)}, bf16[128,1024]{1,0:T(8,128)(2,1)S(1)}, bf16[128,1024]{1,0:T(8,128)(2,1)S(1)}) custom-call(bf16[384,2048]{1,0:T(8,128)(2,1)S(1)} %get-tuple-element.55.gained, bf16[2048,1024]{1,0:T(8,128)(2,1)S(1)} %get-tuple-element.56.tile, bf16[64,128]{1,0:T(8,128)(2,1)S(1)} %get-tuple-element.57.rest_0_, ...), custom_call_target="tpu_custom_call" | custom-call | flops 1 | bytes 1 | tf_op jit(solution)/shard_map/project_values/pallas_call | solution.py:369
  23.8 0.0 collective-permute-done.2.rest_0_.rest_1_
  23.8 0.7 %collective-permute-start.10 = (bf16[128,1024]{1,0:T(8,128)(2,1)S(1)}, bf16[128,1024]{1,0:T(8,128)(2,1)S(1)}, u32[]{:S(2)}, u32[]{:S(2)}) collective-permute-start(bf16[128,1024]{1,0:T(8,128)(2,1)S(1)} %get-tuple-element.72), channel_id=1, source_target_pairs={{0,1},{1,0},{2,3},{3,2},{4,5},{5,4},{6,7},{7,6},{8,9},{9,8},{10,11... | collective-permute-start | bytes 786440 | tf_op jit(solution)/shard_map/ppermute | solution.py:824
  24.5 0.0 collective-permute-done.3.rest_1_.rest_2_
  24.5 0.3 collective-permute-done.4.rest_2_.rest_3_
  24.9 0.1 carry.3.rest_0_
  25.0 3.3 %collective-permute-start.11 = (bf16[128,1024]{1,0:T(8,128)(2,1)S(1)}, bf16[128,1024]{1,0:T(8,128)(2,1)S(1)}, u32[]{:S(2)}, u32[]{:S(2)}) collective-permute-start(bf16[128,1024]{1,0:T(8,128)(2,1)S(1)} %carry.3.rest_0_), channel_id=1, source_target_pairs={{0,3},{3,0},{1,2},{2,1},{4,7},{7,4},{5,6},{6,5},{8,11},{11,8},{9,1... | collective-permute-start | bytes 786440 | tf_op jit(solution)/shard_map/ppermute | solution.py:824
  28.3 0.1 maximum_bitcast_fusion.frequency
  28.3 0.0 collective-permute-done.5.near
  28.3 5.9 %collective-permute-done.6.third = bf16[136,1024]{1,0:T(8,128)(2,1)S(1)} collective-permute-done((bf16[136,1024]{1,0:T(8,128)(2,1)S(1)}, bf16[136,1024]{1,0:T(8,128)(2,1)S(1)}, u32[]{:S(2)}, u32[]{:S(2)}) %collective-permute-start.6) | collective-permute-done | bytes 278560 | tf_op jit(solution)/shard_map/ppermute | solution.py:824
  34.2 1.6 %finish_keys.1 = (bf16[64,1024]{1,0:T(8,128)(2,1)S(1)}, bf16[64,1024]{1,0:T(8,128)(2,1)S(1)}, bf16[64,1024]{1,0:T(8,128)(2,1)S(1)}, bf16[64,1024]{1,0:T(8,128)(2...) custom-call(s32[3,8]{1,0:T(4,128)S(1)} %bitcast.14, ...), custom_call_target="tpu_custom_call" | custom-call | flops 1 | bytes 1 | tf_op jit(solution)/shard_map/finish_keys/pallas_call | solution.py:622
  35.9 0.1 collective-permute-start.7
  35.9 1.6 %collective-permute-start.8 = (bf16[64,1024]{1,0:T(8,128)(2,1)S(1)}, bf16[64,1024]{1,0:T(8,128)(2,1)S(1)}, u32[]{:S(2)}, u32[]{:S(2)}) collective-permute-start(bf16[64,1024]{1,0:T(8,128)(2,1)S(1)} %get-tuple-element.68), channel_id=1, source_target_pairs={{0,8},{4,12},{8,0},{12,4},{1,9},{5,13},{9,1},{13,5},{2,10},{6,14},... | collective-permute-start | bytes 393224 | tf_op jit(solution)/shard_map/ppermute | solution.py:827
  37.5 0.3 collective-permute-start.9
  37.8 0.0 copy-done.2
  37.8 6.0 %kept.1 = (bf16[144,128]{1,0:T(8,128)(2,1)S(1)}, bf16[144,128]{1,0:T(8,128)(2,1)S(1)}, bf16[144,128]{1,0:T(8,128)(2,1)S(1)}, bf16[144,128]{1,0:T(8,128)(2,1)S(1)}, bf16[16,64,2048]{2,1,0:T(8,128)(2,1)}) custom-call(s32[3,8]{1,0:T(4,128)S(1)} %bitcast.15, s32[2,8]{1,0:T(2,128)S(1)} %bitcast.17, s32[8]{0:T(128)S(1)} %copy-done.2, ...), custom_call_target="tpu_custom_call" | custom-call | flops 1 | bytes 1 | tf_op jit(solution)/shard_map/kept/pallas_call | solution.py:501
  43.8 0.0 collective-permute-done.10.near
  43.8 0.5 collective-permute-done.11.third
  44.3 0.0 collective-permute-done.7.rest_4_.rest_1_
  44.3 0.0 collective-permute-done.8.rest_5_.rest_2_
  44.3 0.0 collective-permute-done.9.rest_6_.rest_3_
  44.3 0.5 finish_values.1
  44.8 1.7 %collective-permute-start.12 = (bf16[176,128]{1,0:T(8,128)(2,1)S(1)}, bf16[176,128]{1,0:T(8,128)(2,1)S(1)}, u32[]{:S(2)}, u32[]{:S(2)}) collective-permute-start(bf16[176,128]{1,0:T(8,128)(2,1)S(1)} %get-tuple-element.83), channel_id=1, source_target_pairs={{0,2},{1,3},{2,0},{3,1},{4,6},{5,7},{6,4},{7,5},{8,10},{9,11},{10,... | collective-permute-start | bytes 135176 | tf_op jit(solution)/shard_map/ppermute | solution.py:824
  46.5 0.9 %collective-permute-start.13 = (bf16[176,128]{1,0:T(8,128)(2,1)S(1)}, bf16[176,128]{1,0:T(8,128)(2,1)S(1)}, u32[]{:S(2)}, u32[]{:S(2)}) collective-permute-start(bf16[176,128]{1,0:T(8,128)(2,1)S(1)} %get-tuple-element.84), channel_id=1, source_target_pairs={{0,3},{1,2},{2,1},{3,0},{4,7},{5,6},{6,5},{7,4},{8,11},{9,10},{10,... | collective-permute-start | bytes 135176 | tf_op jit(solution)/shard_map/ppermute | solution.py:824
  47.4 1.0 %collective-permute-start.14 = (bf16[176,128]{1,0:T(8,128)(2,1)S(1)}, bf16[176,128]{1,0:T(8,128)(2,1)S(1)}, u32[]{:S(2)}, u32[]{:S(2)}) collective-permute-start(bf16[176,128]{1,0:T(8,128)(2,1)S(1)} %get-tuple-element.85), channel_id=1, source_target_pairs={{0,1},{1,0},{2,3},{3,2},{4,5},{5,4},{6,7},{7,6},{8,9},{9,8},{10,11... | collective-permute-start | bytes 135176 | tf_op jit(solution)/shard_map/ppermute | solution.py:824
  48.4 1.5 %collective-permute-start.16 = (bf16[64,1024]{1,0:T(8,128)(2,1)S(1)}, bf16[64,1024]{1,0:T(8,128)(2,1)S(1)}, u32[]{:S(2)}, u32[]{:S(2)}) collective-permute-start(bf16[64,1024]{1,0:T(8,128)(2,1)S(1)} %get-tuple-element.88), channel_id=1, source_target_pairs={{0,8},{4,12},{8,0},{12,4},{1,9},{5,13},{9,1},{13,5},{2,10},{6,14},... | collective-permute-start | bytes 393224 | tf_op jit(solution)/shard_map/ppermute | solution.py:827
  49.9 0.0 collective-permute-start.17
  49.9 0.5 collective-permute-done.12.refs_1_
  50.3 2.0 %collective-permute-done.13.refs_2_ = bf16[176,128]{1,0:T(8,128)(2,1)S(1)} collective-permute-done((bf16[176,128]{1,0:T(8,128)(2,1)S(1)}, bf16[176,128]{1,0:T(8,128)(2,1)S(1)}, u32[]{:S(2)}, u32[]{:S(2)}) %collective-permute-start.13) | collective-permute-done | bytes 45088 | tf_op jit(solution)/shard_map/ppermute | solution.py:824
  52.3 0.0 collective-permute-done.14.refs_3_
  52.3 0.2 gather_parts.1
  52.5 0.1 collective-permute-start.15
  52.6 1.5 %collective-permute-start.18 = (bf16[16,256]{1,0:T(8,128)(2,1)S(1)}, bf16[16,256]{1,0:T(8,128)(2,1)S(1)}, u32[]{:S(2)}, u32[]{:S(2)}) collective-permute-start(bf16[16,256]{1,0:T(8,128)(2,1)S(1)} %get-tuple-element.94), channel_id=1, source_target_pairs={{0,8},{4,12},{8,0},{12,4},{1,9},{5,13},{9,1},{13,5},{2,10},{6,14},... | collective-permute-start | bytes 24584 | tf_op jit(solution)/shard_map/ppermute | solution.py:827
  54.1 0.3 collective-permute-start.19
  54.4 0.0 collective-permute-done.16.rest_6_
  54.4 0.3 collective-permute-start.20
  54.8 0.2 blend_kept.1
  55.0 0.7 %collective-permute-done.17.rest_7_ = bf16[64,1024]{1,0:T(8,128)(2,1)S(1)} collective-permute-done((bf16[64,1024]{1,0:T(8,128)(2,1)S(1)}, bf16[64,1024]{1,0:T(8,128)(2,1)S(1)}, u32[]{:S(2)}, u32[]{:S(2)}) %collective-permute-start.17) | collective-permute-done | bytes 131104 | tf_op jit(solution)/shard_map/ppermute | solution.py:827
  55.6 0.0 collective-permute-done.15.rest_5_
  55.6 1.0 %place_pages.1 = (bf16[16,64,2048]{2,1,0:T(8,128)(2,1)}, bf16[16,128]{1,0:T(8,128)(2,1)S(1)}) custom-call(s32[8,128]{1,0:T(8,128)S(1)} %get-tuple-element.54.places, bf16[16,64,2048]{2,1,0:T(8,128)(2,1)} %get-tuple-element.63.pool, bf16[64,1024]{1,0:T(8,128)(2,1)S(1)} %get-tuple-element.66.rest_0_, ...), custom_call_target="tpu_custom_call", output_to_operand_aliasing={{0}: (1, {})} | custom-call | flops 1 | bytes 1 | tf_op jit(solution)/shard_map/place_pages/pallas_call | solution.py:687
  56.7 0.0 collective-permute-done.18.refs_1_
  56.7 0.5 collective-permute-done.19.refs_2_
  57.2 0.0 collective-permute-done.20.refs_3_
  57.2 0.8 %combine.1 = bf16[8,2048]{1,0:T(8,128)(2,1)} custom-call(f32[40,128]{1,0:T(8,128)S(1)} %get-tuple-element.70.marks, f32[128,128]{1,0:T(8,128)S(1)} %get-tuple-element.92.kept_out, f32[128,128]{1,0:T(8,128)S(1)} %get-tuple-element.93.kept_level, bf16[16,256]{1,0:T(8,128)(2,1)S(1)} %get-tuple-element.91.refs_4_.refs_0_, ...), custom_call_target="tpu_custom_call" | custom-call | flops 1 | bytes 1 | tf_op jit(solution)/shard_map/combine/pallas_call | solution.py:793
  (2 shorter events, 0.0 us)
Async XLA Ops:
  3.6 11.1 %collective-permute-start = (bf16[136,1024]{1,0:T(8,128)(2,1)S(1)}, bf16[136,1024]{1,0:T(8,128)(2,1)S(1)}, u32[]{:S(2)}, u32[]{:S(2)}) collective-permute-start(bf16[136,1024]{1,0:T(8,128)(2,1)S(1)} %get-tuple-element.53), channel_id=1, source_target_pairs={{0,1},{3,2},{1,3},{2,0},{4,5},{7,6},{5,7},{6,4},{8,9},{11,10},{9,1... | collective-permute-start | bytes 835592 | tf_op jit(solution)/shard_map/ppermute | solution.py:824
  6.6 12.7 %copy-start.3 = (bf16[8,8192]{1,0:T(8,128)(2,1)S(1)}, bf16[8,8192]{1,0:T(8,128)(2,1)}, u32[]{:S(2)}) copy-start(bf16[8,8192]{1,0:T(8,128)(2,1)} %param.14) | copy-start | bytes 393220
  6.6 12.8 %copy-start = (s32[8,3]{0,1:T(4,128)S(1)}, s32[8,3]{0,1:T(4,128)}, u32[]{:S(2)}) copy-start(s32[8,3]{0,1:T(4,128)} %param.11) | copy-start | bytes 292
  6.6 12.8 %copy-start.1 = (s32[8,2,1]{0,2,1:T(1,128)S(1)}, s32[8,2,1]{0,2,1:T(1,128)}, u32[]{:S(2)}) copy-start(s32[8,2,1]{0,2,1:T(1,128)} %param.12) | copy-start | bytes 196
  10.8 10.9 %collective-permute-start.1 = (bf16[128,1024]{1,0:T(8,128)(2,1)S(1)}, bf16[128,1024]{1,0:T(8,128)(2,1)S(1)}, u32[]{:S(2)}, u32[]{:S(2)}) collective-permute-start(bf16[128,1024]{1,0:T(8,128)(2,1)S(1)} %get-tuple-element.58), channel_id=1, source_target_pairs={{0,1},{3,2},{1,3},{2,0},{4,5},{7,6},{5,7},{6,4},{8,9},{11,10},{9,1... | collective-permute-start | bytes 786440 | tf_op jit(solution)/shard_map/ppermute | solution.py:824
  13.4 14.9 %collective-permute-start.5 = (bf16[136,1024]{1,0:T(8,128)(2,1)S(1)}, bf16[136,1024]{1,0:T(8,128)(2,1)S(1)}, u32[]{:S(2)}, u32[]{:S(2)}) collective-permute-start(bf16[136,1024]{1,0:T(8,128)(2,1)S(1)} %get-tuple-element.65), channel_id=1, source_target_pairs={{0,1},{1,0},{2,3},{3,2},{4,5},{5,4},{6,7},{7,6},{8,9},{9,8},{10,11... | collective-permute-start | bytes 835592 | tf_op jit(solution)/shard_map/ppermute | solution.py:824
  14.8 19.5 %collective-permute-start.6 = (bf16[136,1024]{1,0:T(8,128)(2,1)S(1)}, bf16[136,1024]{1,0:T(8,128)(2,1)S(1)}, u32[]{:S(2)}, u32[]{:S(2)}) collective-permute-start(bf16[136,1024]{1,0:T(8,128)(2,1)S(1)} %carry.2.rest_0_), channel_id=1, source_target_pairs={{0,3},{3,0},{1,2},{2,1},{4,7},{7,4},{5,6},{6,5},{8,11},{11,8},{9,1... | collective-permute-start | bytes 835592 | tf_op jit(solution)/shard_map/ppermute | solution.py:824
  19.4 18.4 %copy-start.2 = (s32[8]{0:T(128)S(1)}, s32[8]{0:T(128)}, u32[]{:S(2)}) copy-start(s32[8]{0:T(128)} %lengths.1) | copy-start | bytes 100
  20.1 3.7 %collective-permute-start.2 = (bf16[64,128]{1,0:T(8,128)(2,1)S(1)}, bf16[64,128]{1,0:T(8,128)(2,1)S(1)}, u32[]{:S(2)}, u32[]{:S(2)}) collective-permute-start(bf16[64,128]{1,0:T(8,128)(2,1)S(1)} %get-tuple-element.60), channel_id=1, source_target_pairs={{0,4},{4,0},{8,12},{12,8},{1,5},{5,1},{9,13},{13,9},{2,6},{6,2},{1... | collective-permute-start | bytes 49160 | tf_op jit(solution)/shard_map/ppermute | solution.py:827
  20.2 4.4 %collective-permute-start.3 = (bf16[64,128]{1,0:T(8,128)(2,1)S(1)}, bf16[64,128]{1,0:T(8,128)(2,1)S(1)}, u32[]{:S(2)}, u32[]{:S(2)}) collective-permute-start(bf16[64,128]{1,0:T(8,128)(2,1)S(1)} %get-tuple-element.61), channel_id=1, source_target_pairs={{0,8},{4,12},{8,0},{12,4},{1,9},{5,13},{9,1},{13,5},{2,10},{6,14},... | collective-permute-start | bytes 49160 | tf_op jit(solution)/shard_map/ppermute | solution.py:827
  21.7 3.2 %collective-permute-start.4 = (bf16[64,128]{1,0:T(8,128)(2,1)S(1)}, bf16[64,128]{1,0:T(8,128)(2,1)S(1)}, u32[]{:S(2)}, u32[]{:S(2)}) collective-permute-start(bf16[64,128]{1,0:T(8,128)(2,1)S(1)} %get-tuple-element.62), channel_id=1, source_target_pairs={{0,12},{4,8},{8,4},{12,0},{1,13},{5,9},{9,5},{13,1},{2,14},{6,10},... | collective-permute-start | bytes 49160 | tf_op jit(solution)/shard_map/ppermute | solution.py:827
  23.8 20.0 %collective-permute-start.10 = (bf16[128,1024]{1,0:T(8,128)(2,1)S(1)}, bf16[128,1024]{1,0:T(8,128)(2,1)S(1)}, u32[]{:S(2)}, u32[]{:S(2)}) collective-permute-start(bf16[128,1024]{1,0:T(8,128)(2,1)S(1)} %get-tuple-element.72), channel_id=1, source_target_pairs={{0,1},{1,0},{2,3},{3,2},{4,5},{5,4},{6,7},{7,6},{8,9},{9,8},{10,11... | collective-permute-start | bytes 786440 | tf_op jit(solution)/shard_map/ppermute | solution.py:824
  25.0 19.4 %collective-permute-start.11 = (bf16[128,1024]{1,0:T(8,128)(2,1)S(1)}, bf16[128,1024]{1,0:T(8,128)(2,1)S(1)}, u32[]{:S(2)}, u32[]{:S(2)}) collective-permute-start(bf16[128,1024]{1,0:T(8,128)(2,1)S(1)} %carry.3.rest_0_), channel_id=1, source_target_pairs={{0,3},{3,0},{1,2},{2,1},{4,7},{7,4},{5,6},{6,5},{8,11},{11,8},{9,1... | collective-permute-start | bytes 786440 | tf_op jit(solution)/shard_map/ppermute | solution.py:824
  35.9 8.5 %collective-permute-start.7 = (bf16[64,1024]{1,0:T(8,128)(2,1)S(1)}, bf16[64,1024]{1,0:T(8,128)(2,1)S(1)}, u32[]{:S(2)}, u32[]{:S(2)}) collective-permute-start(bf16[64,1024]{1,0:T(8,128)(2,1)S(1)} %get-tuple-element.67), channel_id=1, source_target_pairs={{0,4},{4,0},{8,12},{12,8},{1,5},{5,1},{9,13},{13,9},{2,6},{6,2},{1... | collective-permute-start | bytes 393224 | tf_op jit(solution)/shard_map/ppermute | solution.py:827
  35.9 8.4 %collective-permute-start.8 = (bf16[64,1024]{1,0:T(8,128)(2,1)S(1)}, bf16[64,1024]{1,0:T(8,128)(2,1)S(1)}, u32[]{:S(2)}, u32[]{:S(2)}) collective-permute-start(bf16[64,1024]{1,0:T(8,128)(2,1)S(1)} %get-tuple-element.68), channel_id=1, source_target_pairs={{0,8},{4,12},{8,0},{12,4},{1,9},{5,13},{9,1},{13,5},{2,10},{6,14},... | collective-permute-start | bytes 393224 | tf_op jit(solution)/shard_map/ppermute | solution.py:827
  37.5 6.8 %collective-permute-start.9 = (bf16[64,1024]{1,0:T(8,128)(2,1)S(1)}, bf16[64,1024]{1,0:T(8,128)(2,1)S(1)}, u32[]{:S(2)}, u32[]{:S(2)}) collective-permute-start(bf16[64,1024]{1,0:T(8,128)(2,1)S(1)} %get-tuple-element.69), channel_id=1, source_target_pairs={{0,12},{4,8},{8,4},{12,0},{1,13},{5,9},{9,5},{13,1},{2,14},{6,10},... | collective-permute-start | bytes 393224 | tf_op jit(solution)/shard_map/ppermute | solution.py:827
  44.8 5.5 %collective-permute-start.12 = (bf16[176,128]{1,0:T(8,128)(2,1)S(1)}, bf16[176,128]{1,0:T(8,128)(2,1)S(1)}, u32[]{:S(2)}, u32[]{:S(2)}) collective-permute-start(bf16[176,128]{1,0:T(8,128)(2,1)S(1)} %get-tuple-element.83), channel_id=1, source_target_pairs={{0,2},{1,3},{2,0},{3,1},{4,6},{5,7},{6,4},{7,5},{8,10},{9,11},{10,... | collective-permute-start | bytes 135176 | tf_op jit(solution)/shard_map/ppermute | solution.py:824
  46.5 5.8 %collective-permute-start.13 = (bf16[176,128]{1,0:T(8,128)(2,1)S(1)}, bf16[176,128]{1,0:T(8,128)(2,1)S(1)}, u32[]{:S(2)}, u32[]{:S(2)}) collective-permute-start(bf16[176,128]{1,0:T(8,128)(2,1)S(1)} %get-tuple-element.84), channel_id=1, source_target_pairs={{0,3},{1,2},{2,1},{3,0},{4,7},{5,6},{6,5},{7,4},{8,11},{9,10},{10,... | collective-permute-start | bytes 135176 | tf_op jit(solution)/shard_map/ppermute | solution.py:824
  47.4 4.9 %collective-permute-start.14 = (bf16[176,128]{1,0:T(8,128)(2,1)S(1)}, bf16[176,128]{1,0:T(8,128)(2,1)S(1)}, u32[]{:S(2)}, u32[]{:S(2)}) collective-permute-start(bf16[176,128]{1,0:T(8,128)(2,1)S(1)} %get-tuple-element.85), channel_id=1, source_target_pairs={{0,1},{1,0},{2,3},{3,2},{4,5},{5,4},{6,7},{7,6},{8,9},{9,8},{10,11... | collective-permute-start | bytes 135176 | tf_op jit(solution)/shard_map/ppermute | solution.py:824
  48.4 6.1 %collective-permute-start.16 = (bf16[64,1024]{1,0:T(8,128)(2,1)S(1)}, bf16[64,1024]{1,0:T(8,128)(2,1)S(1)}, u32[]{:S(2)}, u32[]{:S(2)}) collective-permute-start(bf16[64,1024]{1,0:T(8,128)(2,1)S(1)} %get-tuple-element.88), channel_id=1, source_target_pairs={{0,8},{4,12},{8,0},{12,4},{1,9},{5,13},{9,1},{13,5},{2,10},{6,14},... | collective-permute-start | bytes 393224 | tf_op jit(solution)/shard_map/ppermute | solution.py:827
  49.9 5.8 %collective-permute-start.17 = (bf16[64,1024]{1,0:T(8,128)(2,1)S(1)}, bf16[64,1024]{1,0:T(8,128)(2,1)S(1)}, u32[]{:S(2)}, u32[]{:S(2)}) collective-permute-start(bf16[64,1024]{1,0:T(8,128)(2,1)S(1)} %get-tuple-element.89), channel_id=1, source_target_pairs={{0,12},{4,8},{8,4},{12,0},{1,13},{5,9},{9,5},{13,1},{2,14},{6,10},... | collective-permute-start | bytes 393224 | tf_op jit(solution)/shard_map/ppermute | solution.py:827
  52.5 3.2 %collective-permute-start.15 = (bf16[64,1024]{1,0:T(8,128)(2,1)S(1)}, bf16[64,1024]{1,0:T(8,128)(2,1)S(1)}, u32[]{:S(2)}, u32[]{:S(2)}) collective-permute-start(bf16[64,1024]{1,0:T(8,128)(2,1)S(1)} %get-tuple-element.87), channel_id=1, source_target_pairs={{0,4},{4,0},{8,12},{12,8},{1,5},{5,1},{9,13},{13,9},{2,6},{6,2},{1... | collective-permute-start | bytes 393224 | tf_op jit(solution)/shard_map/ppermute | solution.py:827
  52.6 4.1 %collective-permute-start.18 = (bf16[16,256]{1,0:T(8,128)(2,1)S(1)}, bf16[16,256]{1,0:T(8,128)(2,1)S(1)}, u32[]{:S(2)}, u32[]{:S(2)}) collective-permute-start(bf16[16,256]{1,0:T(8,128)(2,1)S(1)} %get-tuple-element.94), channel_id=1, source_target_pairs={{0,8},{4,12},{8,0},{12,4},{1,9},{5,13},{9,1},{13,5},{2,10},{6,14},... | collective-permute-start | bytes 24584 | tf_op jit(solution)/shard_map/ppermute | solution.py:827
  54.1 3.1 %collective-permute-start.19 = (bf16[16,256]{1,0:T(8,128)(2,1)S(1)}, bf16[16,256]{1,0:T(8,128)(2,1)S(1)}, u32[]{:S(2)}, u32[]{:S(2)}) collective-permute-start(bf16[16,256]{1,0:T(8,128)(2,1)S(1)} %get-tuple-element.95), channel_id=1, source_target_pairs={{0,12},{4,8},{8,4},{12,0},{1,13},{5,9},{9,5},{13,1},{2,14},{6,10},... | collective-permute-start | bytes 24584 | tf_op jit(solution)/shard_map/ppermute | solution.py:827
  54.4 2.8 %collective-permute-start.20 = (bf16[16,256]{1,0:T(8,128)(2,1)S(1)}, bf16[16,256]{1,0:T(8,128)(2,1)S(1)}, u32[]{:S(2)}, u32[]{:S(2)}) collective-permute-start(bf16[16,256]{1,0:T(8,128)(2,1)S(1)} %get-tuple-element.96), channel_id=1, source_target_pairs={{0,4},{4,0},{8,12},{12,8},{1,5},{5,1},{9,13},{13,9},{2,6},{6,2},{1... | collective-permute-start | bytes 24584 | tf_op jit(solution)/shard_map/ppermute | solution.py:827
